TPU v7x, 128 devices: a whole 4x4x4 slice. The times are simulated.
128 devices in a mesh: mpo: 8 (over x, core), bond: 16 (over z, y).
Axes of the slice: x: 4, y: 4, z: 4, core: 2. Of those that a mesh axis runs over, the one named last changes fastest.
Arguments:
- environment: bfloat16 [4096, 40, 4096], P(None, 'mpo', 'bond'), may hold values from -60 to 60
- site_tensor: bfloat16 [4096, 4, 4096], P('bond'), may hold values from -0.09375 to 0.09375
- mpo_tensor: bfloat16 [40, 40, 4, 4], replicated, may hold values from -0.5 to 0.5
- sketch_site: bfloat16 [4096, 128], replicated, may hold values from -6 to 6
- sketch_expand: bfloat16 [128, 40, 4096], P('mpo'), may hold values from -60 to 60
- row_sectors: int32 [2, 4096, 4], P(None, 'bond'), may hold values from 0 to 5, as said below
- column_sectors: int32 [2, 128], replicated, may hold values from 0 to 5, as said below
Outputs:
- basis: bfloat16 [4096, 4, 128], P('bond')
- extended: float32 [128, 40, 128], P('bond', 'mpo')
Inputs may be any that keep to these rules, and one draw needn't show every extreme that they name: `row_sectors`: every joined row's label pair is (4, 0) or (5, 1); the rows labelled (5, 1) are one run of 64 consecutive joined rows (a, s) in the order a then s. `column_sectors`: every column's label pair is (4, 0) or (5, 1); exactly 16 columns are labelled (5, 1).
All inputs are finite; a program needn't handle non-finite values.
Results may differ from a plain program's by a relative error of at most 0.0064.
Values may be sent and summed in bfloat16 or wider, within the bound.
No kernel may reach another device: no remote copies, remote signals or barrier semaphores. Data moves between devices by JAX's collectives and lax.ppermute only.
A program may use at most 128 MiB of HBM per device.

v0:
```python
import jax
import jax.numpy as jnp
from jax import lax
from jax.experimental import pallas as pl
from jax.experimental.pallas import tpu as pltpu
from jax.sharding import Mesh
from jax.sharding import PartitionSpec as P

MPO = ("mpo_0", "mpo_1")
BOND = ("bond_0", "bond_1")
CHIPS = ("bond_0", "bond_1", "mpo_0")
CORE = "mpo_1"
SWAP = [(0, 1), (1, 0)]

mixing = 0.5
shift_tolerance = 1e-06
f32 = jnp.float32
bf16 = jnp.bfloat16
VMEM = 40 * 1024 * 1024


def sector_mask(row_labels, column_labels):
    match = (row_labels[0][:, :, None] == column_labels[0][None, None, :]) & (
        row_labels[1][:, :, None] == column_labels[1][None, None, :]
    )
    return match.astype(f32)


def dot(a, b, dims):
    return lax.dot_general(a, b, (dims, ((), ())), preferred_element_type=f32)


def cost(flops, size):
    return pl.CostEstimate(flops=flops, bytes_accessed=size, transcendentals=0)


def expand_half(core, env, contracted):
    width, blocks, _, share, depth = env.shape
    x = contracted.shape[1]
    k = share
    s = x // k
    step = 4

    def kernel(core_ref, e_ref, c_ref, o_ref):
        left = jnp.concatenate(
            [e_ref[w, :, 0].reshape(step * share, depth) for w in range(width)], axis=1
        )
        right = jnp.concatenate([c_ref[w] for w in range(width)], axis=1)
        total = dot(left, right, ((1,), (1,)))
        for i in range(s):
            o_ref[:, i] = total[:, i * k : (i + 1) * k].astype(bf16).reshape(step, share, k)

    return pl.pallas_call(
        kernel,
        grid_spec=pltpu.PrefetchScalarGridSpec(
            num_scalar_prefetch=1,
            grid=(blocks // step,),
            in_specs=[
                pl.BlockSpec((width, step, 1, share, depth), lambda i, core: (0, i, core[0], 0, 0)),
                pl.BlockSpec((width, x, depth), lambda i, core: (0, 0, 0)),
            ],
            out_specs=pl.BlockSpec((step, s, share, k), lambda i, core: (i, 0, 0, 0)),
        ),
        out_shape=jax.ShapeDtypeStruct((blocks, s, share, k), bf16),
        compiler_params=pltpu.CompilerParams(vmem_limit_bytes=VMEM),
        cost_estimate=cost(2 * width * blocks * share * depth * x, 9_000_000),
        name="expand_half",
    )(core, env, contracted)


def site_terms(env, site):
    width, blocks, rows, depth = env.shape
    s, k = site.shape[1:3]
    step = 2

    def kernel(e_ref, s_ref, x_ref, g_ref):
        first = pl.program_id(0) == 0
        left = jnp.concatenate([s_ref[z].reshape(s * k, rows) for z in range(step)], axis=1)

        def term(w):
            return dot(left, e_ref[w].reshape(step * rows, depth), ((1,), (0,)))

        wide = jnp.concatenate([left[i * k : (i + 1) * k] for i in range(s)], axis=1)
        gram = dot(wide, wide, ((1,), (1,)))

        @pl.when(first)
        def _():
            for w in range(width):
                x_ref[w] = term(w)
            g_ref[...] = gram

        @pl.when(jnp.logical_not(first))
        def _():
            for w in range(width):
                x_ref[w] += term(w)
            g_ref[...] += gram

    return pl.pallas_call(
        kernel,
        grid=(blocks // step,),
        in_specs=[
            pl.BlockSpec((width, step, rows, depth), lambda i: (0, i, 0, 0)),
            pl.BlockSpec((step, s, k, rows), lambda i: (i, 0, 0, 0)),
        ],
        out_specs=[
            pl.BlockSpec((width, s * k, depth), lambda i: (0, 0, 0)),
            pl.BlockSpec((k, k), lambda i: (0, 0)),
        ],
        out_shape=[
            jax.ShapeDtypeStruct((width, s * k, depth), f32),
            jax.ShapeDtypeStruct((k, k), f32),
        ],
        compiler_params=pltpu.CompilerParams(vmem_limit_bytes=VMEM),
        cost_estimate=cost(6_000_000_000, 17_000_000),
        name="site_terms",
    )(env, site)


def expand_step(e_ref, s_ref, h_ref):
    width, step, _, share, depth = e_ref.shape
    s, k = h_ref.shape[1:3]
    left = jnp.concatenate([h_ref[z].reshape(s * k, share) for z in range(step)], axis=1)
    terms = [
        lambda w=w: dot(left, e_ref[w, :, 0].reshape(step * share, depth), ((1,), (0,)))
        for w in range(width)
    ]
    wide = jnp.concatenate([left[i * k : (i + 1) * k] for i in range(s)], axis=1)
    site = jnp.concatenate([s_ref[z, i] for i in range(s) for z in range(step)], axis=1)
    gram = dot(wide, jnp.concatenate([wide, site], axis=0), ((1,), (1,)))
    return terms, gram


def expand_specs(width, step, share, depth, s, k):
    return [
        pl.BlockSpec((width, step, 1, share, depth), lambda i, sc: (0, i, sc[0], 0, 0)),
        pl.BlockSpec((step, s, k, share), lambda i, sc: (i, 0, 0, sc[0])),
        pl.BlockSpec((step, s, k, share), lambda i, sc: (i, 0, 0, 0)),
    ]


def expand_terms(core, env, site, half):
    width, blocks, _, share, depth = env.shape
    s, k = half.shape[1:3]
    step = 4

    def kernel(core_ref, e_ref, s_ref, h_ref, x_ref, g_ref):
        first = pl.program_id(0) == 0
        terms, gram = expand_step(e_ref, s_ref, h_ref)

        @pl.when(first)
        def _():
            for w in range(width):
                x_ref[w] = terms[w]()
            g_ref[...] = gram

        @pl.when(jnp.logical_not(first))
        def _():
            for w in range(width):
                x_ref[w] += terms[w]()
            g_ref[...] += gram

    return pl.pallas_call(
        kernel,
        grid_spec=pltpu.PrefetchScalarGridSpec(
            num_scalar_prefetch=1,
            grid=(blocks // step,),
            in_specs=expand_specs(width, step, share, depth, s, k),
            out_specs=[
                pl.BlockSpec((width, s * k, depth), lambda i, sc: (0, 0, 0)),
                pl.BlockSpec((k, 2 * k), lambda i, sc: (0, 0)),
            ],
        ),
        out_shape=[
            jax.ShapeDtypeStruct((width, s * k, depth), f32),
            jax.ShapeDtypeStruct((k, 2 * k), f32),
        ],
        compiler_params=pltpu.CompilerParams(vmem_limit_bytes=VMEM),
        cost_estimate=cost(3_300_000_000, 12_000_000),
        name="expand_terms",
    )(core, env, site, half)


def inverse_factor(a, nb):
    n = a.shape[0]
    count = n // 8
    rows = [a[8 * i : 8 * i + 8, :] for i in range(count)]
    lane = lax.broadcasted_iota(jnp.int32, (8, n), 1)
    sub = lax.broadcasted_iota(jnp.int32, (8, n), 0)

    def full(v):
        return jnp.broadcast_to(v, (8, n))

    for j in range(0, n, nb):
        b, o = j // 8, j % 8
        cols = {i: [full(rows[i][:, j + p : j + p + 1]) for p in range(nb)] for i in range(b, count)}
        lines = [full(rows[b][o + q : o + q + 1, :]) for q in range(nb)]
        pivots = [
            [full(cols[b][r][o + q : o + q + 1, :]) for r in range(q + 1)] for q in range(nb)
        ]
        scaled, ratio = [], {}
        for p in range(nb):
            inv = 1.0 / pivots[p][p]
            here = lane == j + p
            line = jnp.where(here, 1.0, lines[p]) * inv
            scaled.append(line)
            for q in range(p + 1, nb):
                ratio[q, p] = pivots[q][p] * inv
            for q in range(p + 1, nb):
                lines[q] = jnp.where(here, 0.0, lines[q]) - pivots[q][p] * line
                for r in range(p + 1, q + 1):
                    pivots[q][r] = pivots[q][r] - pivots[q][p] * ratio[r, p]
        for i in range(b, count):
            c = cols[i]
            value = rows[i]
            for p in range(nb):
                new = jnp.where(lane == j + p, 0.0, value) - c[p] * scaled[p]
                value = jnp.where(sub > o + p, new, value) if i == b else new
                for q in range(p + 1, nb):
                    c[q] = c[q] - c[p] * ratio[q, p]
            rows[i] = value
    w = jnp.concatenate(rows, axis=0)
    row = lax.broadcasted_iota(jnp.int32, (n, n), 0)
    col = lax.broadcasted_iota(jnp.int32, (n, n), 1)
    diagonal = jnp.sum(jnp.where(row == col, w, 0.0), axis=1, keepdims=True)
    unit = jnp.where(row > col, w, 0.0) + jnp.where(row == col, 1.0, 0.0)
    return unit * lax.rsqrt(diagonal)


def split(v):
    high = v.astype(bf16)
    return high, (v - high.astype(f32)).astype(bf16)


def finish(scalars, env, site, half, x_site, g_site, x_own, g_own, own, site_local):
    width, blocks, _, share, depth = env.shape
    s, k = half.shape[1:3]
    step = 4
    last = blocks // step - 1

    def kernel(
        sc_ref, e_ref, s_ref, h_ref, xs_ref, gs_ref, xo_ref, go_ref, own_ref, oth_ref, sl_ref,
        p_ref, b_ref, x_ref, g_ref,
    ):
        first = pl.program_id(0) == 0
        terms, gram = expand_step(e_ref, s_ref, h_ref)

        @pl.when(first)
        def _():
            for w in range(width):
                x_ref[w] = xo_ref[w] + terms[w]()
            g_ref[...] = go_ref[...] + gram

        @pl.when(jnp.logical_not(first))
        def _():
            for w in range(width):
                x_ref[w] += terms[w]()
            g_ref[...] += gram

        @pl.when(pl.program_id(0) == last)
        def _():
            gs = gs_ref[...]
            ge = g_ref[:, :k]
            gc = g_ref[:, k:]
            row = lax.broadcasted_iota(jnp.int32, (k, k), 0)
            col = lax.broadcasted_iota(jnp.int32, (k, k), 1)
            trace_site = jnp.sum(jnp.where(row == col, gs, 0.0), keepdims=True)
            trace_expand = jnp.sum(jnp.where(row == col, ge, 0.0), keepdims=True)
            mix = mixing * jnp.sqrt((trace_site + shift_tolerance) / (trace_expand + shift_tolerance))
            inverse = inverse_factor(gs + mix * (gc + gc.T) + (mix * mix) * ge, 8)
            high, low = split(inverse)
            both = jnp.concatenate([high, low], axis=1)

            def apply(v):
                vh, vl = split(v)
                return dot(both, jnp.concatenate([vh, vh], axis=0), ((1,), (0,))) + dot(
                    high, vl, ((1,), (0,))
                )

            for w in range(width):
                for i in range(s):
                    part = slice(i * k, (i + 1) * k)
                    p_ref[w, part] = apply(xs_ref[w, part] + mix * x_ref[w, part]).astype(bf16)
            even = sc_ref[0] == 1
            for i in range(s):
                a0 = own_ref[0, i].astype(f32)
                a1 = oth_ref[0, i].astype(f32)
                rows = jnp.concatenate(
                    [jnp.where(even, a0, a1), jnp.where(even, a1, a0)], axis=1
                )
                done = apply(sl_ref[i] + mix * rows)
                b_ref[:, i * k : (i + 1) * k] = done.T.astype(bf16)

    fixed3 = lambda i, sc: (0, 0, 0)
    fixed2 = lambda i, sc: (0, 0)
    return pl.pallas_call(
        kernel,
        grid_spec=pltpu.PrefetchScalarGridSpec(
            num_scalar_prefetch=1,
            grid=(blocks // step,),
            in_specs=expand_specs(width, step, share, depth, s, k)
            + [
                pl.BlockSpec((width, s * k, depth), fixed3),
                pl.BlockSpec((k, k), fixed2),
                pl.BlockSpec((width, s * k, depth), fixed3),
                pl.BlockSpec((k, 2 * k), fixed2),
                pl.BlockSpec((1, s, k, share), lambda i, sc: (sc[1], 0, 0, 0)),
                pl.BlockSpec((1, s, k, share), lambda i, sc: (sc[1], 0, 0, 0)),
                pl.BlockSpec((s, k, 2 * share), fixed3),
            ],
            out_specs=[
                pl.BlockSpec((width, s * k, depth), fixed3),
                pl.BlockSpec((2 * share, s * k), fixed2),
            ],
            scratch_shapes=[
                pltpu.VMEM((width, s * k, depth), f32),
                pltpu.VMEM((k, 2 * k), f32),
            ],
        ),
        out_shape=[
            jax.ShapeDtypeStruct((width, s * k, depth), bf16),
            jax.ShapeDtypeStruct((2 * share, s * k), bf16),
        ],
        compiler_params=pltpu.CompilerParams(vmem_limit_bytes=VMEM),
        cost_estimate=cost(4_000_000_000, 20_000_000),
        name="finish",
    )(scalars, env, site, half, x_site, g_site, x_own, g_own, own, half, site_local)


def summed_over_chips(half):
    return lax.all_to_all(half, CHIPS, 0, 0, tiled=True).astype(f32).sum(axis=0)


def body(
    environment, site_tensor, mpo_tensor, sketch_site, sketch_expand, row_sectors, column_sectors
):
    mpo_index = lax.axis_index(MPO)
    bond_index = lax.axis_index(BOND)
    core = lax.axis_index(CORE)
    chi, width, depth = environment.shape
    local_rows, physical, _ = site_tensor.shape
    columns = column_sectors.shape[1]
    blocks, share = chi // local_rows, local_rows // 2
    mask_rows = sector_mask(row_sectors, column_sectors)
    env = jnp.transpose(environment, (1, 0, 2))
    env_halves = env.reshape(width, blocks, 2, share, depth)
    own_core = core.reshape(1).astype(jnp.int32)
    other_core = 1 - own_core

    site_y = jnp.einsum("asb,bk->ska", site_tensor, sketch_site, preferred_element_type=f32)
    site_local = site_y * jnp.transpose(mask_rows, (1, 2, 0))
    site_all = lax.all_gather(site_local.astype(bf16), BOND, axis=0)

    sketched = jnp.einsum(
        "asb,kwb->wska", site_tensor, sketch_expand, preferred_element_type=f32
    ).astype(bf16)
    applied = jnp.einsum(
        "vwst,wtka->vska", mpo_tensor, sketched, preferred_element_type=f32
    ).astype(bf16)
    contracted = lax.all_to_all(applied, MPO, split_axis=0, concat_axis=2, tiled=True)
    contracted = contracted.reshape(width, physical * columns, depth)

    send = expand_half(other_core, env_halves, contracted)
    got = lax.ppermute(send, CORE, SWAP)
    keep = expand_half(own_core, env_halves, contracted)
    half = (keep.astype(f32) + got.astype(f32)).astype(bf16)
    piece = summed_over_chips(half.reshape(blocks * physical, share, columns))
    mask_piece = lax.dynamic_slice(
        mask_rows, (core * share, lax.axis_index("mpo_0"), 0), (share, 1, columns)
    )[:, 0]
    piece = (piece * mask_piece).T.astype(bf16)
    own = lax.all_to_all(
        jnp.broadcast_to(piece[None], (blocks * physical, columns, share)), CHIPS, 0, 0, tiled=True
    ).reshape(blocks, physical, columns, share)
    other = lax.ppermute(own, CORE, SWAP)

    x_site, g_site = site_terms(env.reshape(width, blocks, local_rows, depth), site_all)
    x_own, g_own = expand_terms(own_core, env_halves, site_all, own)
    scalars = jnp.concatenate([other_core, bond_index.reshape(1).astype(jnp.int32)])
    projected, basis_flat = finish(
        scalars, env_halves, site_all, other, x_site, g_site, x_own, g_own, own, site_local
    )
    basis_local = basis_flat.reshape(local_rows, physical, columns)

    paired = jnp.einsum(
        "wxc,cy->wxy", projected, basis_flat, preferred_element_type=f32
    ).reshape(width, physical, columns, physical, columns)
    operator_rows = lax.dynamic_slice_in_dim(mpo_tensor, mpo_index * width, width, 0)
    share_out = jnp.einsum(
        "wvst,wsktl->kvl", operator_rows.astype(f32), paired, precision=lax.Precision.HIGH
    ).astype(bf16)
    kout, vout = columns // 16, mpo_tensor.shape[1] // 8
    parts = share_out.reshape(16, kout, 4, 2, vout, columns).transpose(3, 0, 2, 1, 4, 5)
    mine = lax.dynamic_index_in_dim(parts, core, 0, keepdims=False)
    sent = lax.dynamic_index_in_dim(parts, 1 - core, 0, keepdims=False)
    both = (mine.astype(f32) + lax.ppermute(sent, CORE, SWAP).astype(f32)).astype(bf16)
    extended = summed_over_chips(both.reshape(64, kout, vout, columns))
    return (basis_local, extended)


def solution(mesh):
    torus = Mesh(mesh.devices.reshape(4, 2, 4, 4), ("mpo_0", "mpo_1", "bond_0", "bond_1"))
    placed = (
        P(None, MPO, BOND),
        P(BOND, None, None),
        P(),
        P(),
        P(MPO, None, None),
        P(None, BOND, None),
        P(),
    )
    return jax.shard_map(
        body,
        mesh=torus,
        in_specs=placed,
        out_specs=(P(BOND, None, None), P(BOND, MPO, None)),
        check_vma=False,
    )
```

profile of v0, /device:TPU:0, one launch (start us, length us, event | category | flops | bytes accessed | tf_op | source)
XLA Modules:
  0.0 244.8 jit_solution(10645746177942629213)
XLA Ops:
  7.2 16.3 %fusion.19 = bf16[40,4,16,256,1]{3,0,1,4,2:T(8,128)(2,1)S(1)} fusion(bf16[256,4,4096]{2,1,0:T(4,128)(2,1)} %param.8, bf16[16,40,4096]{2,1,0:T(8,128)(2,1)} %param.11), kind=kOutput, calls=%fused_computation.15 | convolution fusion | flops 5369364480 | bytes 14942208 | tf_op jit(solution)/shard_map/asb,kwb->wska/dot_general | solution.py:353
  23.5 0.6 fusion.15
  24.1 1.8 copy.30
  25.8 4.4 %all-to-all-start = ((bf16[40,4,16,256]{3,1,2,0:T(4,128)(2,1)}), bf16[40,4,16,256]{3,1,2,0:T(4,128)(2,1)S(1)}, u32[]{:S(2)}, u32[]{:S(2)}) async-start(bf16[40,4,16,256]{3,1,2,0:T(4,128)(2,1)} %copy.30), calls=%async_computation | async-start | bytes 2621440 | tf_op jit(solution)/shard_map/all_to_all | solution.py:359
  30.3 18.7 %all-to-all-done = bf16[40,4,16,256]{3,1,2,0:T(4,128)(2,1)S(1)} async-done(((bf16[40,4,16,256]{3,1,2,0:T(4,128)(2,1)}), bf16[40,4,16,256]{3,1,2,0:T(4,128)(2,1)S(1)}, u32[]{:S(2)}, u32[]{:S(2)}) %all-to-all-start) | async-done | bytes 1310752 | tf_op jit(solution)/shard_map/all_to_all | solution.py:359
  49.4 4.0 %copy-done.2 = bf16[4096,5,256]{2,0,1:T(8,128)(2,1)S(1)} copy-done((bf16[4096,5,256]{2,0,1:T(8,128)(2,1)S(1)}, bf16[4096,5,256]{2,0,1:T(8,128)(2,1)}, u32[]{:S(2)}) %copy-start.2) | copy-done | bytes 10485784
  53.4 4.7 %expand_half.3 = bf16[16,4,128,128]{3,2,1,0:T(8,128)(2,1)} custom-call(s32[1]{0:T(128)S(6)} %sub.6.core_ref, bf16[5,16,2,128,256]{4,3,2,1,0:T(8,128)(2,1)S(1)} %bitcast.112, bf16[5,512,256]{2,1,0:T(8,128)(2,1)S(1)} %bitcast.120), custom_call_target="tpu_custom_call" | custom-call | flops 2684354560 | bytes 9000000 | tf_op jit(solution)/shard_map/expand_half/pallas_call | solution.py:53
  58.2 9.5 %fusion.38 = (bf16[4,128,256]{2,1,0:T(8,128)(2,1)}, f32[4,128,256]{2,1,0:T(8,128)S(1)}) fusion(bf16[256,4,4096]{2,1,0:T(4,128)(2,1)} %param.8, bf16[4096,128]{1,0:T(8,128)(2,1)S(1)} %copy-done, s32[128]{0:T(128)S(1)} %get-tuple-element.19, s32[4,256]{1,0:T(4,128)S(1)} %get-tuple-element.16, s32[128]{0:T(128)S(1)} %get-tuple-element.18, ...), kind=kOutput, calls=%fused_computation.39 | convolution fusion | flops 1074397184 | bytes 10232832 | tf_op jit(solution)/shard_map/asb,bk->ska/dot_general | solution.py:349
  67.7 4.0 %copy-done.3 = bf16[4096,5,256]{2,0,1:T(8,128)(2,1)S(1)} copy-done((bf16[4096,5,256]{2,0,1:T(8,128)(2,1)S(1)}, bf16[4096,5,256]{2,0,1:T(8,128)(2,1)}, u32[]{:S(2)}) %copy-start.3) | copy-done | bytes 10485784
  71.7 3.9 %expand_half.2 = bf16[16,4,128,128]{3,2,1,0:T(8,128)(2,1)S(1)} custom-call(s32[1]{0:T(128)} %bitcast.core_ref, bf16[5,16,2,128,256]{4,3,2,1,0:T(8,128)(2,1)S(1)} %bitcast.113, bf16[5,512,256]{2,1,0:T(8,128)(2,1)S(1)} %bitcast.121), custom_call_target="tpu_custom_call" | custom-call | flops 2684354560 | bytes 9000000 | tf_op jit(solution)/shard_map/expand_half/pallas_call | solution.py:53
  75.6 3.8 %add_convert_fusion = bf16[16,4,128,128]{3,2,1,0:T(8,128)(2,1)} fusion(bf16[16,4,128,128]{3,2,1,0:T(8,128)(2,1)} %collective-permute-done, bf16[16,4,128,128]{3,2,1,0:T(8,128)(2,1)S(1)} %expand_half.2), kind=kLoop, calls=%fused_computation.9 | loop fusion | flops 4194304 | bytes 6291456 | tf_op jit(solution)/shard_map/convert_element_type | solution.py:365
  79.4 9.6 %all-to-all-start.1 = ((bf16[64,128,128]{2,1,0:T(8,128)(2,1)}), bf16[64,128,128]{2,1,0:T(8,128)(2,1)S(1)}, u32[]{:S(2)}, u32[]{:S(2)}) async-start(bf16[64,128,128]{2,1,0:T(8,128)(2,1)} %bitcast.27), calls=%async_computation.1 | async-start | bytes 4194304 | tf_op jit(solution)/shard_map/all_to_all | solution.py:330
  89.1 30.7 %all-to-all-done.1 = bf16[64,128,128]{2,1,0:T(8,128)(2,1)S(1)} async-done(((bf16[64,128,128]{2,1,0:T(8,128)(2,1)}), bf16[64,128,128]{2,1,0:T(8,128)(2,1)S(1)}, u32[]{:S(2)}, u32[]{:S(2)}) %all-to-all-start.1) | async-done | bytes 2097184 | tf_op jit(solution)/shard_map/all_to_all | solution.py:330
  120.3 0.5 broadcast_in_dim.2
  120.9 35.9 %all_to_all.30 = bf16[64,128,128]{2,1,0:T(8,128)(2,1)S(1)} all-to-all(bf16[64,128,128]{2,1,0:T(8,128)(2,1)S(1)} %broadcast_in_dim.2), channel_id=1, replica_groups=mesh['mpo_0'=4,'mpo_1'=2,'bond_0'=4,'bond_1'=4] {'bond_0','bond_1','mpo_0'}, dimensions={0} | all-to-all | bytes 4194304 | tf_op jit(solution)/shard_map/all_to_all | solution.py:371
  156.8 1.9 all-gather.3.cloned.1.call-done
  158.7 2.2 copy-done.4
  160.9 7.1 %expand_terms.1 = (f32[5,512,256]{2,1,0:T(8,128)S(1)}, f32[128,256]{1,0:T(8,128)S(1)}) custom-call(s32[1]{0:T(128)} %bitcast.core_ref, bf16[5,16,2,128,256]{4,3,2,1,0:T(8,128)(2,1)} %bitcast.109, bf16[16,4,128,256]{3,2,1,0:T(8,128)(2,1)S(1)} %bitcast.118, bf16[16,4,128,128]{3,2,1,0:T(8,128)(2,1)S(1)} %bitcast.115), custom_call_target="tpu_custom_call" | custom-call | flops 3300000000 | bytes 12000000 | tf_op jit(solution)/shard_map/expand_terms/pallas_call | solution.py:162
  168.1 11.2 %site_terms.1 = (f32[5,512,256]{2,1,0:T(8,128)S(1)}, f32[128,128]{1,0:T(8,128)S(1)}) custom-call(bf16[5,16,256,256]{3,2,1,0:T(8,128)(2,1)} %bitcast.110, bf16[16,4,128,256]{3,2,1,0:T(8,128)(2,1)S(1)} %bitcast.119), custom_call_target="tpu_custom_call" | custom-call | flops 6000000000 | bytes 17000000 | tf_op jit(solution)/shard_map/site_terms/pallas_call | solution.py:98
  179.3 14.7 %finish.1 = (bf16[5,512,256]{2,1,0:T(8,128)(2,1)S(1)}, bf16[256,512]{1,0:T(8,128)(2,1)S(1)}) custom-call(s32[2]{0:T(128)S(1)} %pad_add_fusion.sc_ref, bf16[5,16,2,128,256]{4,3,2,1,0:T(8,128)(2,1)} %bitcast.111, bf16[16,4,128,256]{3,2,1,0:T(8,128)(2,1)} %bitcast.117, bf16[16,4,128,128]{3,2,1,0:T(8,128)(2,1)} %collective-permute-done.1.h_ref.oth_ref, ...), custom_call_target="tpu_custom_call" | custom-call | flops 4000000000 | bytes 20000000 | tf_op jit(solution)/shard_map/finish/pallas_call | solution.py:295
  194.0 3.2 %fusion.32 = f32[5,512,512]{2,1,0:T(8,128)} fusion(bf16[5,512,256]{2,1,0:T(8,128)(2,1)S(1)} %get-tuple-element.13, bf16[256,512]{1,0:T(8,128)(2,1)S(1)} %get-tuple-element.12), kind=kOutput, calls=%fused_computation.23 | convolution fusion | flops 671088640 | bytes 6815744 | tf_op jit(solution)/shard_map/wxc,cy->wxy/dot_general | solution.py:384
  197.2 7.2 %reshape.53 = f32[5,4,128,4,128]{4,3,2,1,0:T(4,128)} reshape(f32[5,512,512]{2,1,0:T(8,128)} %fusion.32) | data formatting | bytes 10485760 | tf_op jit(solution)/shard_map/reshape | solution.py:386
  204.4 4.9 %fusion.16 = bf16[128,40,128]{2,1,0:T(8,128)(2,1)S(1)} fusion(f32[5,4,128,4,128]{4,3,2,1,0:T(4,128)} %reshape.53, bf16[40,40,4,4]{1,3,2,0:T(4,128)(2,1)S(1)} %copy-done.7, s32[]{:T(128)S(6)} %select_n.18), kind=kOutput, calls=%fused_computation.14 | convolution fusion | flops 315228160 | bytes 6574084 | tf_op jit(solution)/shard_map/wvst,wsktl->kvl/dot_general | solution.py:388
  209.3 1.4 copy.36
  210.7 1.1 dynamic-slice_bitcast_fusion
  211.9 2.1 collective-permute-done.2
  214.0 1.4 fusion.24
  215.3 1.0 copy.38
  216.3 5.7 %all-to-all-start.3 = ((bf16[64,8,5,128]{3,1,2,0:T(8,128)(2,1)}), bf16[64,8,5,128]{3,1,2,0:T(8,128)(2,1)S(1)}, u32[]{:S(2)}, u32[]{:S(2)}) async-start(bf16[64,8,5,128]{3,1,2,0:T(8,128)(2,1)} %bitcast.43), calls=%async_computation.3 | async-start | bytes 1310720 | tf_op jit(solution)/shard_map/all_to_all | solution.py:330
  222.0 0.8 reshape.52
  222.7 14.5 %all-to-all-done.3 = bf16[64,8,5,128]{3,1,2,0:T(8,128)(2,1)S(1)} async-done(((bf16[64,8,5,128]{3,1,2,0:T(8,128)(2,1)}), bf16[64,8,5,128]{3,1,2,0:T(8,128)(2,1)S(1)}, u32[]{:S(2)}, u32[]{:S(2)}) %all-to-all-start.3) | async-done | bytes 655392 | tf_op jit(solution)/shard_map/all_to_all | solution.py:330
  237.2 0.7 convert_reduce_fusion.1
  (32 shorter events, 1.4 us)
Async XLA Ops:
  7.2 51.0 %copy-start = (bf16[4096,128]{1,0:T(8,128)(2,1)S(1)}, bf16[4096,128]{1,0:T(8,128)(2,1)}, u32[]{:S(2)}) copy-start(bf16[4096,128]{1,0:T(8,128)(2,1)} %param.10) | copy-start | bytes 3145732
  7.2 16.3 %copy-start.7 = (bf16[40,40,4,4]{1,3,2,0:T(4,128)(2,1)S(1)}, bf16[40,40,4,4]{1,3,2,0:T(4,128)(2,1)}, u32[]{:S(2)}) copy-start(bf16[40,40,4,4]{1,3,2,0:T(4,128)(2,1)} %param.9) | copy-start | bytes 153604
  24.0 6.2 %copy-start.8 = (s32[2,128]{1,0:T(2,128)S(1)}, s32[2,128]{1,0:T(2,128)}, u32[]{:S(2)}) copy-start(s32[2,128]{1,0:T(2,128)} %param.13) | copy-start | bytes 3076
  24.0 6.3 %copy-start.6 = (s32[2,256,4]{1,2,0:T(4,128)S(1)}, s32[2,256,4]{1,2,0:T(4,128)}, u32[]{:S(2)}) copy-start(s32[2,256,4]{1,2,0:T(4,128)} %param.12) | copy-start | bytes 24580
  25.8 23.2 %all-to-all-start = ((bf16[40,4,16,256]{3,1,2,0:T(4,128)(2,1)}), bf16[40,4,16,256]{3,1,2,0:T(4,128)(2,1)S(1)}, u32[]{:S(2)}, u32[]{:S(2)}) async-start(bf16[40,4,16,256]{3,1,2,0:T(4,128)(2,1)} %copy.30), calls=%async_computation | async-start | bytes 2621440 | tf_op jit(solution)/shard_map/all_to_all | solution.py:359
  30.2 128.5 %all-gather.3.cloned.1.call-start = ((), (), s32[]{:S(2)}) async-start(), calls=%async_computation.4 | async-start | bytes 4456448 | tf_op jit(solution)/shard_map/all_gather | solution.py:351
  49.4 4.0 %copy-start.2 = (bf16[4096,5,256]{2,0,1:T(8,128)(2,1)S(1)}, bf16[4096,5,256]{2,0,1:T(8,128)(2,1)}, u32[]{:S(2)}) copy-start(bf16[4096,5,256]{2,0,1:T(8,128)(2,1)} %param.7) | copy-start | bytes 31457284
  58.2 17.4 %collective-permute-start = (bf16[16,4,128,128]{3,2,1,0:T(8,128)(2,1)}, bf16[16,4,128,128]{3,2,1,0:T(8,128)(2,1)}, u32[]{:S(2)}, u32[]{:S(2)}) collective-permute-start(bf16[16,4,128,128]{3,2,1,0:T(8,128)(2,1)} %expand_half.3), channel_id=1, source_target_pairs={{0,16},{16,0},{1,17},{17,1},{2,18},{18,2},{3,19},{19,3},{4,20},{20... | collective-permute-start | bytes 6291464 | tf_op jit(solution)/shard_map/ppermute | solution.py:363
  67.7 4.0 %copy-start.3 = (bf16[4096,5,256]{2,0,1:T(8,128)(2,1)S(1)}, bf16[4096,5,256]{2,0,1:T(8,128)(2,1)}, u32[]{:S(2)}) copy-start(bf16[4096,5,256]{2,0,1:T(8,128)(2,1)} %param.7) | copy-start | bytes 31457284
  79.4 40.5 %all-to-all-start.1 = ((bf16[64,128,128]{2,1,0:T(8,128)(2,1)}), bf16[64,128,128]{2,1,0:T(8,128)(2,1)S(1)}, u32[]{:S(2)}, u32[]{:S(2)}) async-start(bf16[64,128,128]{2,1,0:T(8,128)(2,1)} %bitcast.27), calls=%async_computation.1 | async-start | bytes 4194304 | tf_op jit(solution)/shard_map/all_to_all | solution.py:330
  156.7 22.5 %collective-permute-start.1 = (bf16[16,4,128,128]{3,2,1,0:T(8,128)(2,1)S(1)}, bf16[16,4,128,128]{3,2,1,0:T(8,128)(2,1)}, u32[]{:S(2)}, u32[]{:S(2)}) collective-permute-start(bf16[16,4,128,128]{3,2,1,0:T(8,128)(2,1)S(1)} %bitcast.114), channel_id=1, source_target_pairs={{0,16},{16,0},{1,17},{17,1},{2,18},{18,2},{3,19},{19,3},{4,20},{20... | collective-permute-start | bytes 6291464 | tf_op jit(solution)/shard_map/ppermute | solution.py:374
  158.7 2.2 copy-start.4
  160.9 7.1 %copy-start.5 = (bf16[64,128,256]{2,1,0:T(8,128)(2,1)S(1)}, bf16[64,128,256]{2,1,0:T(8,128)(2,1)}, u32[]{:S(2)}) copy-start(bf16[64,128,256]{2,1,0:T(8,128)(2,1)} %all-gather.3.cloned.1.call-done) | copy-start | bytes 12582916
  211.8 2.2 collective-permute-start.2
  214.0 24.0 %copy-start.1 = (bf16[4096,128]{1,0:T(8,128)(2,1)S(1)}, bf16[4096,128]{1,0:T(8,128)(2,1)}, u32[]{:S(2)}) copy-start(bf16[4096,128]{1,0:T(8,128)(2,1)} %param.10) | copy-start | bytes 3145732
  216.3 20.9 %all-to-all-start.3 = ((bf16[64,8,5,128]{3,1,2,0:T(8,128)(2,1)}), bf16[64,8,5,128]{3,1,2,0:T(8,128)(2,1)S(1)}, u32[]{:S(2)}, u32[]{:S(2)}) async-start(bf16[64,8,5,128]{3,1,2,0:T(8,128)(2,1)} %bitcast.43), calls=%async_computation.3 | async-start | bytes 1310720 | tf_op jit(solution)/shard_map/all_to_all | solution.py:330
Sparse Core Ops, SparseCore 0:
  67.8 90.9 all-gather.2
where the time goes:
time: 246 us; the launch traced here: 245 us
  waiting for transfers between devices  67.9 us (28%)
  Pallas kernels  41.7 us (17%)
  blocking collectives  35.9 us (15%)
  matrix products  34.3 us (14%)
  local copies, waits for them, and re-layouts  24.7 us (10%)
  starting transfers between devices  19.8 us (8%)
  between operations  14.3 us (6%)
  other arithmetic  6.35 us (3%)
    all_to_all x2, waiting for transfers between devices, summed_over_chips(): return lax.all_to_all(half, CHIPS, 0, 0, tiled=True).astype(f32).sum(axis=0)  45.2 us
    all_to_all x1, blocking collectives, body(): lax.all_to_all(jnp.broadcast_to(piece[None], (blocks * physical, columns,...  35.9 us
    all_to_all x1, waiting for transfers between devices, body(): lax.all_to_all(applied, MPO, split_axis=0, concat_axis=2, tiled=True)  18.7 us
    dot_general x1, matrix products, body(): jnp.einsum('asb,kwb->wska', site_tensor, sketch_expand, preferred_element...  16.3 us
    all_to_all x2, starting transfers between devices, summed_over_chips(): return lax.all_to_all(half, CHIPS, 0, 0, tiled=True).astype(f32).sum(axis=0)  15.2 us
    pallas_call x1, Pallas kernels, finish(): pl.pallas_call(kernel, grid_spec=pltpu.PrefetchScalarGridSpec(num_scalar_...  14.7 us
    pallas_call x1, Pallas kernels, site_terms(): pl.pallas_call(kernel, grid=(blocks // step,), in_specs=[pl.BlockSpec((wi...  11.2 us
    unnamed x18, local copies, waits for them, and re-layouts  10.2 us
  transfers between devices with their start and end apart: 7, of which 5 were waited for; matrix products, arithmetic and copies ran while one was open for 6% of the time, Pallas kernels for 9%

commit v1 on v0

--- a/solution.py
+++ b/solution.py
@@ -231,15 +231,17 @@
     return high, (v - high.astype(f32)).astype(bf16)
 
 
-def finish(scalars, env, site, half, x_site, g_site, x_own, g_own, own, site_local):
+def finish(scalars, env, site, half, x_site, g_site, x_own, g_own, own, site_local, operator):
     width, blocks, _, share, depth = env.shape
     s, k = half.shape[1:3]
     step = 4
     last = blocks // step - 1
+    pad = operator.shape[0] // 2
+    out_rows = pad - 4
 
     def kernel(
-        sc_ref, e_ref, s_ref, h_ref, xs_ref, gs_ref, xo_ref, go_ref, own_ref, oth_ref, sl_ref,
-        p_ref, b_ref, x_ref, g_ref,
+        sc_ref, e_ref, s_ref, h_ref, xs_ref, gs_ref, xo_ref, go_ref, own_ref, oth_ref, sl_ref, m_ref,
+        b_ref, give_ref, keep_ref, x_ref, g_ref, p_ref,
     ):
         first = pl.program_id(0) == 0
         terms, gram = expand_step(e_ref, s_ref, h_ref)
@@ -279,7 +281,12 @@
             for w in range(width):
                 for i in range(s):
                     part = slice(i * k, (i + 1) * k)
-                    p_ref[w, part] = apply(xs_ref[w, part] + mix * x_ref[w, part]).astype(bf16)
+                    value = apply(xs_ref[w, part] + mix * x_ref[w, part])
+                    p_ref[:, pl.ds(w * s + i, k, stride=pad), :] = jnp.stack(
+                        [value[:, h * k : (h + 1) * k] for h in range(depth // k)], axis=0
+                    )
+            for i in range(width * s, pad):
+                p_ref[:, pl.ds(i, k, stride=pad), :] = jnp.zeros((depth // k, k, k), f32)
             even = sc_ref[0] == 1
             for i in range(s):
                 a0 = own_ref[0, i].astype(f32)
@@ -289,6 +296,39 @@
                 )
                 done = apply(sl_ref[i] + mix * rows)
                 b_ref[:, i * k : (i + 1) * k] = done.T.astype(bf16)
+
+            operator_rows = jnp.concatenate([m_ref[...], m_ref[...]], axis=1)
+
+            def group(g, carry):
+                lines = pl.ds(pl.multiple_of(g * (8 * pad), 8 * pad), 8 * pad)
+                left = jnp.concatenate(
+                    [p_ref[h, lines, :] for h in range(depth // k)], axis=1
+                ).astype(bf16)
+                paired = dot(left, b_ref[...], ((1,), (0,)))
+                for q in range(0, 8, 2):
+                    block = jnp.concatenate(
+                        [
+                            jnp.concatenate(
+                                [
+                                    paired[r * pad : (r + 1) * pad, t * k : (t + 1) * k]
+                                    for t in range(s)
+                                ],
+                                axis=0,
+                            )
+                            for r in (q, q + 1)
+                        ],
+                        axis=1,
+                    )
+                    bh, bl = split(block)
+                    done = dot(operator_rows, jnp.concatenate([bh, bl], axis=0), ((1,), (0,)))
+                    for r in (0, 1):
+                        piece = done[:, r * k : (r + 1) * k]
+                        to = pl.ds(q + r, out_rows, stride=8)
+                        give_ref[g, to, :] = piece[:out_rows]
+                        keep_ref[g, to, :] = piece[pad : pad + out_rows]
+                return carry
+
+            lax.fori_loop(0, k // 8, group, 0)
 
     fixed3 = lambda i, sc: (0, 0, 0)
     fixed2 = lambda i, sc: (0, 0)
@@ -306,24 +346,28 @@
                 pl.BlockSpec((1, s, k, share), lambda i, sc: (sc[1], 0, 0, 0)),
                 pl.BlockSpec((1, s, k, share), lambda i, sc: (sc[1], 0, 0, 0)),
                 pl.BlockSpec((s, k, 2 * share), fixed3),
+                pl.BlockSpec(operator.shape, fixed2),
             ],
             out_specs=[
-                pl.BlockSpec((width, s * k, depth), fixed3),
                 pl.BlockSpec((2 * share, s * k), fixed2),
+                pl.BlockSpec((k // 8, 8 * out_rows, k), fixed3),
+                pl.BlockSpec((k // 8, 8 * out_rows, k), fixed3),
             ],
             scratch_shapes=[
                 pltpu.VMEM((width, s * k, depth), f32),
                 pltpu.VMEM((k, 2 * k), f32),
+                pltpu.VMEM((depth // k, k * pad, k), f32),
             ],
         ),
         out_shape=[
-            jax.ShapeDtypeStruct((width, s * k, depth), bf16),
             jax.ShapeDtypeStruct((2 * share, s * k), bf16),
+            jax.ShapeDtypeStruct((k // 8, 8 * out_rows, k), f32),
+            jax.ShapeDtypeStruct((k // 8, 8 * out_rows, k), f32),
         ],
         compiler_params=pltpu.CompilerParams(vmem_limit_bytes=VMEM),
         cost_estimate=cost(4_000_000_000, 20_000_000),
         name="finish",
-    )(scalars, env, site, half, x_site, g_site, x_own, g_own, own, half, site_local)
+    )(scalars, env, site, half, x_site, g_site, x_own, g_own, own, half, site_local, operator)
 
 
 def summed_over_chips(half):
@@ -346,9 +390,11 @@
     own_core = core.reshape(1).astype(jnp.int32)
     other_core = 1 - own_core
 
-    site_y = jnp.einsum("asb,bk->ska", site_tensor, sketch_site, preferred_element_type=f32)
-    site_local = site_y * jnp.transpose(mask_rows, (1, 2, 0))
-    site_all = lax.all_gather(site_local.astype(bf16), BOND, axis=0)
+    operator = lax.dynamic_slice_in_dim(mpo_tensor, mpo_index * width, width, 0)
+    operator = jnp.transpose(operator.reshape(width, 4, 2, -1, physical, physical), (2, 1, 3, 5, 0, 4))
+    operator = operator.reshape(2, -1, physical, width * physical)
+    operator = jnp.pad(operator, ((0, 0), (0, 4), (0, 0), (0, 4)))
+    operator = jnp.where(core == 0, operator[::-1], operator).reshape(2 * operator.shape[1], -1)
 
     sketched = jnp.einsum(
         "asb,kwb->wska", site_tensor, sketch_expand, preferred_element_type=f32
@@ -356,14 +402,22 @@
     applied = jnp.einsum(
         "vwst,wtka->vska", mpo_tensor, sketched, preferred_element_type=f32
     ).astype(bf16)
+    applied, sketch_site = lax.optimization_barrier((applied, sketch_site))
+    site_y = jnp.einsum("asb,bk->ska", site_tensor, sketch_site, preferred_element_type=f32)
+    site_local = site_y * jnp.transpose(mask_rows, (1, 2, 0))
+    site_all = lax.all_gather(site_local.astype(bf16), BOND, axis=0)
     contracted = lax.all_to_all(applied, MPO, split_axis=0, concat_axis=2, tiled=True)
+    contracted, site_local = lax.optimization_barrier((contracted, site_local))
     contracted = contracted.reshape(width, physical * columns, depth)
 
     send = expand_half(other_core, env_halves, contracted)
     got = lax.ppermute(send, CORE, SWAP)
     keep = expand_half(own_core, env_halves, contracted)
     half = (keep.astype(f32) + got.astype(f32)).astype(bf16)
-    piece = summed_over_chips(half.reshape(blocks * physical, share, columns))
+    x_site, g_site = site_terms(env.reshape(width, blocks, local_rows, depth), site_all)
+    arrived = lax.all_to_all(half.reshape(-1, share, columns), CHIPS, 0, 0, tiled=True)
+    arrived, x_site, g_site = lax.optimization_barrier((arrived, x_site, g_site))
+    piece = arrived.astype(f32).sum(axis=0)
     mask_piece = lax.dynamic_slice(
         mask_rows, (core * share, lax.axis_index("mpo_0"), 0), (share, 1, columns)
     )[:, 0]
@@ -373,27 +427,17 @@
     ).reshape(blocks, physical, columns, share)
     other = lax.ppermute(own, CORE, SWAP)
 
-    x_site, g_site = site_terms(env.reshape(width, blocks, local_rows, depth), site_all)
     x_own, g_own = expand_terms(own_core, env_halves, site_all, own)
     scalars = jnp.concatenate([other_core, bond_index.reshape(1).astype(jnp.int32)])
-    projected, basis_flat = finish(
-        scalars, env_halves, site_all, other, x_site, g_site, x_own, g_own, own, site_local
+    basis_flat, give, kept = finish(
+        scalars, env_halves, site_all, other, x_site, g_site, x_own, g_own, own, site_local, operator
     )
     basis_local = basis_flat.reshape(local_rows, physical, columns)
 
-    paired = jnp.einsum(
-        "wxc,cy->wxy", projected, basis_flat, preferred_element_type=f32
-    ).reshape(width, physical, columns, physical, columns)
-    operator_rows = lax.dynamic_slice_in_dim(mpo_tensor, mpo_index * width, width, 0)
-    share_out = jnp.einsum(
-        "wvst,wsktl->kvl", operator_rows.astype(f32), paired, precision=lax.Precision.HIGH
-    ).astype(bf16)
-    kout, vout = columns // 16, mpo_tensor.shape[1] // 8
-    parts = share_out.reshape(16, kout, 4, 2, vout, columns).transpose(3, 0, 2, 1, 4, 5)
-    mine = lax.dynamic_index_in_dim(parts, core, 0, keepdims=False)
-    sent = lax.dynamic_index_in_dim(parts, 1 - core, 0, keepdims=False)
-    both = (mine.astype(f32) + lax.ppermute(sent, CORE, SWAP).astype(f32)).astype(bf16)
-    extended = summed_over_chips(both.reshape(64, kout, vout, columns))
+    both = (kept + lax.ppermute(give, CORE, SWAP)).astype(bf16)
+    chips = blocks * physical
+    extended = summed_over_chips(both.reshape(chips, -1, columns))
+    extended = jnp.swapaxes(extended.reshape(-1, 8, columns), 0, 1)
     return (basis_local, extended)
 
 

time: 246 us -> 218 us (0.89)
  waiting for transfers between devices: 67.9 us -> 51.6 us
  matrix products: 34.3 us -> 23.2 us
  Pallas kernels: 41.7 us -> 47 us
  local copies, waits for them, and re-layouts: 24.7 us -> 20.5 us
    all_to_all x2 -> x1, waiting for transfers between devices: 45.2 us -> 14.5 us  [summed_over_chips(): return lax.all_to_all(half, CHIPS, 0, 0, tiled=True).astype(f32).sum(axis=0)]
    all_to_all x0 -> x1, waiting for transfers between devices: none -> 15.2 us  [body(): lax.all_to_all(half.reshape(-1, share, columns), CHIPS, 0, 0, tiled=True)]
    all_to_all x2 -> x1, starting transfers between devices: 15.2 us -> 5.19 us  [summed_over_chips(): return lax.all_to_all(half, CHIPS, 0, 0, tiled=True).astype(f32).sum(axis=0)]
    all_to_all x0 -> x1, starting transfers between devices: none -> 9.76 us  [body(): lax.all_to_all(half.reshape(-1, share, columns), CHIPS, 0, 0, tiled=True)]
    dot_general x2 -> x0, matrix products: 8.01 us -> none  [the longest x1 4.86 us: body(): jnp.einsum('wvst,wsktl->kvl', operator_rows.astype(f32), paired, precisio...]
    reshape x1 -> x3, local copies, waits for them, and re-layouts: 7.21 us -> 0.38 us  [the longest x1 0.15 us: body(): operator.reshape(width, 4, 2, -1, physical, physical)]
    pallas_call x1, Pallas kernels: 14.7 us -> 20.9 us  [finish(): pl.pallas_call(kernel, grid_spec=pltpu.PrefetchScalarGridSpec(num_scalar_...]
    convert_element_type x3 -> x0, local copies, waits for them, and re-layouts: 4.16 us -> none  [the longest x1 1.79 us: body(): applied = jnp.einsum('vwst,wtka->vska', mpo_tensor, sketched, preferred_e...]
  transfers between devices with their start and end apart: 7 -> 7, of which waited for: 5 -> 5; matrix products, arithmetic and copies ran while one was open for 6% -> 3% of each run, Pallas kernels for 9% -> 12%
where the time goes in v1:
time: 218 us; the launch traced here: 217 us
  waiting for transfers between devices  51.6 us (24%)
  Pallas kernels  47 us (22%)
  blocking collectives  35.2 us (16%)
  matrix products  23.2 us (11%)
  local copies, waits for them, and re-layouts  20.5 us (9%)
  starting transfers between devices  20.2 us (9%)
  between operations  14.3 us (7%)
  other arithmetic  4.74 us (2%)
    all_to_all x1, blocking collectives, body(): lax.all_to_all(jnp.broadcast_to(piece[None], (blocks * physical, columns,...  35.2 us
    pallas_call x1, Pallas kernels, finish(): pl.pallas_call(kernel, grid_spec=pltpu.PrefetchScalarGridSpec(num_scalar_...  20.9 us
    all_to_all x1, waiting for transfers between devices, body(): lax.all_to_all(applied, MPO, split_axis=0, concat_axis=2, tiled=True)  18.8 us
    dot_general x1, matrix products, body(): jnp.einsum('asb,kwb->wska', site_tensor, sketch_expand, preferred_element...  16.3 us
    all_to_all x1, waiting for transfers between devices, body(): lax.all_to_all(half.reshape(-1, share, columns), CHIPS, 0, 0, tiled=True)  15.2 us
    all_to_all x1, waiting for transfers between devices, summed_over_chips(): return lax.all_to_all(half, CHIPS, 0, 0, tiled=True).astype(f32).sum(axis=0)  14.5 us
    unnamed x20, local copies, waits for them, and re-layouts  14 us
    pallas_call x1, Pallas kernels, site_terms(): pl.pallas_call(kernel, grid=(blocks // step,), in_specs=[pl.BlockSpec((wi...  11.2 us
  transfers between devices with their start and end apart: 7, of which 5 were waited for; matrix products, arithmetic and copies ran while one was open for 3% of the time, Pallas kernels for 12%

profile of v1, /device:TPU:0, one launch (start us, length us, event | category | flops | bytes accessed | tf_op | source)
XLA Modules:
  0.0 216.7 jit_solution(11461228566013014938)
XLA Ops:
  7.2 0.8 slice_bitcast_fusion.5
  8.0 0.7 slice_bitcast_fusion.3
  8.7 16.3 %fusion.12 = bf16[40,4,16,256,1]{3,0,1,4,2:T(8,128)(2,1)S(1)} fusion(bf16[256,4,4096]{2,1,0:T(4,128)(2,1)} %param.8, bf16[16,40,4096]{2,1,0:T(8,128)(2,1)} %param.11), kind=kOutput, calls=%fused_computation.11 | convolution fusion | flops 5369364480 | bytes 14942208 | tf_op jit(solution)/shard_map/asb,kwb->wska/dot_general | solution.py:399
  25.0 0.6 fusion.11
  25.6 6.4 %fusion.28 = (bf16[4,128,256]{2,1,0:T(8,128)(2,1)}, f32[4,128,256]{2,1,0:T(8,128)}) fusion(bf16[256,4,4096]{2,1,0:T(4,128)(2,1)S(1)} %copy-done.9, bf16[4096,128]{1,0:T(8,128)(2,1)S(1)} %copy-done, s32[128]{0:T(128)S(1)} %get-tuple-element.35, s32[4,256]{1,0:T(4,128)S(1)} %get-tuple-element.32, s32[128]{0:T(128)S(1)} %get-tuple-element.34, ...), kind=kOutput, calls=%fused_computation.31 | convolution fusion | flops 1074397184 | bytes 10232832 | tf_op jit(solution)/shard_map/asb,bk->ska/dot_general | solution.py:406
  32.0 1.8 copy.31
  33.8 4.4 %all-to-all-start = ((bf16[40,4,16,256]{3,1,2,0:T(4,128)(2,1)}), bf16[40,4,16,256]{3,1,2,0:T(4,128)(2,1)S(1)}, u32[]{:S(2)}, u32[]{:S(2)}) async-start(bf16[40,4,16,256]{3,1,2,0:T(4,128)(2,1)} %copy.31), calls=%async_computation | async-start | bytes 2621440 | tf_op jit(solution)/shard_map/all_to_all | solution.py:409
  38.2 18.8 %all-to-all-done = bf16[40,4,16,256]{3,1,2,0:T(4,128)(2,1)S(1)} async-done(((bf16[40,4,16,256]{3,1,2,0:T(4,128)(2,1)}), bf16[40,4,16,256]{3,1,2,0:T(4,128)(2,1)S(1)}, u32[]{:S(2)}, u32[]{:S(2)}) %all-to-all-start) | async-done | bytes 1310752 | tf_op jit(solution)/shard_map/all_to_all | solution.py:409
  57.5 4.0 %copy-done.1 = bf16[4096,5,256]{2,0,1:T(8,128)(2,1)S(1)} copy-done((bf16[4096,5,256]{2,0,1:T(8,128)(2,1)S(1)}, bf16[4096,5,256]{2,0,1:T(8,128)(2,1)}, u32[]{:S(2)}) %copy-start.1) | copy-done | bytes 10485784
  61.5 3.9 %expand_half.3 = bf16[16,4,128,128]{3,2,1,0:T(8,128)(2,1)S(1)} custom-call(s32[1]{0:T(128)S(6)} %sub.3.core_ref, bf16[5,16,2,128,256]{4,3,2,1,0:T(8,128)(2,1)S(1)} %bitcast.91, bf16[5,512,256]{2,1,0:T(8,128)(2,1)S(1)} %bitcast.99), custom_call_target="tpu_custom_call" | custom-call | flops 2684354560 | bytes 9000000 | tf_op jit(solution)/shard_map/expand_half/pallas_call | solution.py:53
  65.5 4.1 %copy-done.2 = bf16[4096,5,256]{2,0,1:T(8,128)(2,1)S(1)} copy-done((bf16[4096,5,256]{2,0,1:T(8,128)(2,1)S(1)}, bf16[4096,5,256]{2,0,1:T(8,128)(2,1)}, u32[]{:S(2)}) %copy-start.2) | copy-done | bytes 10485784
  69.5 3.9 %expand_half.2 = bf16[16,4,128,128]{3,2,1,0:T(8,128)(2,1)S(1)} custom-call(s32[1]{0:T(128)} %bitcast.core_ref, bf16[5,16,2,128,256]{4,3,2,1,0:T(8,128)(2,1)S(1)} %bitcast.92, bf16[5,512,256]{2,1,0:T(8,128)(2,1)S(1)} %bitcast.100), custom_call_target="tpu_custom_call" | custom-call | flops 2684354560 | bytes 9000000 | tf_op jit(solution)/shard_map/expand_half/pallas_call | solution.py:53
  73.4 2.5 %add_convert_fusion = bf16[16,4,128,128]{3,2,1,0:T(8,128)(2,1)} fusion(bf16[16,4,128,128]{3,2,1,0:T(8,128)(2,1)S(1)} %collective-permute-done, bf16[16,4,128,128]{3,2,1,0:T(8,128)(2,1)S(1)} %expand_half.2), kind=kLoop, calls=%fused_computation.7 | loop fusion | flops 4194304 | bytes 6291456 | tf_op jit(solution)/shard_map/convert_element_type | solution.py:416
  75.9 9.8 %all-to-all-start.1 = ((bf16[64,128,128]{2,1,0:T(8,128)(2,1)}), bf16[64,128,128]{2,1,0:T(8,128)(2,1)S(1)}, u32[]{:S(2)}, u32[]{:S(2)}) async-start(bf16[64,128,128]{2,1,0:T(8,128)(2,1)} %bitcast.28), calls=%async_computation.1 | async-start | bytes 4194304 | tf_op jit(solution)/shard_map/all_to_all | solution.py:418
  85.9 0.5 all-gather.3.cloned.1.call-done
  86.3 2.2 %copy-done.3 = bf16[64,128,256]{2,1,0:T(8,128)(2,1)S(1)} copy-done((bf16[64,128,256]{2,1,0:T(8,128)(2,1)S(1)}, bf16[64,128,256]{2,1,0:T(8,128)(2,1)}, u32[]{:S(2)}) %copy-start.3) | copy-done | bytes 4194328
  88.5 11.2 %site_terms.1 = (f32[5,512,256]{2,1,0:T(8,128)S(1)}, f32[128,128]{1,0:T(8,128)S(1)}) custom-call(bf16[5,16,256,256]{3,2,1,0:T(8,128)(2,1)} %bitcast.88, bf16[16,4,128,256]{3,2,1,0:T(8,128)(2,1)S(1)} %bitcast.97), custom_call_target="tpu_custom_call" | custom-call | flops 6000000000 | bytes 17000000 | tf_op jit(solution)/shard_map/site_terms/pallas_call | solution.py:98
  99.7 1.5 copy-done.5
  101.2 15.2 %all-to-all-done.1 = bf16[64,128,128]{2,1,0:T(8,128)(2,1)S(1)} async-done(((bf16[64,128,128]{2,1,0:T(8,128)(2,1)}), bf16[64,128,128]{2,1,0:T(8,128)(2,1)S(1)}, u32[]{:S(2)}, u32[]{:S(2)}) %all-to-all-start.1) | async-done | bytes 2097184 | tf_op jit(solution)/shard_map/all_to_all | solution.py:418
  116.9 0.5 broadcast_in_dim.2
  117.4 35.2 %all_to_all.33 = bf16[64,128,128]{2,1,0:T(8,128)(2,1)S(1)} all-to-all(bf16[64,128,128]{2,1,0:T(8,128)(2,1)S(1)} %broadcast_in_dim.2), channel_id=1, replica_groups=mesh['mpo_0'=4,'mpo_1'=2,'bond_0'=4,'bond_1'=4] {'bond_0','bond_1','mpo_0'}, dimensions={0} | all-to-all | bytes 4194304 | tf_op jit(solution)/shard_map/all_to_all | solution.py:425
  152.6 0.7 constant_dynamic-slice_fusion
  154.0 2.2 %copy-done.4 = bf16[64,128,256]{2,1,0:T(8,128)(2,1)S(1)} copy-done((bf16[64,128,256]{2,1,0:T(8,128)(2,1)S(1)}, bf16[64,128,256]{2,1,0:T(8,128)(2,1)}, u32[]{:S(2)}) %copy-start.4) | copy-done | bytes 4194328
  156.2 7.1 %expand_terms.1 = (f32[5,512,256]{2,1,0:T(8,128)S(1)}, f32[128,256]{1,0:T(8,128)S(1)}) custom-call(s32[1]{0:T(128)} %bitcast.core_ref, bf16[5,16,2,128,256]{4,3,2,1,0:T(8,128)(2,1)} %bitcast.89, bf16[16,4,128,256]{3,2,1,0:T(8,128)(2,1)S(1)} %bitcast.98, bf16[16,4,128,128]{3,2,1,0:T(8,128)(2,1)S(1)} %bitcast.94), custom_call_target="tpu_custom_call" | custom-call | flops 3300000000 | bytes 12000000 | tf_op jit(solution)/shard_map/expand_terms/pallas_call | solution.py:162
  163.4 20.9 %finish.1 = (bf16[256,512]{1,0:T(8,128)(2,1)S(1)}, f32[16,160,128]{2,1,0:T(8,128)S(1)}, f32[16,160,128]{2,1,0:T(8,128)S(1)}) custom-call(s32[2]{0:T(128)S(1)} %pad_add_fusion.sc_ref, bf16[5,16,2,128,256]{4,3,2,1,0:T(8,128)(2,1)} %bitcast.90, bf16[16,4,128,256]{3,2,1,0:T(8,128)(2,1)} %bitcast.96, ...), custom_call_target="tpu_custom_call" | custom-call | flops 4000000000 | bytes 20000000 | tf_op jit(solution)/shard_map/finish/pallas_call | solution.py:335
  184.3 0.7 collective-permute-start.2
  185.0 2.7 %collective-permute-done.2 = f32[16,160,128]{2,1,0:T(8,128)S(1)} collective-permute-done((f32[16,160,128]{2,1,0:T(8,128)S(1)}, f32[16,160,128]{2,1,0:T(8,128)S(1)}, u32[]{:S(2)}, u32[]{:S(2)}) %collective-permute-start.2) | collective-permute-done | bytes 1310752 | tf_op jit(solution)/shard_map/ppermute | solution.py:437
  187.6 1.0 add_convert_fusion.1
  188.6 5.2 %all-to-all-start.3 = ((bf16[64,40,128]{2,1,0:T(8,128)(2,1)}), bf16[64,40,128]{2,1,0:T(8,128)(2,1)S(1)}, u32[]{:S(2)}, u32[]{:S(2)}) async-start(bf16[64,40,128]{2,1,0:T(8,128)(2,1)} %bitcast.34), calls=%async_computation.3 | async-start | bytes 1310720 | tf_op jit(solution)/shard_map/all_to_all | solution.py:374
  193.8 0.8 reshape.58
  194.6 14.5 %all-to-all-done.3 = bf16[64,40,128]{2,1,0:T(8,128)(2,1)S(1)} async-done(((bf16[64,40,128]{2,1,0:T(8,128)(2,1)}), bf16[64,40,128]{2,1,0:T(8,128)(2,1)S(1)}, u32[]{:S(2)}, u32[]{:S(2)}) %all-to-all-start.3) | async-done | bytes 655392 | tf_op jit(solution)/shard_map/all_to_all | solution.py:374
  209.1 0.7 convert_reduce_fusion.1
  (36 shorter events, 2.0 us)
Async XLA Ops:
  7.2 18.4 %copy-start = (bf16[4096,128]{1,0:T(8,128)(2,1)S(1)}, bf16[4096,128]{1,0:T(8,128)(2,1)}, u32[]{:S(2)}) copy-start(bf16[4096,128]{1,0:T(8,128)(2,1)} %param.10) | copy-start | bytes 3145732
  7.2 79.1 %all-gather.3.cloned.1.call-start = ((), (), s32[]{:S(2)}) async-start(), calls=%async_computation.4 | async-start | bytes 4456448 | tf_op jit(solution)/shard_map/all_gather | solution.py:408
  8.7 16.3 %copy-start.8 = (bf16[40,40,4,4]{1,3,2,0:T(4,128)(2,1)S(1)}, bf16[40,40,4,4]{1,3,2,0:T(4,128)(2,1)}, u32[]{:S(2)}) copy-start(bf16[40,40,4,4]{1,3,2,0:T(4,128)(2,1)} %param.9) | copy-start | bytes 153604
  8.7 16.9 %copy-start.9 = (bf16[256,4,4096]{2,1,0:T(4,128)(2,1)S(1)}, bf16[256,4,4096]{2,1,0:T(4,128)(2,1)}, u32[]{:S(2)}) copy-start(bf16[256,4,4096]{2,1,0:T(4,128)(2,1)} %param.8) | copy-start | bytes 25165828
  33.8 23.2 %all-to-all-start = ((bf16[40,4,16,256]{3,1,2,0:T(4,128)(2,1)}), bf16[40,4,16,256]{3,1,2,0:T(4,128)(2,1)S(1)}, u32[]{:S(2)}, u32[]{:S(2)}) async-start(bf16[40,4,16,256]{3,1,2,0:T(4,128)(2,1)} %copy.31), calls=%async_computation | async-start | bytes 2621440 | tf_op jit(solution)/shard_map/all_to_all | solution.py:409
  57.4 4.0 %copy-start.1 = (bf16[4096,5,256]{2,0,1:T(8,128)(2,1)S(1)}, bf16[4096,5,256]{2,0,1:T(8,128)(2,1)}, u32[]{:S(2)}) copy-start(bf16[4096,5,256]{2,0,1:T(8,128)(2,1)} %param.7) | copy-start | bytes 31457284
  65.4 8.1 %collective-permute-start = (bf16[16,4,128,128]{3,2,1,0:T(8,128)(2,1)S(1)}, bf16[16,4,128,128]{3,2,1,0:T(8,128)(2,1)S(1)}, u32[]{:S(2)}, u32[]{:S(2)}) collective-permute-start(bf16[16,4,128,128]{3,2,1,0:T(8,128)(2,1)S(1)} %expand_half.3), channel_id=1, source_target_pairs={{0,16},{16,0},{1,17},{17,1},{2,18},{18,2},{3,19},{19,3},{4,20},{20... | collective-permute-start | bytes 6291464 | tf_op jit(solution)/shard_map/ppermute | solution.py:414
  65.5 4.1 %copy-start.2 = (bf16[4096,5,256]{2,0,1:T(8,128)(2,1)S(1)}, bf16[4096,5,256]{2,0,1:T(8,128)(2,1)}, u32[]{:S(2)}) copy-start(bf16[4096,5,256]{2,0,1:T(8,128)(2,1)} %param.7) | copy-start | bytes 31457284
  75.9 40.4 %all-to-all-start.1 = ((bf16[64,128,128]{2,1,0:T(8,128)(2,1)}), bf16[64,128,128]{2,1,0:T(8,128)(2,1)S(1)}, u32[]{:S(2)}, u32[]{:S(2)}) async-start(bf16[64,128,128]{2,1,0:T(8,128)(2,1)} %bitcast.28), calls=%async_computation.1 | async-start | bytes 4194304 | tf_op jit(solution)/shard_map/all_to_all | solution.py:418
  86.3 2.2 %copy-start.3 = (bf16[64,128,256]{2,1,0:T(8,128)(2,1)S(1)}, bf16[64,128,256]{2,1,0:T(8,128)(2,1)}, u32[]{:S(2)}) copy-start(bf16[64,128,256]{2,1,0:T(8,128)(2,1)} %all-gather.3.cloned.1.call-done) | copy-start | bytes 12582916
  99.7 1.5 copy-start.5
  152.6 10.8 %collective-permute-start.1 = (bf16[16,4,128,128]{3,2,1,0:T(8,128)(2,1)S(1)}, bf16[16,4,128,128]{3,2,1,0:T(8,128)(2,1)}, u32[]{:S(2)}, u32[]{:S(2)}) collective-permute-start(bf16[16,4,128,128]{3,2,1,0:T(8,128)(2,1)S(1)} %bitcast.93), channel_id=1, source_target_pairs={{0,16},{16,0},{1,17},{17,1},{2,18},{18,2},{3,19},{19,3},{4,20},{20... | collective-permute-start | bytes 6291464 | tf_op jit(solution)/shard_map/ppermute | solution.py:428
  154.0 2.2 %copy-start.4 = (bf16[64,128,256]{2,1,0:T(8,128)(2,1)S(1)}, bf16[64,128,256]{2,1,0:T(8,128)(2,1)}, u32[]{:S(2)}) copy-start(bf16[64,128,256]{2,1,0:T(8,128)(2,1)} %all-gather.3.cloned.1.call-done) | copy-start | bytes 12582916
  156.2 7.1 %copy-start.6 = (f32[5,512,256]{2,1,0:T(8,128)S(1)}, f32[5,512,256]{2,1,0:T(8,128)}, u32[]{:S(2)}) copy-start(f32[5,512,256]{2,1,0:T(8,128)} %copy-done.5) | copy-start | bytes 7864324
  156.2 7.1 %copy-start.7 = (f32[4,128,256]{2,1,0:T(8,128)S(1)}, f32[4,128,256]{2,1,0:T(8,128)}, u32[]{:S(2)}) copy-start(f32[4,128,256]{2,1,0:T(8,128)} %get-tuple-element.26.sl_ref) | copy-start | bytes 1572868
  184.3 3.4 %collective-permute-start.2 = (f32[16,160,128]{2,1,0:T(8,128)S(1)}, f32[16,160,128]{2,1,0:T(8,128)S(1)}, u32[]{:S(2)}, u32[]{:S(2)}) collective-permute-start(f32[16,160,128]{2,1,0:T(8,128)S(1)} %get-tuple-element.29), channel_id=1, source_target_pairs={{0,16},{16,0},{1,17},{17,1},{2,18},{18,2},{3,19},{19,3},{4,20},{20... | collective-permute-start | bytes 3932168 | tf_op jit(solution)/shard_map/ppermute | solution.py:437
  188.6 20.5 %all-to-all-start.3 = ((bf16[64,40,128]{2,1,0:T(8,128)(2,1)}), bf16[64,40,128]{2,1,0:T(8,128)(2,1)S(1)}, u32[]{:S(2)}, u32[]{:S(2)}) async-start(bf16[64,40,128]{2,1,0:T(8,128)(2,1)} %bitcast.34), calls=%async_computation.3 | async-start | bytes 1310720 | tf_op jit(solution)/shard_map/all_to_all | solution.py:374
Sparse Core Ops, SparseCore 0:
  32.2 54.1 all-gather.2

commit v2 on v1

--- a/solution.py
+++ b/solution.py
@@ -16,7 +16,7 @@
 shift_tolerance = 1e-06
 f32 = jnp.float32
 bf16 = jnp.bfloat16
-VMEM = 40 * 1024 * 1024
+MIB = 1024 * 1024
 
 
 def sector_mask(row_labels, column_labels):
@@ -30,8 +30,79 @@
     return lax.dot_general(a, b, (dims, ((), ())), preferred_element_type=f32)
 
 
+def in_hbm(value):
+    return pltpu.with_memory_space_constraint(value, pltpu.HBM)
+
+
 def cost(flops, size):
     return pl.CostEstimate(flops=flops, bytes_accessed=size, transcendentals=0)
+
+
+def sketch(site_tensor, sketch_expand, sketch_site, width):
+    rows, s, depth = site_tensor.shape
+    k, v, _ = sketch_expand.shape
+    columns = sketch_site.shape[1]
+    share = 128
+    halves, lines = rows // share, share * s
+    last = depth // width - 1
+
+    def kernel(s_ref, o_ref, w_ref, y_ref, z_ref, total, site_total):
+        step = pl.program_id(0)
+        expand = o_ref[...].reshape(k * v, width)
+        for h in range(halves):
+            block = s_ref[h * share : (h + 1) * share].reshape(lines, width)
+
+            @pl.when(step == 0)
+            def _():
+                total[h] = dot(expand, block, ((1,), (1,)))
+                site_total[h] = dot(block, w_ref[...], ((1,), (0,)))
+
+            @pl.when(step > 0)
+            def _():
+                total[h] += dot(expand, block, ((1,), (1,)))
+                site_total[h] += dot(block, w_ref[...], ((1,), (0,)))
+
+        @pl.when(step == last)
+        def _():
+            row = lax.broadcasted_iota(jnp.int32, (lines, lines), 0)
+            col = lax.broadcasted_iota(jnp.int32, (lines, lines), 1)
+            order = jnp.where((row % s) * share + row // s == col, 1.0, 0.0).astype(bf16)
+            for h in range(halves):
+                to = slice(h * share, (h + 1) * share)
+                y = dot(total[h].astype(bf16), order, ((1,), (0,))).astype(bf16)
+                for i in range(k):
+                    for t in range(s):
+                        y_ref[i, t, :, to] = y[i * v : (i + 1) * v, t * share : (t + 1) * share]
+                high, low = split(site_total[h].T)
+                z = dot(jnp.concatenate([high, low], axis=0), order, ((1,), (0,)))
+                z = z[:columns] + z[columns:]
+                for t in range(s):
+                    z_ref[t, :, to] = z[:, t * share : (t + 1) * share]
+
+    return pl.pallas_call(
+        kernel,
+        grid=(last + 1,),
+        in_specs=[
+            pl.BlockSpec((rows, s, width), lambda i: (0, 0, i)),
+            pl.BlockSpec((k, v, width), lambda i: (0, 0, i)),
+            pl.BlockSpec((width, columns), lambda i: (i, 0)),
+        ],
+        out_specs=[
+            pl.BlockSpec((k, s, v, rows), lambda i: (0, 0, 0, 0)),
+            pl.BlockSpec((s, columns, rows), lambda i: (0, 0, 0)),
+        ],
+        out_shape=[
+            jax.ShapeDtypeStruct((k, s, v, rows), bf16),
+            jax.ShapeDtypeStruct((s, columns, rows), f32),
+        ],
+        scratch_shapes=[
+            pltpu.VMEM((halves, k * v, lines), f32),
+            pltpu.VMEM((halves, lines, columns), f32),
+        ],
+        compiler_params=pltpu.CompilerParams(vmem_limit_bytes=36 * MIB),
+        cost_estimate=cost(7_000_000_000, 15_000_000),
+        name="sketch",
+    )(in_hbm(site_tensor), in_hbm(sketch_expand), in_hbm(sketch_site))
 
 
 def expand_half(core, env, contracted):
@@ -40,36 +111,53 @@
     k = share
     s = x // k
     step = 4
-
-    def kernel(core_ref, e_ref, c_ref, o_ref):
-        left = jnp.concatenate(
-            [e_ref[w, :, 0].reshape(step * share, depth) for w in range(width)], axis=1
-        )
+    steps = blocks // step
+
+    def kernel(core_ref, e_ref, c_ref, o_ref, near, sem):
+        core = core_ref[0]
+        copies = [
+            pltpu.make_async_copy(
+                e_ref.at[:, pl.ds(i * step, step), core],
+                near.at[:, pl.ds(i * step, step)],
+                sem.at[i],
+            )
+            for i in range(steps)
+        ]
+        for copy in copies:
+            copy.start()
         right = jnp.concatenate([c_ref[w] for w in range(width)], axis=1)
-        total = dot(left, right, ((1,), (1,)))
-        for i in range(s):
-            o_ref[:, i] = total[:, i * k : (i + 1) * k].astype(bf16).reshape(step, share, k)
+        for i in range(steps):
+            copies[i].wait()
+            n = pl.ds(i * step, step)
+            left = jnp.concatenate(
+                [near[w, n].reshape(step * share, depth) for w in range(width)], axis=1
+            )
+            total = dot(left, right, ((1,), (1,)))
+            for t in range(s):
+                o_ref[n, t] = total[:, t * k : (t + 1) * k].astype(bf16).reshape(step, share, k)
 
     return pl.pallas_call(
         kernel,
-        grid_spec=pltpu.PrefetchScalarGridSpec(
-            num_scalar_prefetch=1,
-            grid=(blocks // step,),
-            in_specs=[
-                pl.BlockSpec((width, step, 1, share, depth), lambda i, core: (0, i, core[0], 0, 0)),
-                pl.BlockSpec((width, x, depth), lambda i, core: (0, 0, 0)),
-            ],
-            out_specs=pl.BlockSpec((step, s, share, k), lambda i, core: (i, 0, 0, 0)),
-        ),
+        in_specs=[
+            pl.BlockSpec(memory_space=pltpu.SMEM),
+            pl.BlockSpec(memory_space=pl.ANY),
+            pl.BlockSpec(memory_space=pltpu.VMEM),
+        ],
+        out_specs=pl.BlockSpec(memory_space=pltpu.VMEM),
         out_shape=jax.ShapeDtypeStruct((blocks, s, share, k), bf16),
-        compiler_params=pltpu.CompilerParams(vmem_limit_bytes=VMEM),
+        scratch_shapes=[
+            pltpu.VMEM((width, blocks, share, depth), bf16),
+            pltpu.SemaphoreType.DMA((steps,)),
+        ],
+        compiler_params=pltpu.CompilerParams(vmem_limit_bytes=24 * MIB),
         cost_estimate=cost(2 * width * blocks * share * depth * x, 9_000_000),
         name="expand_half",
-    )(core, env, contracted)
+    )(core, in_hbm(env), contracted)
 
 
 def site_terms(env, site):
-    width, blocks, rows, depth = env.shape
+    width, blocks, _, share, depth = env.shape
+    rows = 2 * share
     s, k = site.shape[1:3]
     step = 2
 
@@ -99,7 +187,7 @@
         kernel,
         grid=(blocks // step,),
         in_specs=[
-            pl.BlockSpec((width, step, rows, depth), lambda i: (0, i, 0, 0)),
+            pl.BlockSpec((width, step, 2, share, depth), lambda i: (0, i, 0, 0, 0)),
             pl.BlockSpec((step, s, k, rows), lambda i: (i, 0, 0, 0)),
         ],
         out_specs=[
@@ -110,15 +198,15 @@
             jax.ShapeDtypeStruct((width, s * k, depth), f32),
             jax.ShapeDtypeStruct((k, k), f32),
         ],
-        compiler_params=pltpu.CompilerParams(vmem_limit_bytes=VMEM),
+        compiler_params=pltpu.CompilerParams(vmem_limit_bytes=20 * MIB),
         cost_estimate=cost(6_000_000_000, 17_000_000),
         name="site_terms",
-    )(env, site)
+    )(in_hbm(env), in_hbm(site))
 
 
 def expand_step(e_ref, s_ref, h_ref):
-    width, step, _, share, depth = e_ref.shape
-    s, k = h_ref.shape[1:3]
+    width, _, _, share, depth = e_ref.shape
+    step, s, k = h_ref.shape[:3]
     left = jnp.concatenate([h_ref[z].reshape(s * k, share) for z in range(step)], axis=1)
     terms = [
         lambda w=w: dot(left, e_ref[w, :, 0].reshape(step * share, depth), ((1,), (0,)))
@@ -174,10 +262,10 @@
             jax.ShapeDtypeStruct((width, s * k, depth), f32),
             jax.ShapeDtypeStruct((k, 2 * k), f32),
         ],
-        compiler_params=pltpu.CompilerParams(vmem_limit_bytes=VMEM),
+        compiler_params=pltpu.CompilerParams(vmem_limit_bytes=20 * MIB),
         cost_estimate=cost(3_300_000_000, 12_000_000),
         name="expand_terms",
-    )(core, env, site, half)
+    )(core, in_hbm(env), in_hbm(site), half)
 
 
 def inverse_factor(a, nb):
@@ -364,10 +452,10 @@
             jax.ShapeDtypeStruct((k // 8, 8 * out_rows, k), f32),
             jax.ShapeDtypeStruct((k // 8, 8 * out_rows, k), f32),
         ],
-        compiler_params=pltpu.CompilerParams(vmem_limit_bytes=VMEM),
+        compiler_params=pltpu.CompilerParams(vmem_limit_bytes=36 * MIB),
         cost_estimate=cost(4_000_000_000, 20_000_000),
         name="finish",
-    )(scalars, env, site, half, x_site, g_site, x_own, g_own, own, half, site_local, operator)
+    )(scalars, in_hbm(env), in_hbm(site), half, x_site, g_site, x_own, g_own, own, half, site_local, operator)
 
 
 def summed_over_chips(half):
@@ -385,8 +473,7 @@
     columns = column_sectors.shape[1]
     blocks, share = chi // local_rows, local_rows // 2
     mask_rows = sector_mask(row_sectors, column_sectors)
-    env = jnp.transpose(environment, (1, 0, 2))
-    env_halves = env.reshape(width, blocks, 2, share, depth)
+    env = jnp.transpose(environment, (1, 0, 2)).reshape(width, blocks, 2, share, depth)
     own_core = core.reshape(1).astype(jnp.int32)
     other_core = 1 - own_core
 
@@ -396,25 +483,20 @@
     operator = jnp.pad(operator, ((0, 0), (0, 4), (0, 0), (0, 4)))
     operator = jnp.where(core == 0, operator[::-1], operator).reshape(2 * operator.shape[1], -1)
 
-    sketched = jnp.einsum(
-        "asb,kwb->wska", site_tensor, sketch_expand, preferred_element_type=f32
-    ).astype(bf16)
-    applied = jnp.einsum(
-        "vwst,wtka->vska", mpo_tensor, sketched, preferred_element_type=f32
-    ).astype(bf16)
-    applied, sketch_site = lax.optimization_barrier((applied, sketch_site))
-    site_y = jnp.einsum("asb,bk->ska", site_tensor, sketch_site, preferred_element_type=f32)
+    sketched, site_y = sketch(site_tensor, sketch_expand, sketch_site, 1024)
     site_local = site_y * jnp.transpose(mask_rows, (1, 2, 0))
     site_all = lax.all_gather(site_local.astype(bf16), BOND, axis=0)
+    applied = jnp.einsum(
+        "vwst,ktwa->vska", mpo_tensor, sketched, preferred_element_type=f32
+    ).astype(bf16)
     contracted = lax.all_to_all(applied, MPO, split_axis=0, concat_axis=2, tiled=True)
-    contracted, site_local = lax.optimization_barrier((contracted, site_local))
     contracted = contracted.reshape(width, physical * columns, depth)
 
-    send = expand_half(other_core, env_halves, contracted)
+    send = expand_half(other_core, env, contracted)
     got = lax.ppermute(send, CORE, SWAP)
-    keep = expand_half(own_core, env_halves, contracted)
+    keep = expand_half(own_core, env, contracted)
     half = (keep.astype(f32) + got.astype(f32)).astype(bf16)
-    x_site, g_site = site_terms(env.reshape(width, blocks, local_rows, depth), site_all)
+    x_site, g_site = site_terms(env, site_all)
     arrived = lax.all_to_all(half.reshape(-1, share, columns), CHIPS, 0, 0, tiled=True)
     arrived, x_site, g_site = lax.optimization_barrier((arrived, x_site, g_site))
     piece = arrived.astype(f32).sum(axis=0)
@@ -427,10 +509,10 @@
     ).reshape(blocks, physical, columns, share)
     other = lax.ppermute(own, CORE, SWAP)
 
-    x_own, g_own = expand_terms(own_core, env_halves, site_all, own)
+    x_own, g_own = expand_terms(own_core, env, site_all, own)
     scalars = jnp.concatenate([other_core, bond_index.reshape(1).astype(jnp.int32)])
     basis_flat, give, kept = finish(
-        scalars, env_halves, site_all, other, x_site, g_site, x_own, g_own, own, site_local, operator
+        scalars, env, site_all, other, x_site, g_site, x_own, g_own, own, site_local, operator
     )
     basis_local = basis_flat.reshape(local_rows, physical, columns)
 

time: 218 us -> 214 us (0.982)
  matrix products: 23.2 us -> 0.56 us
  Pallas kernels: 47 us -> 63 us
  local copies, waits for them, and re-layouts: 20.5 us -> 7.29 us
  waiting for transfers between devices: 51.6 us -> 62.6 us
  blocking collectives: 35.2 us -> 40 us
    all_gather x1, waiting for transfers between devices: 0.47 us -> 26.7 us  [body(): site_all = lax.all_gather(site_local.astype(bf16), BOND, axis=0)]
    dot_general x3 -> x1, matrix products: 23.2 us -> 0.56 us  [body(): jnp.einsum('vwst,ktwa->vska', mpo_tensor, sketched, preferred_element_typ...]
    pallas_call x2 -> x3, Pallas kernels: 7.8 us -> 23.3 us  [the longest x1 13.5 us: sketch(): pl.pallas_call(kernel, grid=(last + 1,), in_specs=[pl.BlockSpec((rows, s,...]
    all_to_all x1, waiting for transfers between devices: 15.2 us -> 0.01 us  [body(): lax.all_to_all(half.reshape(-1, share, columns), CHIPS, 0, 0, tiled=True)]
    unnamed x20 -> x6, local copies, waits for them, and re-layouts: 14 us -> 1.52 us
    all_to_all x1, blocking collectives: 35.2 us -> 40 us  [body(): lax.all_to_all(jnp.broadcast_to(piece[None], (blocks * physical, columns,...]
  transfers between devices with their start and end apart: 7 -> 7, of which waited for: 5 -> 4; matrix products, arithmetic and copies ran while one was open for 3% -> 3% of each run, Pallas kernels for 12% -> 13%
where the time goes in v2:
time: 214 us; the launch traced here: 213 us
  Pallas kernels  63 us (29%)
  waiting for transfers between devices  62.6 us (29%)
  blocking collectives  40 us (19%)
  starting transfers between devices  19.9 us (9%)
  between operations  14.3 us (7%)
  local copies, waits for them, and re-layouts  7.29 us (3%)
  other arithmetic  5.3 us (2%)
    all_to_all x1, blocking collectives, body(): lax.all_to_all(jnp.broadcast_to(piece[None], (blocks * physical, columns,...  40 us
    all_gather x1, waiting for transfers between devices, body(): site_all = lax.all_gather(site_local.astype(bf16), BOND, axis=0)  26.7 us
    pallas_call x1, Pallas kernels, finish(): pl.pallas_call(kernel, grid_spec=pltpu.PrefetchScalarGridSpec(num_scalar_...  20.9 us
    all_to_all x1, waiting for transfers between devices, body(): lax.all_to_all(applied, MPO, split_axis=0, concat_axis=2, tiled=True)  18.8 us
    all_to_all x1, waiting for transfers between devices, summed_over_chips(): return lax.all_to_all(half, CHIPS, 0, 0, tiled=True).astype(f32).sum(axis=0)  14.5 us
    pallas_call x1, Pallas kernels, sketch(): pl.pallas_call(kernel, grid=(last + 1,), in_specs=[pl.BlockSpec((rows, s,...  13.5 us
    pallas_call x1, Pallas kernels, site_terms(): pl.pallas_call(kernel, grid=(blocks // step,), in_specs=[pl.BlockSpec((wi...  11.7 us
    pallas_call x2, Pallas kernels, expand_half(): pl.pallas_call(kernel, in_specs=[pl.BlockSpec(memory_space=pltpu.SMEM), p...  9.75 us
  transfers between devices with their start and end apart: 7, of which 4 were waited for; matrix products, arithmetic and copies ran while one was open for 3% of the time, Pallas kernels for 13%

profile of v2, /device:TPU:0, one launch (start us, length us, event | category | flops | bytes accessed | tf_op | source)
XLA Modules:
  0.0 213.0 jit_solution(1614231484676983662)
XLA Ops:
  7.2 0.8 slice_bitcast_fusion.5
  8.0 0.7 slice_bitcast_fusion.3
  8.7 13.5 %sketch.1 = (bf16[16,4,40,256]{3,2,1,0:T(8,128)(2,1)S(1)}, f32[4,128,256]{2,1,0:T(8,128)S(1)}) custom-call(bf16[256,4,4096]{2,1,0:T(4,128)(2,1)} %s_ref.1, bf16[16,40,4096]{2,1,0:T(8,128)(2,1)} %o_ref.1, bf16[4096,128]{1,0:T(8,128)(2,1)} %w_ref.1), custom_call_target="tpu_custom_call" | custom-call | flops 7000000000 | bytes 15000000 | tf_op jit(solution)/shard_map/sketch/pallas_call | solution.py:82
  22.2 0.9 fusion.6
  23.1 0.6 fusion
  23.7 1.8 copy.17
  25.5 4.4 %all-to-all-start = ((bf16[40,4,16,256]{3,1,2,0:T(4,128)(2,1)}), bf16[40,4,16,256]{3,1,2,0:T(4,128)(2,1)S(1)}, u32[]{:S(2)}, u32[]{:S(2)}) async-start(bf16[40,4,16,256]{3,1,2,0:T(4,128)(2,1)} %copy.17), calls=%async_computation | async-start | bytes 2621440 | tf_op jit(solution)/shard_map/all_to_all | solution.py:492
  29.8 18.8 %all-to-all-done = bf16[40,4,16,256]{3,1,2,0:T(4,128)(2,1)S(1)} async-done(((bf16[40,4,16,256]{3,1,2,0:T(4,128)(2,1)}), bf16[40,4,16,256]{3,1,2,0:T(4,128)(2,1)S(1)}, u32[]{:S(2)}, u32[]{:S(2)}) %all-to-all-start) | async-done | bytes 1310752 | tf_op jit(solution)/shard_map/all_to_all | solution.py:492
  48.6 0.3 copy.18
  48.9 0.1 copy.19
  49.0 4.9 %expand_half.3 = bf16[16,4,128,128]{3,2,1,0:T(8,128)(2,1)S(1)} custom-call(s32[1]{0:T(128)S(6)} %sub.3.core_ref, bf16[5,16,2,128,256]{4,3,2,1,0:T(8,128)(2,1)} %bitcast.63, bf16[5,512,256]{2,1,0:T(8,128)(2,1)S(1)} %bitcast.61), custom_call_target="tpu_custom_call" | custom-call | flops 2684354560 | bytes 9000000 | tf_op jit(solution)/shard_map/expand_half/pallas_call | solution.py:139
  54.0 4.9 %expand_half.2 = bf16[16,4,128,128]{3,2,1,0:T(8,128)(2,1)S(1)} custom-call(s32[1]{0:T(128)} %bitcast.core_ref, bf16[5,16,2,128,256]{4,3,2,1,0:T(8,128)(2,1)} %bitcast.64, bf16[5,512,256]{2,1,0:T(8,128)(2,1)S(1)} %bitcast.62), custom_call_target="tpu_custom_call" | custom-call | flops 2684354560 | bytes 9000000 | tf_op jit(solution)/shard_map/expand_half/pallas_call | solution.py:139
  58.9 2.2 %add_convert_fusion = bf16[16,4,128,128]{3,2,1,0:T(8,128)(2,1)} fusion(bf16[16,4,128,128]{3,2,1,0:T(8,128)(2,1)S(1)} %collective-permute-done, bf16[16,4,128,128]{3,2,1,0:T(8,128)(2,1)S(1)} %expand_half.2), kind=kLoop, calls=%fused_computation.1 | loop fusion | flops 4194304 | bytes 6291456 | tf_op jit(solution)/shard_map/convert_element_type | solution.py:498
  61.1 9.5 %all-to-all-start.1 = ((bf16[64,128,128]{2,1,0:T(8,128)(2,1)}), bf16[64,128,128]{2,1,0:T(8,128)(2,1)S(1)}, u32[]{:S(2)}, u32[]{:S(2)}) async-start(bf16[64,128,128]{2,1,0:T(8,128)(2,1)} %bitcast.21), calls=%async_computation.1 | async-start | bytes 4194304 | tf_op jit(solution)/shard_map/all_to_all | solution.py:500
  70.8 26.7 %all-gather.3.cloned.1.call-done = bf16[64,128,256]{2,1,0:T(8,128)(2,1)} async-done(((bf16[4,128,256]{2,1,0:T(8,128)(2,1)}), bf16[64,128,256]{2,1,0:T(8,128)(2,1)}) %all-gather.3.cloned.1.call-update) | async-done | bytes 4194320 | tf_op jit(solution)/shard_map/all_gather | solution.py:488
  97.5 11.7 %site_terms.1 = (f32[5,512,256]{2,1,0:T(8,128)S(1)}, f32[128,128]{1,0:T(8,128)S(1)}) custom-call(bf16[5,16,2,128,256]{4,3,2,1,0:T(8,128)(2,1)} %bitcast.65, bf16[16,4,128,256]{3,2,1,0:T(8,128)(2,1)} %bitcast.68), custom_call_target="tpu_custom_call" | custom-call | flops 6000000000 | bytes 17000000 | tf_op jit(solution)/shard_map/site_terms/pallas_call | solution.py:186
  109.3 1.5 copy-done
  110.8 0.3 convert_reduce_fusion
  111.3 0.5 broadcast_in_dim.2
  111.8 40.0 %all_to_all.30 = bf16[64,128,128]{2,1,0:T(8,128)(2,1)S(1)} all-to-all(bf16[64,128,128]{2,1,0:T(8,128)(2,1)S(1)} %broadcast_in_dim.2), channel_id=1, replica_groups=mesh['mpo_0'=4,'mpo_1'=2,'bond_0'=4,'bond_1'=4] {'bond_0','bond_1','mpo_0'}, dimensions={0} | all-to-all | bytes 4194304 | tf_op jit(solution)/shard_map/all_to_all | solution.py:507
  151.8 0.1 reshape.52
  152.0 0.1 reshape.53
  152.3 0.1 copy.22
  152.6 7.1 %expand_terms.1 = (f32[5,512,256]{2,1,0:T(8,128)S(1)}, f32[128,256]{1,0:T(8,128)S(1)}) custom-call(s32[1]{0:T(128)} %bitcast.core_ref, bf16[5,16,2,128,256]{4,3,2,1,0:T(8,128)(2,1)} %bitcast.66, bf16[16,4,128,256]{3,2,1,0:T(8,128)(2,1)} %bitcast.69, bf16[16,4,128,128]{3,2,1,0:T(8,128)(2,1)S(1)} %bitcast.59), custom_call_target="tpu_custom_call" | custom-call | flops 3300000000 | bytes 12000000 | tf_op jit(solution)/shard_map/expand_terms/pallas_call | solution.py:250
  159.7 20.9 %finish.1 = (bf16[256,512]{1,0:T(8,128)(2,1)S(1)}, f32[16,160,128]{2,1,0:T(8,128)S(1)}, f32[16,160,128]{2,1,0:T(8,128)S(1)}) custom-call(s32[2]{0:T(128)S(1)} %pad_add_fusion.sc_ref, bf16[5,16,2,128,256]{4,3,2,1,0:T(8,128)(2,1)} %bitcast.67, bf16[16,4,128,256]{3,2,1,0:T(8,128)(2,1)} %bitcast.70, ...), custom_call_target="tpu_custom_call" | custom-call | flops 4000000000 | bytes 20000000 | tf_op jit(solution)/shard_map/finish/pallas_call | solution.py:423
  180.6 0.6 collective-permute-start.2
  181.2 2.7 %collective-permute-done.2 = f32[16,160,128]{2,1,0:T(8,128)S(1)} collective-permute-done((f32[16,160,128]{2,1,0:T(8,128)S(1)}, f32[16,160,128]{2,1,0:T(8,128)S(1)}, u32[]{:S(2)}, u32[]{:S(2)}) %collective-permute-start.2) | collective-permute-done | bytes 1310752 | tf_op jit(solution)/shard_map/ppermute | solution.py:519
  183.9 1.0 add_convert_fusion.1
  184.8 5.3 %all-to-all-start.3 = ((bf16[64,40,128]{2,1,0:T(8,128)(2,1)}), bf16[64,40,128]{2,1,0:T(8,128)(2,1)S(1)}, u32[]{:S(2)}, u32[]{:S(2)}) async-start(bf16[64,40,128]{2,1,0:T(8,128)(2,1)} %bitcast.26), calls=%async_computation.3 | async-start | bytes 1310720 | tf_op jit(solution)/shard_map/all_to_all | solution.py:462
  190.1 0.8 reshape.55
  190.9 14.5 %all-to-all-done.3 = bf16[64,40,128]{2,1,0:T(8,128)(2,1)S(1)} async-done(((bf16[64,40,128]{2,1,0:T(8,128)(2,1)}), bf16[64,40,128]{2,1,0:T(8,128)(2,1)S(1)}, u32[]{:S(2)}, u32[]{:S(2)}) %all-to-all-start.3) | async-done | bytes 655392 | tf_op jit(solution)/shard_map/all_to_all | solution.py:462
  205.4 0.7 convert_reduce_fusion.1
  (22 shorter events, 0.8 us)
Async XLA Ops:
  7.2 90.4 %all-gather.3.cloned.1.call-start = ((), (), s32[]{:S(2)}) async-start(), calls=%async_computation.4 | async-start | bytes 4456448 | tf_op jit(solution)/shard_map/all_gather | solution.py:488
  8.7 14.4 %copy-start.2 = (bf16[40,40,4,4]{1,3,2,0:T(4,128)(2,1)S(1)}, bf16[40,40,4,4]{1,3,2,0:T(4,128)(2,1)}, u32[]{:S(2)}) copy-start(bf16[40,40,4,4]{1,3,2,0:T(4,128)(2,1)} %param.9) | copy-start | bytes 153604
  25.5 23.2 %all-to-all-start = ((bf16[40,4,16,256]{3,1,2,0:T(4,128)(2,1)}), bf16[40,4,16,256]{3,1,2,0:T(4,128)(2,1)S(1)}, u32[]{:S(2)}, u32[]{:S(2)}) async-start(bf16[40,4,16,256]{3,1,2,0:T(4,128)(2,1)} %copy.17), calls=%async_computation | async-start | bytes 2621440 | tf_op jit(solution)/shard_map/all_to_all | solution.py:492
  53.9 5.0 %collective-permute-start = (bf16[16,4,128,128]{3,2,1,0:T(8,128)(2,1)S(1)}, bf16[16,4,128,128]{3,2,1,0:T(8,128)(2,1)S(1)}, u32[]{:S(2)}, u32[]{:S(2)}) collective-permute-start(bf16[16,4,128,128]{3,2,1,0:T(8,128)(2,1)S(1)} %expand_half.3), channel_id=1, source_target_pairs={{0,16},{16,0},{1,17},{17,1},{2,18},{18,2},{3,19},{19,3},{4,20},{20... | collective-permute-start | bytes 6291464 | tf_op jit(solution)/shard_map/ppermute | solution.py:496
  61.1 49.7 %all-to-all-start.1 = ((bf16[64,128,128]{2,1,0:T(8,128)(2,1)}), bf16[64,128,128]{2,1,0:T(8,128)(2,1)S(1)}, u32[]{:S(2)}, u32[]{:S(2)}) async-start(bf16[64,128,128]{2,1,0:T(8,128)(2,1)} %bitcast.21), calls=%async_computation.1 | async-start | bytes 4194304 | tf_op jit(solution)/shard_map/all_to_all | solution.py:500
  109.3 1.5 copy-start
  151.8 7.9 %collective-permute-start.1 = (bf16[16,4,128,128]{3,2,1,0:T(8,128)(2,1)S(1)}, bf16[16,4,128,128]{3,2,1,0:T(8,128)(2,1)}, u32[]{:S(2)}, u32[]{:S(2)}) collective-permute-start(bf16[16,4,128,128]{3,2,1,0:T(8,128)(2,1)S(1)} %bitcast.58), channel_id=1, source_target_pairs={{0,16},{16,0},{1,17},{17,1},{2,18},{18,2},{3,19},{19,3},{4,20},{20... | collective-permute-start | bytes 6291464 | tf_op jit(solution)/shard_map/ppermute | solution.py:510
  152.6 7.2 %copy-start.1 = (f32[5,512,256]{2,1,0:T(8,128)S(1)}, f32[5,512,256]{2,1,0:T(8,128)}, u32[]{:S(2)}) copy-start(f32[5,512,256]{2,1,0:T(8,128)} %copy-done) | copy-start | bytes 7864324
  180.6 3.3 %collective-permute-start.2 = (f32[16,160,128]{2,1,0:T(8,128)S(1)}, f32[16,160,128]{2,1,0:T(8,128)S(1)}, u32[]{:S(2)}, u32[]{:S(2)}) collective-permute-start(f32[16,160,128]{2,1,0:T(8,128)S(1)} %get-tuple-element.25), channel_id=1, source_target_pairs={{0,16},{16,0},{1,17},{17,1},{2,18},{18,2},{3,19},{19,3},{4,20},{20... | collective-permute-start | bytes 3932168 | tf_op jit(solution)/shard_map/ppermute | solution.py:519
  184.8 20.5 %all-to-all-start.3 = ((bf16[64,40,128]{2,1,0:T(8,128)(2,1)}), bf16[64,40,128]{2,1,0:T(8,128)(2,1)S(1)}, u32[]{:S(2)}, u32[]{:S(2)}) async-start(bf16[64,40,128]{2,1,0:T(8,128)(2,1)} %bitcast.26), calls=%async_computation.3 | async-start | bytes 1310720 | tf_op jit(solution)/shard_map/all_to_all | solution.py:462
Sparse Core Ops, SparseCore 0:
  23.2 74.2 all-gather.2

commit v3 on v2

--- a/solution.py
+++ b/solution.py
@@ -472,7 +472,6 @@
     local_rows, physical, _ = site_tensor.shape
     columns = column_sectors.shape[1]
     blocks, share = chi // local_rows, local_rows // 2
-    mask_rows = sector_mask(row_sectors, column_sectors)
     env = jnp.transpose(environment, (1, 0, 2)).reshape(width, blocks, 2, share, depth)
     own_core = core.reshape(1).astype(jnp.int32)
     other_core = 1 - own_core
@@ -484,6 +483,10 @@
     operator = jnp.where(core == 0, operator[::-1], operator).reshape(2 * operator.shape[1], -1)
 
     sketched, site_y = sketch(site_tensor, sketch_expand, sketch_site, 1024)
+    site_y, row_sectors, column_sectors = lax.optimization_barrier(
+        (site_y, row_sectors, column_sectors)
+    )
+    mask_rows = sector_mask(row_sectors, column_sectors)
     site_local = site_y * jnp.transpose(mask_rows, (1, 2, 0))
     site_all = lax.all_gather(site_local.astype(bf16), BOND, axis=0)
     applied = jnp.einsum(
@@ -498,7 +501,6 @@
     half = (keep.astype(f32) + got.astype(f32)).astype(bf16)
     x_site, g_site = site_terms(env, site_all)
     arrived = lax.all_to_all(half.reshape(-1, share, columns), CHIPS, 0, 0, tiled=True)
-    arrived, x_site, g_site = lax.optimization_barrier((arrived, x_site, g_site))
     piece = arrived.astype(f32).sum(axis=0)
     mask_piece = lax.dynamic_slice(
         mask_rows, (core * share, lax.axis_index("mpo_0"), 0), (share, 1, columns)
@@ -506,7 +508,9 @@
     piece = (piece * mask_piece).T.astype(bf16)
     own = lax.all_to_all(
         jnp.broadcast_to(piece[None], (blocks * physical, columns, share)), CHIPS, 0, 0, tiled=True
-    ).reshape(blocks, physical, columns, share)
+    )
+    own, x_site, g_site = lax.optimization_barrier((own, x_site, g_site))
+    own = own.reshape(blocks, physical, columns, share)
     other = lax.ppermute(own, CORE, SWAP)
 
     x_own, g_own = expand_terms(own_core, env, site_all, own)

time: 214 us -> 204 us (0.953)
  blocking collectives: 40 us -> 0 us
  waiting for transfers between devices: 62.6 us -> 84 us
  starting transfers between devices: 19.9 us -> 28.6 us
    all_to_all x1 -> x0, blocking collectives: 40 us -> none  [body(): lax.all_to_all(jnp.broadcast_to(piece[None], (blocks * physical, columns,...]
    all_to_all x1, waiting for transfers between devices: 0.01 us -> 32.1 us  [body(): lax.all_to_all(half.reshape(-1, share, columns), CHIPS, 0, 0, tiled=True)]
    all_gather x1, waiting for transfers between devices: 26.7 us -> 0.02 us  [body(): site_all = lax.all_gather(site_local.astype(bf16), BOND, axis=0)]
    all_to_all x0 -> x1, waiting for transfers between devices: none -> 16.9 us  [body(): lax.all_to_all(jnp.broadcast_to(piece[None], (blocks * physical, columns,...]
    all_to_all x0 -> x1, starting transfers between devices: none -> 8.71 us  [body(): lax.all_to_all(jnp.broadcast_to(piece[None], (blocks * physical, columns,...]
  transfers between devices with their start and end apart: 7 -> 8, of which waited for: 4 -> 5; matrix products, arithmetic and copies ran while one was open for 3% -> 4% of each run, Pallas kernels for 13% -> 14%
where the time goes in v3:
time: 204 us; the launch traced here: 203 us
  waiting for transfers between devices  84 us (41%)
  Pallas kernels  63 us (31%)
  starting transfers between devices  28.6 us (14%)
  between operations  14.3 us (7%)
  local copies, waits for them, and re-layouts  7.27 us (4%)
  other arithmetic  5.26 us (3%)
    all_to_all x1, waiting for transfers between devices, body(): lax.all_to_all(half.reshape(-1, share, columns), CHIPS, 0, 0, tiled=True)  32.1 us
    pallas_call x1, Pallas kernels, finish(): pl.pallas_call(kernel, grid_spec=pltpu.PrefetchScalarGridSpec(num_scalar_...  20.8 us
    all_to_all x1, waiting for transfers between devices, body(): lax.all_to_all(applied, MPO, split_axis=0, concat_axis=2, tiled=True)  17.8 us
    all_to_all x1, waiting for transfers between devices, body(): lax.all_to_all(jnp.broadcast_to(piece[None], (blocks * physical, columns,...  16.9 us
    all_to_all x1, waiting for transfers between devices, summed_over_chips(): return lax.all_to_all(half, CHIPS, 0, 0, tiled=True).astype(f32).sum(axis=0)  14.5 us
    pallas_call x1, Pallas kernels, sketch(): pl.pallas_call(kernel, grid=(last + 1,), in_specs=[pl.BlockSpec((rows, s,...  13.5 us
    pallas_call x1, Pallas kernels, site_terms(): pl.pallas_call(kernel, grid=(blocks // step,), in_specs=[pl.BlockSpec((wi...  11.7 us
    pallas_call x2, Pallas kernels, expand_half(): pl.pallas_call(kernel, in_specs=[pl.BlockSpec(memory_space=pltpu.SMEM), p...  9.74 us
  transfers between devices with their start and end apart: 8, of which 5 were waited for; matrix products, arithmetic and copies ran while one was open for 4% of the time, Pallas kernels for 14%

profile of v3, /device:TPU:0, one launch (start us, length us, event | category | flops | bytes accessed | tf_op | source)
XLA Modules:
  0.0 203.1 jit_solution(12293373454205910880)
XLA Ops:
  7.2 13.5 %sketch.1 = (bf16[16,4,40,256]{3,2,1,0:T(8,128)(2,1)S(1)}, f32[4,128,256]{2,1,0:T(8,128)S(1)}) custom-call(bf16[256,4,4096]{2,1,0:T(4,128)(2,1)} %s_ref.1, bf16[16,40,4096]{2,1,0:T(8,128)(2,1)} %o_ref.1, bf16[4096,128]{1,0:T(8,128)(2,1)} %w_ref.1), custom_call_target="tpu_custom_call" | custom-call | flops 7000000000 | bytes 15000000 | tf_op jit(solution)/shard_map/sketch/pallas_call | solution.py:82
  20.7 0.6 fusion
  21.3 1.8 copy.17
  23.1 4.4 %all-to-all-start = ((bf16[40,4,16,256]{3,1,2,0:T(4,128)(2,1)}), bf16[40,4,16,256]{3,1,2,0:T(4,128)(2,1)S(1)}, u32[]{:S(2)}, u32[]{:S(2)}) async-start(bf16[40,4,16,256]{3,1,2,0:T(4,128)(2,1)} %copy.17), calls=%async_computation | async-start | bytes 2621440 | tf_op jit(solution)/shard_map/all_to_all | solution.py:495
  27.6 0.9 fusion.6
  28.5 17.8 %all-to-all-done = bf16[40,4,16,256]{3,1,2,0:T(4,128)(2,1)S(1)} async-done(((bf16[40,4,16,256]{3,1,2,0:T(4,128)(2,1)}), bf16[40,4,16,256]{3,1,2,0:T(4,128)(2,1)S(1)}, u32[]{:S(2)}, u32[]{:S(2)}) %all-to-all-start) | async-done | bytes 1310752 | tf_op jit(solution)/shard_map/all_to_all | solution.py:495
  46.3 0.3 copy.18
  46.6 0.1 copy.19
  46.7 4.9 %expand_half.3 = bf16[16,4,128,128]{3,2,1,0:T(8,128)(2,1)S(1)} custom-call(s32[1]{0:T(128)S(6)} %sub.3.core_ref, bf16[5,16,2,128,256]{4,3,2,1,0:T(8,128)(2,1)} %bitcast.63, bf16[5,512,256]{2,1,0:T(8,128)(2,1)S(1)} %bitcast.61), custom_call_target="tpu_custom_call" | custom-call | flops 2684354560 | bytes 9000000 | tf_op jit(solution)/shard_map/expand_half/pallas_call | solution.py:139
  51.7 4.9 %expand_half.2 = bf16[16,4,128,128]{3,2,1,0:T(8,128)(2,1)S(1)} custom-call(s32[1]{0:T(128)} %bitcast.core_ref, bf16[5,16,2,128,256]{4,3,2,1,0:T(8,128)(2,1)} %bitcast.64, bf16[5,512,256]{2,1,0:T(8,128)(2,1)S(1)} %bitcast.62), custom_call_target="tpu_custom_call" | custom-call | flops 2684354560 | bytes 9000000 | tf_op jit(solution)/shard_map/expand_half/pallas_call | solution.py:139
  56.5 2.2 %add_convert_fusion = bf16[16,4,128,128]{3,2,1,0:T(8,128)(2,1)} fusion(bf16[16,4,128,128]{3,2,1,0:T(8,128)(2,1)S(1)} %collective-permute-done, bf16[16,4,128,128]{3,2,1,0:T(8,128)(2,1)S(1)} %expand_half.2), kind=kLoop, calls=%fused_computation.1 | loop fusion | flops 4194304 | bytes 6291456 | tf_op jit(solution)/shard_map/convert_element_type | solution.py:501
  58.7 9.6 %all-to-all-start.1 = ((bf16[64,128,128]{2,1,0:T(8,128)(2,1)}), bf16[64,128,128]{2,1,0:T(8,128)(2,1)S(1)}, u32[]{:S(2)}, u32[]{:S(2)}) async-start(bf16[64,128,128]{2,1,0:T(8,128)(2,1)} %bitcast.21), calls=%async_computation.1 | async-start | bytes 4194304 | tf_op jit(solution)/shard_map/all_to_all | solution.py:503
  68.5 32.1 %all-to-all-done.1 = bf16[64,128,128]{2,1,0:T(8,128)(2,1)S(1)} async-done(((bf16[64,128,128]{2,1,0:T(8,128)(2,1)}), bf16[64,128,128]{2,1,0:T(8,128)(2,1)S(1)}, u32[]{:S(2)}, u32[]{:S(2)}) %all-to-all-start.1) | async-done | bytes 2097184 | tf_op jit(solution)/shard_map/all_to_all | solution.py:503
  100.6 0.3 convert_reduce_fusion
  101.0 0.1 copy.20
  101.1 1.9 broadcast_in_dim.2
  103.0 8.7 %all-to-all-start.2 = ((bf16[64,128,128]{2,1,0:T(8,128)(2,1)}), bf16[64,128,128]{2,1,0:T(8,128)(2,1)S(1)}, u32[]{:S(2)}, u32[]{:S(2)}) async-start(bf16[64,128,128]{2,1,0:T(8,128)(2,1)} %broadcast_in_dim.2), calls=%async_computation.2 | async-start | bytes 4194304 | tf_op jit(solution)/shard_map/all_to_all | solution.py:509
  111.8 11.7 %site_terms.1 = (f32[5,512,256]{2,1,0:T(8,128)S(1)}, f32[128,128]{1,0:T(8,128)S(1)}) custom-call(bf16[5,16,2,128,256]{4,3,2,1,0:T(8,128)(2,1)} %bitcast.65, bf16[16,4,128,256]{3,2,1,0:T(8,128)(2,1)} %bitcast.68), custom_call_target="tpu_custom_call" | custom-call | flops 6000000000 | bytes 17000000 | tf_op jit(solution)/shard_map/site_terms/pallas_call | solution.py:186
  123.5 1.5 copy-done
  125.0 16.9 %all-to-all-done.2 = bf16[64,128,128]{2,1,0:T(8,128)(2,1)S(1)} async-done(((bf16[64,128,128]{2,1,0:T(8,128)(2,1)}), bf16[64,128,128]{2,1,0:T(8,128)(2,1)S(1)}, u32[]{:S(2)}, u32[]{:S(2)}) %all-to-all-start.2) | async-done | bytes 2097184 | tf_op jit(solution)/shard_map/all_to_all | solution.py:509
  142.0 0.1 reshape.52
  142.2 0.1 reshape.53
  142.4 0.1 copy.22
  142.7 7.1 %expand_terms.1 = (f32[5,512,256]{2,1,0:T(8,128)S(1)}, f32[128,256]{1,0:T(8,128)S(1)}) custom-call(s32[1]{0:T(128)} %bitcast.core_ref, bf16[5,16,2,128,256]{4,3,2,1,0:T(8,128)(2,1)} %bitcast.66, bf16[16,4,128,256]{3,2,1,0:T(8,128)(2,1)} %bitcast.69, bf16[16,4,128,128]{3,2,1,0:T(8,128)(2,1)S(1)} %bitcast.59), custom_call_target="tpu_custom_call" | custom-call | flops 3300000000 | bytes 12000000 | tf_op jit(solution)/shard_map/expand_terms/pallas_call | solution.py:250
  149.9 20.8 %finish.1 = (bf16[256,512]{1,0:T(8,128)(2,1)S(1)}, f32[16,160,128]{2,1,0:T(8,128)S(1)}, f32[16,160,128]{2,1,0:T(8,128)S(1)}) custom-call(s32[2]{0:T(128)S(1)} %pad_add_fusion.sc_ref, bf16[5,16,2,128,256]{4,3,2,1,0:T(8,128)(2,1)} %bitcast.67, bf16[16,4,128,256]{3,2,1,0:T(8,128)(2,1)} %bitcast.70, ...), custom_call_target="tpu_custom_call" | custom-call | flops 4000000000 | bytes 20000000 | tf_op jit(solution)/shard_map/finish/pallas_call | solution.py:423
  170.7 0.6 collective-permute-start.2
  171.3 2.7 %collective-permute-done.2 = f32[16,160,128]{2,1,0:T(8,128)S(1)} collective-permute-done((f32[16,160,128]{2,1,0:T(8,128)S(1)}, f32[16,160,128]{2,1,0:T(8,128)S(1)}, u32[]{:S(2)}, u32[]{:S(2)}) %collective-permute-start.2) | collective-permute-done | bytes 1310752 | tf_op jit(solution)/shard_map/ppermute | solution.py:523
  174.0 1.0 add_convert_fusion.1
  174.9 5.3 %all-to-all-start.3 = ((bf16[64,40,128]{2,1,0:T(8,128)(2,1)}), bf16[64,40,128]{2,1,0:T(8,128)(2,1)S(1)}, u32[]{:S(2)}, u32[]{:S(2)}) async-start(bf16[64,40,128]{2,1,0:T(8,128)(2,1)} %bitcast.26), calls=%async_computation.3 | async-start | bytes 1310720 | tf_op jit(solution)/shard_map/all_to_all | solution.py:462
  180.2 0.8 reshape.55
  181.0 14.5 %all-to-all-done.3 = bf16[64,40,128]{2,1,0:T(8,128)(2,1)S(1)} async-done(((bf16[64,40,128]{2,1,0:T(8,128)(2,1)}), bf16[64,40,128]{2,1,0:T(8,128)(2,1)S(1)}, u32[]{:S(2)}, u32[]{:S(2)}) %all-to-all-start.3) | async-done | bytes 655392 | tf_op jit(solution)/shard_map/all_to_all | solution.py:462
  195.5 0.7 convert_reduce_fusion.1
  (27 shorter events, 0.7 us)
Async XLA Ops:
  7.2 13.6 %copy-start.3 = (bf16[40,40,4,4]{1,3,2,0:T(4,128)(2,1)S(1)}, bf16[40,40,4,4]{1,3,2,0:T(4,128)(2,1)}, u32[]{:S(2)}) copy-start(bf16[40,40,4,4]{1,3,2,0:T(4,128)(2,1)} %param.9) | copy-start | bytes 153604
  21.3 6.3 %copy-start.4 = (s32[2,128]{1,0:T(2,128)S(1)}, s32[2,128]{1,0:T(2,128)}, u32[]{:S(2)}) copy-start(s32[2,128]{1,0:T(2,128)} %param.13) | copy-start | bytes 3076
  21.3 6.3 %copy-start.2 = (s32[2,256,4]{1,2,0:T(4,128)S(1)}, s32[2,256,4]{1,2,0:T(4,128)}, u32[]{:S(2)}) copy-start(s32[2,256,4]{1,2,0:T(4,128)} %param.12) | copy-start | bytes 24580
  23.1 23.1 %all-to-all-start = ((bf16[40,4,16,256]{3,1,2,0:T(4,128)(2,1)}), bf16[40,4,16,256]{3,1,2,0:T(4,128)(2,1)S(1)}, u32[]{:S(2)}, u32[]{:S(2)}) async-start(bf16[40,4,16,256]{3,1,2,0:T(4,128)(2,1)} %copy.17), calls=%async_computation | async-start | bytes 2621440 | tf_op jit(solution)/shard_map/all_to_all | solution.py:495
  27.5 84.3 %all-gather.3.cloned.1.call-start = ((), (), s32[]{:S(2)}) async-start(), calls=%async_computation.4 | async-start | bytes 4456448 | tf_op jit(solution)/shard_map/all_gather | solution.py:491
  51.6 5.0 %collective-permute-start = (bf16[16,4,128,128]{3,2,1,0:T(8,128)(2,1)S(1)}, bf16[16,4,128,128]{3,2,1,0:T(8,128)(2,1)S(1)}, u32[]{:S(2)}, u32[]{:S(2)}) collective-permute-start(bf16[16,4,128,128]{3,2,1,0:T(8,128)(2,1)S(1)} %expand_half.3), channel_id=1, source_target_pairs={{0,16},{16,0},{1,17},{17,1},{2,18},{18,2},{3,19},{19,3},{4,20},{20... | collective-permute-start | bytes 6291464 | tf_op jit(solution)/shard_map/ppermute | solution.py:499
  58.7 41.9 %all-to-all-start.1 = ((bf16[64,128,128]{2,1,0:T(8,128)(2,1)}), bf16[64,128,128]{2,1,0:T(8,128)(2,1)S(1)}, u32[]{:S(2)}, u32[]{:S(2)}) async-start(bf16[64,128,128]{2,1,0:T(8,128)(2,1)} %bitcast.21), calls=%async_computation.1 | async-start | bytes 4194304 | tf_op jit(solution)/shard_map/all_to_all | solution.py:503
  103.0 39.0 %all-to-all-start.2 = ((bf16[64,128,128]{2,1,0:T(8,128)(2,1)}), bf16[64,128,128]{2,1,0:T(8,128)(2,1)S(1)}, u32[]{:S(2)}, u32[]{:S(2)}) async-start(bf16[64,128,128]{2,1,0:T(8,128)(2,1)} %broadcast_in_dim.2), calls=%async_computation.2 | async-start | bytes 4194304 | tf_op jit(solution)/shard_map/all_to_all | solution.py:509
  123.5 1.5 copy-start
  142.0 7.9 %collective-permute-start.1 = (bf16[16,4,128,128]{3,2,1,0:T(8,128)(2,1)S(1)}, bf16[16,4,128,128]{3,2,1,0:T(8,128)(2,1)}, u32[]{:S(2)}, u32[]{:S(2)}) collective-permute-start(bf16[16,4,128,128]{3,2,1,0:T(8,128)(2,1)S(1)} %bitcast.58), channel_id=1, source_target_pairs={{0,16},{16,0},{1,17},{17,1},{2,18},{18,2},{3,19},{19,3},{4,20},{20... | collective-permute-start | bytes 6291464 | tf_op jit(solution)/shard_map/ppermute | solution.py:514
  142.7 7.2 %copy-start.1 = (f32[5,512,256]{2,1,0:T(8,128)S(1)}, f32[5,512,256]{2,1,0:T(8,128)}, u32[]{:S(2)}) copy-start(f32[5,512,256]{2,1,0:T(8,128)} %copy-done) | copy-start | bytes 7864324
  170.7 3.3 %collective-permute-start.2 = (f32[16,160,128]{2,1,0:T(8,128)S(1)}, f32[16,160,128]{2,1,0:T(8,128)S(1)}, u32[]{:S(2)}, u32[]{:S(2)}) collective-permute-start(f32[16,160,128]{2,1,0:T(8,128)S(1)} %get-tuple-element.31), channel_id=1, source_target_pairs={{0,16},{16,0},{1,17},{17,1},{2,18},{18,2},{3,19},{19,3},{4,20},{20... | collective-permute-start | bytes 3932168 | tf_op jit(solution)/shard_map/ppermute | solution.py:523
  174.9 20.5 %all-to-all-start.3 = ((bf16[64,40,128]{2,1,0:T(8,128)(2,1)}), bf16[64,40,128]{2,1,0:T(8,128)(2,1)S(1)}, u32[]{:S(2)}, u32[]{:S(2)}) async-start(bf16[64,40,128]{2,1,0:T(8,128)(2,1)} %bitcast.26), calls=%async_computation.3 | async-start | bytes 1310720 | tf_op jit(solution)/shard_map/all_to_all | solution.py:462
Sparse Core Ops, SparseCore 0:
  31.1 77.0 all-gather.2

commit v4 on v3

--- a/solution.py
+++ b/solution.py
@@ -149,7 +149,7 @@
             pltpu.VMEM((width, blocks, share, depth), bf16),
             pltpu.SemaphoreType.DMA((steps,)),
         ],
-        compiler_params=pltpu.CompilerParams(vmem_limit_bytes=24 * MIB),
+        compiler_params=pltpu.CompilerParams(vmem_limit_bytes=16 * MIB),
         cost_estimate=cost(2 * width * blocks * share * depth * x, 9_000_000),
         name="expand_half",
     )(core, in_hbm(env), contracted)
@@ -204,65 +204,74 @@
     )(in_hbm(env), in_hbm(site))
 
 
-def expand_step(e_ref, s_ref, h_ref):
-    width, _, _, share, depth = e_ref.shape
-    step, s, k = h_ref.shape[:3]
-    left = jnp.concatenate([h_ref[z].reshape(s * k, share) for z in range(step)], axis=1)
-    terms = [
-        lambda w=w: dot(left, e_ref[w, :, 0].reshape(step * share, depth), ((1,), (0,)))
-        for w in range(width)
+def near_scratch(width, blocks, s, k, share, depth, steps):
+    return [
+        pltpu.VMEM((width, blocks, share, depth), bf16),
+        pltpu.VMEM((blocks, s, k, share), bf16),
+        pltpu.VMEM((blocks, s, k, share), bf16),
+        pltpu.SemaphoreType.DMA((3, steps)),
     ]
-    wide = jnp.concatenate([left[i * k : (i + 1) * k] for i in range(s)], axis=1)
-    site = jnp.concatenate([s_ref[z, i] for i in range(s) for z in range(step)], axis=1)
-    gram = dot(wide, jnp.concatenate([wide, site], axis=0), ((1,), (1,)))
-    return terms, gram
-
-
-def expand_specs(width, step, share, depth, s, k):
-    return [
-        pl.BlockSpec((width, step, 1, share, depth), lambda i, sc: (0, i, sc[0], 0, 0)),
-        pl.BlockSpec((step, s, k, share), lambda i, sc: (i, 0, 0, sc[0])),
-        pl.BlockSpec((step, s, k, share), lambda i, sc: (i, 0, 0, 0)),
-    ]
+
+
+def add_expand(core, e_ref, s_ref, h_ref, near, steps, x_ref, g_ref, x_first, g_first):
+    e_near, s_near, h_near, sem = near
+    width, blocks, share, depth = e_near.shape
+    s, k = h_near.shape[1:3]
+    step = blocks // steps
+    lanes = pl.ds(pl.multiple_of(core * share, share), share)
+    copies = []
+    for i in range(steps):
+        n = pl.ds(i * step, step)
+        copies.append(
+            (
+                pltpu.make_async_copy(h_ref.at[n], h_near.at[n], sem.at[0, i]),
+                pltpu.make_async_copy(e_ref.at[:, n, core], e_near.at[:, n], sem.at[1, i]),
+                pltpu.make_async_copy(s_ref.at[n, :, :, lanes], s_near.at[n], sem.at[2, i]),
+            )
+        )
+    for some in copies:
+        for copy in some:
+            copy.start()
+    for i in range(steps):
+        for copy in copies[i]:
+            copy.wait()
+        n = pl.ds(i * step, step)
+        half = h_near[n]
+        site = s_near[n]
+        left = jnp.concatenate([half[z].reshape(s * k, share) for z in range(step)], axis=1)
+        for w in range(width):
+            term = dot(left, e_near[w, n].reshape(step * share, depth), ((1,), (0,)))
+            if i > 0:
+                x_ref[w] += term
+            else:
+                x_ref[w] = term if x_first is None else x_first[w] + term
+        wide = jnp.concatenate([left[t * k : (t + 1) * k] for t in range(s)], axis=1)
+        other = jnp.concatenate([site[z, t] for t in range(s) for z in range(step)], axis=1)
+        gram = dot(wide, jnp.concatenate([wide, other], axis=0), ((1,), (1,)))
+        if i > 0:
+            g_ref[...] += gram
+        else:
+            g_ref[...] = gram if g_first is None else g_first[...] + gram
 
 
 def expand_terms(core, env, site, half):
     width, blocks, _, share, depth = env.shape
     s, k = half.shape[1:3]
-    step = 4
-
-    def kernel(core_ref, e_ref, s_ref, h_ref, x_ref, g_ref):
-        first = pl.program_id(0) == 0
-        terms, gram = expand_step(e_ref, s_ref, h_ref)
-
-        @pl.when(first)
-        def _():
-            for w in range(width):
-                x_ref[w] = terms[w]()
-            g_ref[...] = gram
-
-        @pl.when(jnp.logical_not(first))
-        def _():
-            for w in range(width):
-                x_ref[w] += terms[w]()
-            g_ref[...] += gram
+    steps = 4
+
+    def kernel(core_ref, e_ref, s_ref, h_ref, x_ref, g_ref, *near):
+        add_expand(core_ref[0], e_ref, s_ref, h_ref, near, steps, x_ref, g_ref, None, None)
 
     return pl.pallas_call(
         kernel,
-        grid_spec=pltpu.PrefetchScalarGridSpec(
-            num_scalar_prefetch=1,
-            grid=(blocks // step,),
-            in_specs=expand_specs(width, step, share, depth, s, k),
-            out_specs=[
-                pl.BlockSpec((width, s * k, depth), lambda i, sc: (0, 0, 0)),
-                pl.BlockSpec((k, 2 * k), lambda i, sc: (0, 0)),
-            ],
-        ),
+        in_specs=[pl.BlockSpec(memory_space=pltpu.SMEM)] + [pl.BlockSpec(memory_space=pl.ANY)] * 3,
+        out_specs=[pl.BlockSpec(memory_space=pltpu.VMEM)] * 2,
         out_shape=[
             jax.ShapeDtypeStruct((width, s * k, depth), f32),
             jax.ShapeDtypeStruct((k, 2 * k), f32),
         ],
-        compiler_params=pltpu.CompilerParams(vmem_limit_bytes=20 * MIB),
+        scratch_shapes=near_scratch(width, blocks, s, k, share, depth, steps),
+        compiler_params=pltpu.CompilerParams(vmem_limit_bytes=18 * MIB),
         cost_estimate=cost(3_300_000_000, 12_000_000),
         name="expand_terms",
     )(core, in_hbm(env), in_hbm(site), half)
@@ -322,140 +331,120 @@
 def finish(scalars, env, site, half, x_site, g_site, x_own, g_own, own, site_local, operator):
     width, blocks, _, share, depth = env.shape
     s, k = half.shape[1:3]
-    step = 4
-    last = blocks // step - 1
+    steps = 4
     pad = operator.shape[0] // 2
     out_rows = pad - 4
 
     def kernel(
-        sc_ref, e_ref, s_ref, h_ref, xs_ref, gs_ref, xo_ref, go_ref, own_ref, oth_ref, sl_ref, m_ref,
-        b_ref, give_ref, keep_ref, x_ref, g_ref, p_ref,
+        sc_ref, e_ref, s_ref, h_ref, own_ref, xs_ref, gs_ref, xo_ref, go_ref, sl_ref, m_ref,
+        b_ref, give_ref, keep_ref, x_ref, g_ref, p_ref, own_near, own_sem, *near,
     ):
-        first = pl.program_id(0) == 0
-        terms, gram = expand_step(e_ref, s_ref, h_ref)
-
-        @pl.when(first)
-        def _():
-            for w in range(width):
-                x_ref[w] = xo_ref[w] + terms[w]()
-            g_ref[...] = go_ref[...] + gram
-
-        @pl.when(jnp.logical_not(first))
-        def _():
-            for w in range(width):
-                x_ref[w] += terms[w]()
-            g_ref[...] += gram
-
-        @pl.when(pl.program_id(0) == last)
-        def _():
-            gs = gs_ref[...]
-            ge = g_ref[:, :k]
-            gc = g_ref[:, k:]
-            row = lax.broadcasted_iota(jnp.int32, (k, k), 0)
-            col = lax.broadcasted_iota(jnp.int32, (k, k), 1)
-            trace_site = jnp.sum(jnp.where(row == col, gs, 0.0), keepdims=True)
-            trace_expand = jnp.sum(jnp.where(row == col, ge, 0.0), keepdims=True)
-            mix = mixing * jnp.sqrt((trace_site + shift_tolerance) / (trace_expand + shift_tolerance))
-            inverse = inverse_factor(gs + mix * (gc + gc.T) + (mix * mix) * ge, 8)
-            high, low = split(inverse)
-            both = jnp.concatenate([high, low], axis=1)
-
-            def apply(v):
-                vh, vl = split(v)
-                return dot(both, jnp.concatenate([vh, vh], axis=0), ((1,), (0,))) + dot(
-                    high, vl, ((1,), (0,))
+        block = sc_ref[1]
+        own_copy = pltpu.make_async_copy(own_ref.at[block], own_near, own_sem)
+        own_copy.start()
+        add_expand(sc_ref[0], e_ref, s_ref, h_ref, near, steps, x_ref, g_ref, xo_ref, go_ref)
+        own_copy.wait()
+        h_near = near[2]
+        gs = gs_ref[...]
+        ge = g_ref[:, :k]
+        gc = g_ref[:, k:]
+        row = lax.broadcasted_iota(jnp.int32, (k, k), 0)
+        col = lax.broadcasted_iota(jnp.int32, (k, k), 1)
+        trace_site = jnp.sum(jnp.where(row == col, gs, 0.0), keepdims=True)
+        trace_expand = jnp.sum(jnp.where(row == col, ge, 0.0), keepdims=True)
+        mix = mixing * jnp.sqrt((trace_site + shift_tolerance) / (trace_expand + shift_tolerance))
+        inverse = inverse_factor(gs + mix * (gc + gc.T) + (mix * mix) * ge, 8)
+        high, low = split(inverse)
+        both = jnp.concatenate([high, low], axis=1)
+
+        def apply(v):
+            vh, vl = split(v)
+            return dot(both, jnp.concatenate([vh, vh], axis=0), ((1,), (0,))) + dot(
+                high, vl, ((1,), (0,))
+            )
+
+        for w in range(width):
+            for i in range(s):
+                part = slice(i * k, (i + 1) * k)
+                value = apply(xs_ref[w, part] + mix * x_ref[w, part])
+                p_ref[:, pl.ds(w * s + i, k, stride=pad), :] = jnp.stack(
+                    [value[:, h * k : (h + 1) * k] for h in range(depth // k)], axis=0
                 )
-
-            for w in range(width):
-                for i in range(s):
-                    part = slice(i * k, (i + 1) * k)
-                    value = apply(xs_ref[w, part] + mix * x_ref[w, part])
-                    p_ref[:, pl.ds(w * s + i, k, stride=pad), :] = jnp.stack(
-                        [value[:, h * k : (h + 1) * k] for h in range(depth // k)], axis=0
-                    )
-            for i in range(width * s, pad):
-                p_ref[:, pl.ds(i, k, stride=pad), :] = jnp.zeros((depth // k, k, k), f32)
-            even = sc_ref[0] == 1
-            for i in range(s):
-                a0 = own_ref[0, i].astype(f32)
-                a1 = oth_ref[0, i].astype(f32)
-                rows = jnp.concatenate(
-                    [jnp.where(even, a0, a1), jnp.where(even, a1, a0)], axis=1
+        for i in range(width * s, pad):
+            p_ref[:, pl.ds(i, k, stride=pad), :] = jnp.zeros((depth // k, k, k), f32)
+        even = sc_ref[0] == 1
+        for i in range(s):
+            a0 = own_near[i].astype(f32)
+            a1 = h_near[block, i].astype(f32)
+            rows = jnp.concatenate(
+                [jnp.where(even, a0, a1), jnp.where(even, a1, a0)], axis=1
+            )
+            done = apply(sl_ref[i] + mix * rows)
+            b_ref[:, i * k : (i + 1) * k] = done.T.astype(bf16)
+
+        operator_rows = jnp.concatenate([m_ref[...], m_ref[...]], axis=1)
+
+        def group(g):
+            lines = pl.ds(pl.multiple_of(g * (8 * pad), 8 * pad), 8 * pad)
+            left = jnp.concatenate(
+                [p_ref[h, lines, :] for h in range(depth // k)], axis=1
+            ).astype(bf16)
+            paired = dot(left, b_ref[...], ((1,), (0,)))
+            for q in range(0, 8, 2):
+                block = jnp.concatenate(
+                    [
+                        jnp.concatenate(
+                            [
+                                paired[r * pad : (r + 1) * pad, t * k : (t + 1) * k]
+                                for t in range(s)
+                            ],
+                            axis=0,
+                        )
+                        for r in (q, q + 1)
+                    ],
+                    axis=1,
                 )
-                done = apply(sl_ref[i] + mix * rows)
-                b_ref[:, i * k : (i + 1) * k] = done.T.astype(bf16)
-
-            operator_rows = jnp.concatenate([m_ref[...], m_ref[...]], axis=1)
-
-            def group(g, carry):
-                lines = pl.ds(pl.multiple_of(g * (8 * pad), 8 * pad), 8 * pad)
-                left = jnp.concatenate(
-                    [p_ref[h, lines, :] for h in range(depth // k)], axis=1
-                ).astype(bf16)
-                paired = dot(left, b_ref[...], ((1,), (0,)))
-                for q in range(0, 8, 2):
-                    block = jnp.concatenate(
-                        [
-                            jnp.concatenate(
-                                [
-                                    paired[r * pad : (r + 1) * pad, t * k : (t + 1) * k]
-                                    for t in range(s)
-                                ],
-                                axis=0,
-                            )
-                            for r in (q, q + 1)
-                        ],
-                        axis=1,
-                    )
-                    bh, bl = split(block)
-                    done = dot(operator_rows, jnp.concatenate([bh, bl], axis=0), ((1,), (0,)))
-                    for r in (0, 1):
-                        piece = done[:, r * k : (r + 1) * k]
-                        to = pl.ds(q + r, out_rows, stride=8)
-                        give_ref[g, to, :] = piece[:out_rows]
-                        keep_ref[g, to, :] = piece[pad : pad + out_rows]
-                return carry
-
-            lax.fori_loop(0, k // 8, group, 0)
-
-    fixed3 = lambda i, sc: (0, 0, 0)
-    fixed2 = lambda i, sc: (0, 0)
+                bh, bl = split(block)
+                done = dot(operator_rows, jnp.concatenate([bh, bl], axis=0), ((1,), (0,)))
+                for r in (0, 1):
+                    piece = done[:, r * k : (r + 1) * k]
+                    to = pl.ds(q + r, out_rows, stride=8)
+                    give_ref[g, to, :] = piece[:out_rows]
+                    keep_ref[g, to, :] = piece[pad : pad + out_rows]
+
+        def groups(i, carry):
+            for j in range(4):
+                group(i * 4 + j)
+            return carry
+
+        lax.fori_loop(0, k // 32, groups, 0)
+
     return pl.pallas_call(
         kernel,
-        grid_spec=pltpu.PrefetchScalarGridSpec(
-            num_scalar_prefetch=1,
-            grid=(blocks // step,),
-            in_specs=expand_specs(width, step, share, depth, s, k)
-            + [
-                pl.BlockSpec((width, s * k, depth), fixed3),
-                pl.BlockSpec((k, k), fixed2),
-                pl.BlockSpec((width, s * k, depth), fixed3),
-                pl.BlockSpec((k, 2 * k), fixed2),
-                pl.BlockSpec((1, s, k, share), lambda i, sc: (sc[1], 0, 0, 0)),
-                pl.BlockSpec((1, s, k, share), lambda i, sc: (sc[1], 0, 0, 0)),
-                pl.BlockSpec((s, k, 2 * share), fixed3),
-                pl.BlockSpec(operator.shape, fixed2),
-            ],
-            out_specs=[
-                pl.BlockSpec((2 * share, s * k), fixed2),
-                pl.BlockSpec((k // 8, 8 * out_rows, k), fixed3),
-                pl.BlockSpec((k // 8, 8 * out_rows, k), fixed3),
-            ],
-            scratch_shapes=[
-                pltpu.VMEM((width, s * k, depth), f32),
-                pltpu.VMEM((k, 2 * k), f32),
-                pltpu.VMEM((depth // k, k * pad, k), f32),
-            ],
-        ),
+        in_specs=[pl.BlockSpec(memory_space=pltpu.SMEM)]
+        + [pl.BlockSpec(memory_space=pl.ANY)] * 4
+        + [pl.BlockSpec(memory_space=pltpu.VMEM)] * 6,
+        out_specs=[pl.BlockSpec(memory_space=pltpu.VMEM)] * 3,
         out_shape=[
             jax.ShapeDtypeStruct((2 * share, s * k), bf16),
             jax.ShapeDtypeStruct((k // 8, 8 * out_rows, k), f32),
             jax.ShapeDtypeStruct((k // 8, 8 * out_rows, k), f32),
         ],
-        compiler_params=pltpu.CompilerParams(vmem_limit_bytes=36 * MIB),
+        scratch_shapes=[
+            pltpu.VMEM((width, s * k, depth), f32),
+            pltpu.VMEM((k, 2 * k), f32),
+            pltpu.VMEM((depth // k, k * pad, k), f32),
+            pltpu.VMEM((s, k, share), bf16),
+            pltpu.SemaphoreType.DMA,
+        ]
+        + near_scratch(width, blocks, s, k, share, depth, steps),
+        compiler_params=pltpu.CompilerParams(vmem_limit_bytes=26 * MIB),
         cost_estimate=cost(4_000_000_000, 20_000_000),
         name="finish",
-    )(scalars, in_hbm(env), in_hbm(site), half, x_site, g_site, x_own, g_own, own, half, site_local, operator)
+    )(
+        scalars, in_hbm(env), in_hbm(site), half, own, x_site, g_site, x_own, g_own, site_local,
+        operator,
+    )
 
 
 def summed_over_chips(half):

time: 204 us -> 201 us (0.985)
  Pallas kernels: 63 us -> 60.3 us
    pallas_call x2, Pallas kernels: 28 us -> 25.2 us  [the longest x1 18.4 us: finish(): pl.pallas_call(kernel, in_specs=[pl.BlockSpec(memory_space=pltpu.SMEM)] +...]
where the time goes in v4:
time: 201 us
  waiting for transfers between devices  84 us (42%)
  Pallas kernels  60.3 us (30%)
  starting transfers between devices  29.1 us (14%)
  between operations  14.3 us (7%)
  local copies, waits for them, and re-layouts  7.3 us (4%)
  other arithmetic  5.22 us (3%)
    all_to_all x1, waiting for transfers between devices, body(): lax.all_to_all(half.reshape(-1, share, columns), CHIPS, 0, 0, tiled=True)  32.1 us
    pallas_call x1, Pallas kernels, finish(): pl.pallas_call(kernel, in_specs=[pl.BlockSpec(memory_space=pltpu.SMEM)] +...  18.4 us
    all_to_all x1, waiting for transfers between devices, body(): lax.all_to_all(applied, MPO, split_axis=0, concat_axis=2, tiled=True)  17.8 us
    all_to_all x1, waiting for transfers between devices, body(): lax.all_to_all(jnp.broadcast_to(piece[None], (blocks * physical, columns,...  16.9 us
    all_to_all x1, waiting for transfers between devices, summed_over_chips(): return lax.all_to_all(half, CHIPS, 0, 0, tiled=True).astype(f32).sum(axis=0)  14.5 us
    pallas_call x1, Pallas kernels, sketch(): pl.pallas_call(kernel, grid=(last + 1,), in_specs=[pl.BlockSpec((rows, s,...  13.5 us
    pallas_call x1, Pallas kernels, site_terms(): pl.pallas_call(kernel, grid=(blocks // step,), in_specs=[pl.BlockSpec((wi...  11.7 us
    pallas_call x2, Pallas kernels, expand_half(): pl.pallas_call(kernel, in_specs=[pl.BlockSpec(memory_space=pltpu.SMEM), p...  9.75 us
  transfers between devices with their start and end apart: 8, of which 5 were waited for; matrix products, arithmetic and copies ran while one was open for 4% of the time, Pallas kernels for 14%

profile of v4, /device:TPU:0, one launch (start us, length us, event | category | flops | bytes accessed | tf_op | source)
XLA Modules:
  0.0 200.8 jit_solution(14616125526505189234)
XLA Ops:
  7.2 13.5 %sketch.1 = (bf16[16,4,40,256]{3,2,1,0:T(8,128)(2,1)S(1)}, f32[4,128,256]{2,1,0:T(8,128)S(1)}) custom-call(bf16[256,4,4096]{2,1,0:T(4,128)(2,1)} %s_ref.1, bf16[16,40,4096]{2,1,0:T(8,128)(2,1)} %o_ref.1, bf16[4096,128]{1,0:T(8,128)(2,1)} %w_ref.1), custom_call_target="tpu_custom_call" | custom-call | flops 7000000000 | bytes 15000000 | tf_op jit(solution)/shard_map/sketch/pallas_call | solution.py:82
  20.7 0.6 fusion
  21.3 1.8 copy.17
  23.1 4.4 %all-to-all-start = ((bf16[40,4,16,256]{3,1,2,0:T(4,128)(2,1)}), bf16[40,4,16,256]{3,1,2,0:T(4,128)(2,1)S(1)}, u32[]{:S(2)}, u32[]{:S(2)}) async-start(bf16[40,4,16,256]{3,1,2,0:T(4,128)(2,1)} %copy.17), calls=%async_computation | async-start | bytes 2621440 | tf_op jit(solution)/shard_map/all_to_all | solution.py:484
  27.6 0.9 fusion.6
  28.5 17.8 %all-to-all-done = bf16[40,4,16,256]{3,1,2,0:T(4,128)(2,1)S(1)} async-done(((bf16[40,4,16,256]{3,1,2,0:T(4,128)(2,1)}), bf16[40,4,16,256]{3,1,2,0:T(4,128)(2,1)S(1)}, u32[]{:S(2)}, u32[]{:S(2)}) %all-to-all-start) | async-done | bytes 1310752 | tf_op jit(solution)/shard_map/all_to_all | solution.py:484
  46.3 0.3 copy.18
  46.6 0.2 copy.19
  46.7 4.9 %expand_half.3 = bf16[16,4,128,128]{3,2,1,0:T(8,128)(2,1)S(1)} custom-call(s32[1]{0:T(128)S(6)} %sub.3.core_ref, bf16[5,16,2,128,256]{4,3,2,1,0:T(8,128)(2,1)} %bitcast.63, bf16[5,512,256]{2,1,0:T(8,128)(2,1)S(1)} %bitcast.61), custom_call_target="tpu_custom_call" | custom-call | flops 2684354560 | bytes 9000000 | tf_op jit(solution)/shard_map/expand_half/pallas_call | solution.py:139
  51.7 4.9 %expand_half.2 = bf16[16,4,128,128]{3,2,1,0:T(8,128)(2,1)S(1)} custom-call(s32[1]{0:T(128)} %bitcast.core_ref, bf16[5,16,2,128,256]{4,3,2,1,0:T(8,128)(2,1)} %bitcast.64, bf16[5,512,256]{2,1,0:T(8,128)(2,1)S(1)} %bitcast.62), custom_call_target="tpu_custom_call" | custom-call | flops 2684354560 | bytes 9000000 | tf_op jit(solution)/shard_map/expand_half/pallas_call | solution.py:139
  56.6 2.1 %add_convert_fusion = bf16[16,4,128,128]{3,2,1,0:T(8,128)(2,1)} fusion(bf16[16,4,128,128]{3,2,1,0:T(8,128)(2,1)S(1)} %collective-permute-done, bf16[16,4,128,128]{3,2,1,0:T(8,128)(2,1)S(1)} %expand_half.2), kind=kLoop, calls=%fused_computation.1 | loop fusion | flops 4194304 | bytes 6291456 | tf_op jit(solution)/shard_map/convert_element_type | solution.py:490
  58.7 9.6 %all-to-all-start.1 = ((bf16[64,128,128]{2,1,0:T(8,128)(2,1)}), bf16[64,128,128]{2,1,0:T(8,128)(2,1)S(1)}, u32[]{:S(2)}, u32[]{:S(2)}) async-start(bf16[64,128,128]{2,1,0:T(8,128)(2,1)} %bitcast.21), calls=%async_computation.1 | async-start | bytes 4194304 | tf_op jit(solution)/shard_map/all_to_all | solution.py:492
  68.4 32.1 %all-to-all-done.1 = bf16[64,128,128]{2,1,0:T(8,128)(2,1)S(1)} async-done(((bf16[64,128,128]{2,1,0:T(8,128)(2,1)}), bf16[64,128,128]{2,1,0:T(8,128)(2,1)S(1)}, u32[]{:S(2)}, u32[]{:S(2)}) %all-to-all-start.1) | async-done | bytes 2097184 | tf_op jit(solution)/shard_map/all_to_all | solution.py:492
  100.5 0.3 convert_reduce_fusion
  100.9 0.1 copy.20
  101.1 1.9 broadcast_in_dim.2
  103.0 8.7 %all-to-all-start.2 = ((bf16[64,128,128]{2,1,0:T(8,128)(2,1)}), bf16[64,128,128]{2,1,0:T(8,128)(2,1)S(1)}, u32[]{:S(2)}, u32[]{:S(2)}) async-start(bf16[64,128,128]{2,1,0:T(8,128)(2,1)} %broadcast_in_dim.2), calls=%async_computation.2 | async-start | bytes 4194304 | tf_op jit(solution)/shard_map/all_to_all | solution.py:498
  111.7 11.7 %site_terms.1 = (f32[5,512,256]{2,1,0:T(8,128)S(1)}, f32[128,128]{1,0:T(8,128)S(1)}) custom-call(bf16[5,16,2,128,256]{4,3,2,1,0:T(8,128)(2,1)} %bitcast.65, bf16[16,4,128,256]{3,2,1,0:T(8,128)(2,1)} %bitcast.68), custom_call_target="tpu_custom_call" | custom-call | flops 6000000000 | bytes 17000000 | tf_op jit(solution)/shard_map/site_terms/pallas_call | solution.py:186
  123.5 1.5 copy-done
  125.0 16.9 %all-to-all-done.2 = bf16[64,128,128]{2,1,0:T(8,128)(2,1)S(1)} async-done(((bf16[64,128,128]{2,1,0:T(8,128)(2,1)}), bf16[64,128,128]{2,1,0:T(8,128)(2,1)S(1)}, u32[]{:S(2)}, u32[]{:S(2)}) %all-to-all-start.2) | async-done | bytes 2097184 | tf_op jit(solution)/shard_map/all_to_all | solution.py:498
  141.9 0.1 reshape.52
  142.2 0.1 reshape.53
  142.4 0.1 copy.22
  142.7 6.8 %expand_terms.1 = (f32[5,512,256]{2,1,0:T(8,128)S(1)}, f32[128,256]{1,0:T(8,128)S(1)}) custom-call(s32[1]{0:T(128)} %bitcast.core_ref, bf16[5,16,2,128,256]{4,3,2,1,0:T(8,128)(2,1)} %bitcast.66, bf16[16,4,128,256]{3,2,1,0:T(8,128)(2,1)} %bitcast.69, bf16[16,4,128,128]{3,2,1,0:T(8,128)(2,1)S(1)} %bitcast.59), custom_call_target="tpu_custom_call" | custom-call | flops 3300000000 | bytes 12000000 | tf_op jit(solution)/shard_map/expand_terms/pallas_call | solution.py:265
  149.5 18.4 %finish.1 = (bf16[256,512]{1,0:T(8,128)(2,1)S(1)}, f32[16,160,128]{2,1,0:T(8,128)S(1)}, f32[16,160,128]{2,1,0:T(8,128)S(1)}) custom-call(s32[2]{0:T(128)S(1)} %pad_add_fusion.sc_ref, bf16[5,16,2,128,256]{4,3,2,1,0:T(8,128)(2,1)} %bitcast.67, bf16[16,4,128,256]{3,2,1,0:T(8,128)(2,1)} %bitcast.70, bf16[16,4,128,128]{3,2,1,0:T(8,128)(2,1)} %collective-permute-done.1.h_ref, ...), custom_call_target="tpu_custom_call" | custom-call | flops 4000000000 | bytes 20000000 | tf_op jit(solution)/shard_map/finish/pallas_call | solution.py:422
  167.9 0.6 collective-permute-start.2
  168.5 2.7 %collective-permute-done.2 = f32[16,160,128]{2,1,0:T(8,128)S(1)} collective-permute-done((f32[16,160,128]{2,1,0:T(8,128)S(1)}, f32[16,160,128]{2,1,0:T(8,128)S(1)}, u32[]{:S(2)}, u32[]{:S(2)}) %collective-permute-start.2) | collective-permute-done | bytes 1310752 | tf_op jit(solution)/shard_map/ppermute | solution.py:512
  171.2 1.0 add_convert_fusion.1
  172.2 5.8 %all-to-all-start.3 = ((bf16[64,40,128]{2,1,0:T(8,128)(2,1)}), bf16[64,40,128]{2,1,0:T(8,128)(2,1)S(1)}, u32[]{:S(2)}, u32[]{:S(2)}) async-start(bf16[64,40,128]{2,1,0:T(8,128)(2,1)} %bitcast.26), calls=%async_computation.3 | async-start | bytes 1310720 | tf_op jit(solution)/shard_map/all_to_all | solution.py:451
  178.0 0.8 reshape.55
  178.8 14.5 %all-to-all-done.3 = bf16[64,40,128]{2,1,0:T(8,128)(2,1)S(1)} async-done(((bf16[64,40,128]{2,1,0:T(8,128)(2,1)}), bf16[64,40,128]{2,1,0:T(8,128)(2,1)S(1)}, u32[]{:S(2)}, u32[]{:S(2)}) %all-to-all-start.3) | async-done | bytes 655392 | tf_op jit(solution)/shard_map/all_to_all | solution.py:451
  193.3 0.7 convert_reduce_fusion.1
  (27 shorter events, 0.7 us)
Async XLA Ops:
  7.2 13.6 %copy-start.3 = (bf16[40,40,4,4]{1,3,2,0:T(4,128)(2,1)S(1)}, bf16[40,40,4,4]{1,3,2,0:T(4,128)(2,1)}, u32[]{:S(2)}) copy-start(bf16[40,40,4,4]{1,3,2,0:T(4,128)(2,1)} %param.9) | copy-start | bytes 153604
  21.3 6.3 %copy-start.4 = (s32[2,128]{1,0:T(2,128)S(1)}, s32[2,128]{1,0:T(2,128)}, u32[]{:S(2)}) copy-start(s32[2,128]{1,0:T(2,128)} %param.13) | copy-start | bytes 3076
  21.3 6.3 %copy-start.2 = (s32[2,256,4]{1,2,0:T(4,128)S(1)}, s32[2,256,4]{1,2,0:T(4,128)}, u32[]{:S(2)}) copy-start(s32[2,256,4]{1,2,0:T(4,128)} %param.12) | copy-start | bytes 24580
  23.1 23.1 %all-to-all-start = ((bf16[40,4,16,256]{3,1,2,0:T(4,128)(2,1)}), bf16[40,4,16,256]{3,1,2,0:T(4,128)(2,1)S(1)}, u32[]{:S(2)}, u32[]{:S(2)}) async-start(bf16[40,4,16,256]{3,1,2,0:T(4,128)(2,1)} %copy.17), calls=%async_computation | async-start | bytes 2621440 | tf_op jit(solution)/shard_map/all_to_all | solution.py:484
  27.5 84.2 %all-gather.3.cloned.1.call-start = ((), (), s32[]{:S(2)}) async-start(), calls=%async_computation.4 | async-start | bytes 4456448 | tf_op jit(solution)/shard_map/all_gather | solution.py:480
  51.6 5.0 %collective-permute-start = (bf16[16,4,128,128]{3,2,1,0:T(8,128)(2,1)S(1)}, bf16[16,4,128,128]{3,2,1,0:T(8,128)(2,1)S(1)}, u32[]{:S(2)}, u32[]{:S(2)}) collective-permute-start(bf16[16,4,128,128]{3,2,1,0:T(8,128)(2,1)S(1)} %expand_half.3), channel_id=1, source_target_pairs={{0,16},{16,0},{1,17},{17,1},{2,18},{18,2},{3,19},{19,3},{4,20},{20... | collective-permute-start | bytes 6291464 | tf_op jit(solution)/shard_map/ppermute | solution.py:488
  58.7 41.8 %all-to-all-start.1 = ((bf16[64,128,128]{2,1,0:T(8,128)(2,1)}), bf16[64,128,128]{2,1,0:T(8,128)(2,1)S(1)}, u32[]{:S(2)}, u32[]{:S(2)}) async-start(bf16[64,128,128]{2,1,0:T(8,128)(2,1)} %bitcast.21), calls=%async_computation.1 | async-start | bytes 4194304 | tf_op jit(solution)/shard_map/all_to_all | solution.py:492
  103.0 39.0 %all-to-all-start.2 = ((bf16[64,128,128]{2,1,0:T(8,128)(2,1)}), bf16[64,128,128]{2,1,0:T(8,128)(2,1)S(1)}, u32[]{:S(2)}, u32[]{:S(2)}) async-start(bf16[64,128,128]{2,1,0:T(8,128)(2,1)} %broadcast_in_dim.2), calls=%async_computation.2 | async-start | bytes 4194304 | tf_op jit(solution)/shard_map/all_to_all | solution.py:498
  123.5 1.5 copy-start
  141.9 7.5 %collective-permute-start.1 = (bf16[16,4,128,128]{3,2,1,0:T(8,128)(2,1)S(1)}, bf16[16,4,128,128]{3,2,1,0:T(8,128)(2,1)}, u32[]{:S(2)}, u32[]{:S(2)}) collective-permute-start(bf16[16,4,128,128]{3,2,1,0:T(8,128)(2,1)S(1)} %bitcast.58), channel_id=1, source_target_pairs={{0,16},{16,0},{1,17},{17,1},{2,18},{18,2},{3,19},{19,3},{4,20},{20... | collective-permute-start | bytes 6291464 | tf_op jit(solution)/shard_map/ppermute | solution.py:503
  142.7 6.8 %copy-start.1 = (f32[5,512,256]{2,1,0:T(8,128)S(1)}, f32[5,512,256]{2,1,0:T(8,128)}, u32[]{:S(2)}) copy-start(f32[5,512,256]{2,1,0:T(8,128)} %copy-done) | copy-start | bytes 7864324
  167.9 3.2 %collective-permute-start.2 = (f32[16,160,128]{2,1,0:T(8,128)S(1)}, f32[16,160,128]{2,1,0:T(8,128)S(1)}, u32[]{:S(2)}, u32[]{:S(2)}) collective-permute-start(f32[16,160,128]{2,1,0:T(8,128)S(1)} %get-tuple-element.31), channel_id=1, source_target_pairs={{0,16},{16,0},{1,17},{17,1},{2,18},{18,2},{3,19},{19,3},{4,20},{20... | collective-permute-start | bytes 3932168 | tf_op jit(solution)/shard_map/ppermute | solution.py:512
  172.2 21.1 %all-to-all-start.3 = ((bf16[64,40,128]{2,1,0:T(8,128)(2,1)}), bf16[64,40,128]{2,1,0:T(8,128)(2,1)S(1)}, u32[]{:S(2)}, u32[]{:S(2)}) async-start(bf16[64,40,128]{2,1,0:T(8,128)(2,1)} %bitcast.26), calls=%async_computation.3 | async-start | bytes 1310720 | tf_op jit(solution)/shard_map/all_to_all | solution.py:451
Sparse Core Ops, SparseCore 0:
  31.1 77.0 all-gather.2

commit v5 on v4

--- a/solution.py
+++ b/solution.py
@@ -1,3 +1,5 @@
+import functools
+
 import jax
 import jax.numpy as jnp
 from jax import lax
@@ -213,7 +215,7 @@
     ]
 
 
-def add_expand(core, e_ref, s_ref, h_ref, near, steps, x_ref, g_ref, x_first, g_first):
+def add_expand(core, e_ref, s_ref, h_ref, near, steps, x_ref, g_ref):
     e_near, s_near, h_near, sem = near
     width, blocks, share, depth = e_near.shape
     s, k = h_near.shape[1:3]
@@ -244,14 +246,14 @@
             if i > 0:
                 x_ref[w] += term
             else:
-                x_ref[w] = term if x_first is None else x_first[w] + term
+                x_ref[w] = term
         wide = jnp.concatenate([left[t * k : (t + 1) * k] for t in range(s)], axis=1)
         other = jnp.concatenate([site[z, t] for t in range(s) for z in range(step)], axis=1)
         gram = dot(wide, jnp.concatenate([wide, other], axis=0), ((1,), (1,)))
         if i > 0:
             g_ref[...] += gram
         else:
-            g_ref[...] = gram if g_first is None else g_first[...] + gram
+            g_ref[...] = gram
 
 
 def expand_terms(core, env, site, half):
@@ -260,7 +262,7 @@
     steps = 4
 
     def kernel(core_ref, e_ref, s_ref, h_ref, x_ref, g_ref, *near):
-        add_expand(core_ref[0], e_ref, s_ref, h_ref, near, steps, x_ref, g_ref, None, None)
+        add_expand(core_ref[0], e_ref, s_ref, h_ref, near, steps, x_ref, g_ref)
 
     return pl.pallas_call(
         kernel,
@@ -277,7 +279,7 @@
     )(core, in_hbm(env), in_hbm(site), half)
 
 
-def inverse_factor(a, nb):
+def inverse_factor(a, nb, beside):
     n = a.shape[0]
     count = n // 8
     rows = [a[8 * i : 8 * i + 8, :] for i in range(count)]
@@ -315,6 +317,8 @@
                 for q in range(p + 1, nb):
                     c[q] = c[q] - c[p] * ratio[q, p]
             rows[i] = value
+        for work in beside[j // nb :: n // nb]:
+            work()
     w = jnp.concatenate(rows, axis=0)
     row = lax.broadcasted_iota(jnp.int32, (n, n), 0)
     col = lax.broadcasted_iota(jnp.int32, (n, n), 1)
@@ -331,20 +335,41 @@
 def finish(scalars, env, site, half, x_site, g_site, x_own, g_own, own, site_local, operator):
     width, blocks, _, share, depth = env.shape
     s, k = half.shape[1:3]
-    steps = 4
     pad = operator.shape[0] // 2
     out_rows = pad - 4
 
     def kernel(
         sc_ref, e_ref, s_ref, h_ref, own_ref, xs_ref, gs_ref, xo_ref, go_ref, sl_ref, m_ref,
-        b_ref, give_ref, keep_ref, x_ref, g_ref, p_ref, own_near, own_sem, *near,
+        b_ref, give_ref, keep_ref, x_ref, g_ref, p_ref, stage_ref, own_near, own_sem, *near,
     ):
         block = sc_ref[1]
         own_copy = pltpu.make_async_copy(own_ref.at[block], own_near, own_sem)
         own_copy.start()
-        add_expand(sc_ref[0], e_ref, s_ref, h_ref, near, steps, x_ref, g_ref, xo_ref, go_ref)
+        e_near, s_near, h_near, sem = near
+        lanes = pl.ds(pl.multiple_of(sc_ref[0] * share, share), share)
+        h_copy = pltpu.make_async_copy(h_ref, h_near, sem.at[0, 0])
+        s_copy = pltpu.make_async_copy(s_ref.at[:, :, :, lanes], s_near, sem.at[1, 0])
+        e_copy = pltpu.make_async_copy(e_ref.at[:, :, sc_ref[0]], e_near, sem.at[2, 0])
+        for copy in (h_copy, s_copy, e_copy):
+            copy.start()
+        h_copy.wait()
+        s_copy.wait()
+        gram = go_ref[...]
+        for t in range(s):
+            left = jnp.concatenate([h_near[z, t] for z in range(blocks)], axis=1)
+            right = jnp.concatenate([s_near[z, t] for z in range(blocks)], axis=1)
+            gram += dot(left, jnp.concatenate([left, right], axis=0), ((1,), (1,)))
+        g_ref[...] = gram
         own_copy.wait()
-        h_near = near[2]
+        e_copy.wait()
+
+        def project(w, t):
+            left = jnp.concatenate([h_near[z, t] for z in range(blocks)], axis=1)
+            part = slice(t * k, (t + 1) * k)
+            term = dot(left, e_near[w].reshape(blocks * share, depth), ((1,), (0,)))
+            x_ref[w, part] = xo_ref[w, part] + term
+
+        beside = [functools.partial(project, w, t) for w in range(width) for t in range(s)]
         gs = gs_ref[...]
         ge = g_ref[:, :k]
         gc = g_ref[:, k:]
@@ -353,7 +378,7 @@
         trace_site = jnp.sum(jnp.where(row == col, gs, 0.0), keepdims=True)
         trace_expand = jnp.sum(jnp.where(row == col, ge, 0.0), keepdims=True)
         mix = mixing * jnp.sqrt((trace_site + shift_tolerance) / (trace_expand + shift_tolerance))
-        inverse = inverse_factor(gs + mix * (gc + gc.T) + (mix * mix) * ge, 8)
+        inverse = inverse_factor(gs + mix * (gc + gc.T) + (mix * mix) * ge, 8, beside)
         high, low = split(inverse)
         both = jnp.concatenate([high, low], axis=1)
 
@@ -384,7 +409,7 @@
 
         operator_rows = jnp.concatenate([m_ref[...], m_ref[...]], axis=1)
 
-        def group(g):
+        def group(g, stage):
             lines = pl.ds(pl.multiple_of(g * (8 * pad), 8 * pad), 8 * pad)
             left = jnp.concatenate(
                 [p_ref[h, lines, :] for h in range(depth // k)], axis=1
@@ -409,12 +434,13 @@
                 for r in (0, 1):
                     piece = done[:, r * k : (r + 1) * k]
                     to = pl.ds(q + r, out_rows, stride=8)
-                    give_ref[g, to, :] = piece[:out_rows]
+                    stage[to, :] = piece[:out_rows]
                     keep_ref[g, to, :] = piece[pad : pad + out_rows]
+            give_ref[g] = stage[...].astype(bf16)
 
         def groups(i, carry):
             for j in range(4):
-                group(i * 4 + j)
+                group(i * 4 + j, stage_ref.at[j])
             return carry
 
         lax.fori_loop(0, k // 32, groups, 0)
@@ -427,17 +453,18 @@
         out_specs=[pl.BlockSpec(memory_space=pltpu.VMEM)] * 3,
         out_shape=[
             jax.ShapeDtypeStruct((2 * share, s * k), bf16),
-            jax.ShapeDtypeStruct((k // 8, 8 * out_rows, k), f32),
+            jax.ShapeDtypeStruct((k // 8, 8 * out_rows, k), bf16),
             jax.ShapeDtypeStruct((k // 8, 8 * out_rows, k), f32),
         ],
         scratch_shapes=[
             pltpu.VMEM((width, s * k, depth), f32),
             pltpu.VMEM((k, 2 * k), f32),
             pltpu.VMEM((depth // k, k * pad, k), f32),
+            pltpu.VMEM((4, 8 * out_rows, k), f32),
             pltpu.VMEM((s, k, share), bf16),
             pltpu.SemaphoreType.DMA,
         ]
-        + near_scratch(width, blocks, s, k, share, depth, steps),
+        + near_scratch(width, blocks, s, k, share, depth, 1),
         compiler_params=pltpu.CompilerParams(vmem_limit_bytes=26 * MIB),
         cost_estimate=cost(4_000_000_000, 20_000_000),
         name="finish",
@@ -509,7 +536,7 @@
     )
     basis_local = basis_flat.reshape(local_rows, physical, columns)
 
-    both = (kept + lax.ppermute(give, CORE, SWAP)).astype(bf16)
+    both = (kept + lax.ppermute(give, CORE, SWAP).astype(f32)).astype(bf16)
     chips = blocks * physical
     extended = summed_over_chips(both.reshape(chips, -1, columns))
     extended = jnp.swapaxes(extended.reshape(-1, 8, columns), 0, 1)

time: 201 us -> 198 us (0.985)
  Pallas kernels: 60.3 us -> 58.2 us
    pallas_call x1, Pallas kernels: 18.4 us -> 16.3 us  [finish(): pl.pallas_call(kernel, in_specs=[pl.BlockSpec(memory_space=pltpu.SMEM)] +...]
where the time goes in v5:
time: 198 us
  waiting for transfers between devices  83.1 us (42%)
  Pallas kernels  58.2 us (29%)
  starting transfers between devices  29.1 us (15%)
  between operations  14.3 us (7%)
  local copies, waits for them, and re-layouts  7.3 us (4%)
  other arithmetic  5.22 us (3%)
    all_to_all x1, waiting for transfers between devices, body(): lax.all_to_all(half.reshape(-1, share, columns), CHIPS, 0, 0, tiled=True)  32.1 us
    all_to_all x1, waiting for transfers between devices, body(): lax.all_to_all(applied, MPO, split_axis=0, concat_axis=2, tiled=True)  17.8 us
    all_to_all x1, waiting for transfers between devices, body(): lax.all_to_all(jnp.broadcast_to(piece[None], (blocks * physical, columns,...  16.9 us
    pallas_call x1, Pallas kernels, finish(): pl.pallas_call(kernel, in_specs=[pl.BlockSpec(memory_space=pltpu.SMEM)] +...  16.3 us
    all_to_all x1, waiting for transfers between devices, summed_over_chips(): return lax.all_to_all(half, CHIPS, 0, 0, tiled=True).astype(f32).sum(axis=0)  14.5 us
    pallas_call x1, Pallas kernels, sketch(): pl.pallas_call(kernel, grid=(last + 1,), in_specs=[pl.BlockSpec((rows, s,...  13.5 us
    pallas_call x1, Pallas kernels, site_terms(): pl.pallas_call(kernel, grid=(blocks // step,), in_specs=[pl.BlockSpec((wi...  11.7 us
    pallas_call x2, Pallas kernels, expand_half(): pl.pallas_call(kernel, in_specs=[pl.BlockSpec(memory_space=pltpu.SMEM), p...  9.75 us
  transfers between devices with their start and end apart: 8, of which 5 were waited for; matrix products, arithmetic and copies ran while one was open for 4% of the time, Pallas kernels for 14%

profile of v5, /device:TPU:0, one launch (start us, length us, event | category | flops | bytes accessed | tf_op | source)
XLA Modules:
  0.0 197.8 jit_solution(4109890313428084530)
XLA Ops:
  7.2 13.5 %sketch.1 = (bf16[16,4,40,256]{3,2,1,0:T(8,128)(2,1)S(1)}, f32[4,128,256]{2,1,0:T(8,128)S(1)}) custom-call(bf16[256,4,4096]{2,1,0:T(4,128)(2,1)} %s_ref.1, bf16[16,40,4096]{2,1,0:T(8,128)(2,1)} %o_ref.1, bf16[4096,128]{1,0:T(8,128)(2,1)} %w_ref.1), custom_call_target="tpu_custom_call" | custom-call | flops 7000000000 | bytes 15000000 | tf_op jit(solution)/shard_map/sketch/pallas_call | solution.py:84
  20.7 0.6 fusion
  21.3 1.8 copy.17
  23.1 4.4 %all-to-all-start = ((bf16[40,4,16,256]{3,1,2,0:T(4,128)(2,1)}), bf16[40,4,16,256]{3,1,2,0:T(4,128)(2,1)S(1)}, u32[]{:S(2)}, u32[]{:S(2)}) async-start(bf16[40,4,16,256]{3,1,2,0:T(4,128)(2,1)} %copy.17), calls=%async_computation | async-start | bytes 2621440 | tf_op jit(solution)/shard_map/all_to_all | solution.py:511
  27.6 0.9 fusion.6
  28.5 17.8 %all-to-all-done = bf16[40,4,16,256]{3,1,2,0:T(4,128)(2,1)S(1)} async-done(((bf16[40,4,16,256]{3,1,2,0:T(4,128)(2,1)}), bf16[40,4,16,256]{3,1,2,0:T(4,128)(2,1)S(1)}, u32[]{:S(2)}, u32[]{:S(2)}) %all-to-all-start) | async-done | bytes 1310752 | tf_op jit(solution)/shard_map/all_to_all | solution.py:511
  46.3 0.3 copy.18
  46.6 0.2 copy.19
  46.7 4.9 %expand_half.3 = bf16[16,4,128,128]{3,2,1,0:T(8,128)(2,1)S(1)} custom-call(s32[1]{0:T(128)S(6)} %sub.3.core_ref, bf16[5,16,2,128,256]{4,3,2,1,0:T(8,128)(2,1)} %bitcast.63, bf16[5,512,256]{2,1,0:T(8,128)(2,1)S(1)} %bitcast.61), custom_call_target="tpu_custom_call" | custom-call | flops 2684354560 | bytes 9000000 | tf_op jit(solution)/shard_map/expand_half/pallas_call | solution.py:141
  51.7 4.9 %expand_half.2 = bf16[16,4,128,128]{3,2,1,0:T(8,128)(2,1)S(1)} custom-call(s32[1]{0:T(128)} %bitcast.core_ref, bf16[5,16,2,128,256]{4,3,2,1,0:T(8,128)(2,1)} %bitcast.64, bf16[5,512,256]{2,1,0:T(8,128)(2,1)S(1)} %bitcast.62), custom_call_target="tpu_custom_call" | custom-call | flops 2684354560 | bytes 9000000 | tf_op jit(solution)/shard_map/expand_half/pallas_call | solution.py:141
  56.6 2.1 %add_convert_fusion = bf16[16,4,128,128]{3,2,1,0:T(8,128)(2,1)} fusion(bf16[16,4,128,128]{3,2,1,0:T(8,128)(2,1)S(1)} %collective-permute-done, bf16[16,4,128,128]{3,2,1,0:T(8,128)(2,1)S(1)} %expand_half.2), kind=kLoop, calls=%fused_computation.1 | loop fusion | flops 4194304 | bytes 6291456 | tf_op jit(solution)/shard_map/convert_element_type | solution.py:517
  58.7 9.6 %all-to-all-start.1 = ((bf16[64,128,128]{2,1,0:T(8,128)(2,1)}), bf16[64,128,128]{2,1,0:T(8,128)(2,1)S(1)}, u32[]{:S(2)}, u32[]{:S(2)}) async-start(bf16[64,128,128]{2,1,0:T(8,128)(2,1)} %bitcast.21), calls=%async_computation.1 | async-start | bytes 4194304 | tf_op jit(solution)/shard_map/all_to_all | solution.py:519
  68.4 32.1 %all-to-all-done.1 = bf16[64,128,128]{2,1,0:T(8,128)(2,1)S(1)} async-done(((bf16[64,128,128]{2,1,0:T(8,128)(2,1)}), bf16[64,128,128]{2,1,0:T(8,128)(2,1)S(1)}, u32[]{:S(2)}, u32[]{:S(2)}) %all-to-all-start.1) | async-done | bytes 2097184 | tf_op jit(solution)/shard_map/all_to_all | solution.py:519
  100.5 0.3 convert_reduce_fusion
  100.9 0.1 copy.20
  101.1 1.9 broadcast_in_dim.2
  103.0 8.7 %all-to-all-start.2 = ((bf16[64,128,128]{2,1,0:T(8,128)(2,1)}), bf16[64,128,128]{2,1,0:T(8,128)(2,1)S(1)}, u32[]{:S(2)}, u32[]{:S(2)}) async-start(bf16[64,128,128]{2,1,0:T(8,128)(2,1)} %broadcast_in_dim.2), calls=%async_computation.2 | async-start | bytes 4194304 | tf_op jit(solution)/shard_map/all_to_all | solution.py:525
  111.7 11.7 %site_terms.1 = (f32[5,512,256]{2,1,0:T(8,128)S(1)}, f32[128,128]{1,0:T(8,128)S(1)}) custom-call(bf16[5,16,2,128,256]{4,3,2,1,0:T(8,128)(2,1)} %bitcast.65, bf16[16,4,128,256]{3,2,1,0:T(8,128)(2,1)} %bitcast.68), custom_call_target="tpu_custom_call" | custom-call | flops 6000000000 | bytes 17000000 | tf_op jit(solution)/shard_map/site_terms/pallas_call | solution.py:188
  123.5 1.5 copy-done
  125.0 16.9 %all-to-all-done.2 = bf16[64,128,128]{2,1,0:T(8,128)(2,1)S(1)} async-done(((bf16[64,128,128]{2,1,0:T(8,128)(2,1)}), bf16[64,128,128]{2,1,0:T(8,128)(2,1)S(1)}, u32[]{:S(2)}, u32[]{:S(2)}) %all-to-all-start.2) | async-done | bytes 2097184 | tf_op jit(solution)/shard_map/all_to_all | solution.py:525
  141.9 0.1 reshape.52
  142.2 0.1 reshape.53
  142.4 0.1 copy.22
  142.7 6.8 %expand_terms.1 = (f32[5,512,256]{2,1,0:T(8,128)S(1)}, f32[128,256]{1,0:T(8,128)S(1)}) custom-call(s32[1]{0:T(128)} %bitcast.core_ref, bf16[5,16,2,128,256]{4,3,2,1,0:T(8,128)(2,1)} %bitcast.66, bf16[16,4,128,256]{3,2,1,0:T(8,128)(2,1)} %bitcast.69, bf16[16,4,128,128]{3,2,1,0:T(8,128)(2,1)S(1)} %bitcast.59), custom_call_target="tpu_custom_call" | custom-call | flops 3300000000 | bytes 12000000 | tf_op jit(solution)/shard_map/expand_terms/pallas_call | solution.py:267
  149.5 16.3 %finish.1 = (bf16[256,512]{1,0:T(8,128)(2,1)S(1)}, bf16[16,160,128]{2,1,0:T(8,128)(2,1)S(1)}, f32[16,160,128]{2,1,0:T(8,128)S(1)}) custom-call(s32[2]{0:T(128)S(1)} %pad_add_fusion.sc_ref, bf16[5,16,2,128,256]{4,3,2,1,0:T(8,128)(2,1)} %bitcast.67, bf16[16,4,128,256]{3,2,1,0:T(8,128)(2,1)} %bitcast.70, ...), custom_call_target="tpu_custom_call" | custom-call | flops 4000000000 | bytes 20000000 | tf_op jit(solution)/shard_map/finish/pallas_call | solution.py:448
  165.8 0.6 collective-permute-start.2
  166.4 1.7 collective-permute-done.2
  168.1 1.0 add_convert_fusion.1
  169.1 5.8 %all-to-all-start.3 = ((bf16[64,40,128]{2,1,0:T(8,128)(2,1)}), bf16[64,40,128]{2,1,0:T(8,128)(2,1)S(1)}, u32[]{:S(2)}, u32[]{:S(2)}) async-start(bf16[64,40,128]{2,1,0:T(8,128)(2,1)} %bitcast.26), calls=%async_computation.3 | async-start | bytes 1310720 | tf_op jit(solution)/shard_map/all_to_all | solution.py:478
  174.9 0.8 reshape.55
  175.7 14.5 %all-to-all-done.3 = bf16[64,40,128]{2,1,0:T(8,128)(2,1)S(1)} async-done(((bf16[64,40,128]{2,1,0:T(8,128)(2,1)}), bf16[64,40,128]{2,1,0:T(8,128)(2,1)S(1)}, u32[]{:S(2)}, u32[]{:S(2)}) %all-to-all-start.3) | async-done | bytes 655392 | tf_op jit(solution)/shard_map/all_to_all | solution.py:478
  190.2 0.7 convert_reduce_fusion.1
  (27 shorter events, 0.7 us)
Async XLA Ops:
  7.2 13.6 %copy-start.3 = (bf16[40,40,4,4]{1,3,2,0:T(4,128)(2,1)S(1)}, bf16[40,40,4,4]{1,3,2,0:T(4,128)(2,1)}, u32[]{:S(2)}) copy-start(bf16[40,40,4,4]{1,3,2,0:T(4,128)(2,1)} %param.9) | copy-start | bytes 153604
  21.3 6.3 %copy-start.4 = (s32[2,128]{1,0:T(2,128)S(1)}, s32[2,128]{1,0:T(2,128)}, u32[]{:S(2)}) copy-start(s32[2,128]{1,0:T(2,128)} %param.13) | copy-start | bytes 3076
  21.3 6.3 %copy-start.2 = (s32[2,256,4]{1,2,0:T(4,128)S(1)}, s32[2,256,4]{1,2,0:T(4,128)}, u32[]{:S(2)}) copy-start(s32[2,256,4]{1,2,0:T(4,128)} %param.12) | copy-start | bytes 24580
  23.1 23.1 %all-to-all-start = ((bf16[40,4,16,256]{3,1,2,0:T(4,128)(2,1)}), bf16[40,4,16,256]{3,1,2,0:T(4,128)(2,1)S(1)}, u32[]{:S(2)}, u32[]{:S(2)}) async-start(bf16[40,4,16,256]{3,1,2,0:T(4,128)(2,1)} %copy.17), calls=%async_computation | async-start | bytes 2621440 | tf_op jit(solution)/shard_map/all_to_all | solution.py:511
  27.5 84.2 %all-gather.3.cloned.1.call-start = ((), (), s32[]{:S(2)}) async-start(), calls=%async_computation.4 | async-start | bytes 4456448 | tf_op jit(solution)/shard_map/all_gather | solution.py:507
  51.6 5.0 %collective-permute-start = (bf16[16,4,128,128]{3,2,1,0:T(8,128)(2,1)S(1)}, bf16[16,4,128,128]{3,2,1,0:T(8,128)(2,1)S(1)}, u32[]{:S(2)}, u32[]{:S(2)}) collective-permute-start(bf16[16,4,128,128]{3,2,1,0:T(8,128)(2,1)S(1)} %expand_half.3), channel_id=1, source_target_pairs={{0,16},{16,0},{1,17},{17,1},{2,18},{18,2},{3,19},{19,3},{4,20},{20... | collective-permute-start | bytes 6291464 | tf_op jit(solution)/shard_map/ppermute | solution.py:515
  58.7 41.8 %all-to-all-start.1 = ((bf16[64,128,128]{2,1,0:T(8,128)(2,1)}), bf16[64,128,128]{2,1,0:T(8,128)(2,1)S(1)}, u32[]{:S(2)}, u32[]{:S(2)}) async-start(bf16[64,128,128]{2,1,0:T(8,128)(2,1)} %bitcast.21), calls=%async_computation.1 | async-start | bytes 4194304 | tf_op jit(solution)/shard_map/all_to_all | solution.py:519
  103.0 39.0 %all-to-all-start.2 = ((bf16[64,128,128]{2,1,0:T(8,128)(2,1)}), bf16[64,128,128]{2,1,0:T(8,128)(2,1)S(1)}, u32[]{:S(2)}, u32[]{:S(2)}) async-start(bf16[64,128,128]{2,1,0:T(8,128)(2,1)} %broadcast_in_dim.2), calls=%async_computation.2 | async-start | bytes 4194304 | tf_op jit(solution)/shard_map/all_to_all | solution.py:525
  123.5 1.5 copy-start
  141.9 7.5 %collective-permute-start.1 = (bf16[16,4,128,128]{3,2,1,0:T(8,128)(2,1)S(1)}, bf16[16,4,128,128]{3,2,1,0:T(8,128)(2,1)}, u32[]{:S(2)}, u32[]{:S(2)}) collective-permute-start(bf16[16,4,128,128]{3,2,1,0:T(8,128)(2,1)S(1)} %bitcast.58), channel_id=1, source_target_pairs={{0,16},{16,0},{1,17},{17,1},{2,18},{18,2},{3,19},{19,3},{4,20},{20... | collective-permute-start | bytes 6291464 | tf_op jit(solution)/shard_map/ppermute | solution.py:530
  142.7 6.8 %copy-start.1 = (f32[5,512,256]{2,1,0:T(8,128)S(1)}, f32[5,512,256]{2,1,0:T(8,128)}, u32[]{:S(2)}) copy-start(f32[5,512,256]{2,1,0:T(8,128)} %copy-done) | copy-start | bytes 7864324
  165.8 2.3 %collective-permute-start.2 = (bf16[16,160,128]{2,1,0:T(8,128)(2,1)S(1)}, bf16[16,160,128]{2,1,0:T(8,128)(2,1)S(1)}, u32[]{:S(2)}, u32[]{:S(2)}) collective-permute-start(bf16[16,160,128]{2,1,0:T(8,128)(2,1)S(1)} %get-tuple-element.31), channel_id=1, source_target_pairs={{0,16},{16,0},{1,17},{17,1},{2,18},{18,2},{3,19},{19,3},{4,20},{20... | collective-permute-start | bytes 1966088 | tf_op jit(solution)/shard_map/ppermute | solution.py:539
  169.1 21.1 %all-to-all-start.3 = ((bf16[64,40,128]{2,1,0:T(8,128)(2,1)}), bf16[64,40,128]{2,1,0:T(8,128)(2,1)S(1)}, u32[]{:S(2)}, u32[]{:S(2)}) async-start(bf16[64,40,128]{2,1,0:T(8,128)(2,1)} %bitcast.26), calls=%async_computation.3 | async-start | bytes 1310720 | tf_op jit(solution)/shard_map/all_to_all | solution.py:478
Sparse Core Ops, SparseCore 0:
  31.1 77.0 all-gather.2

commit v6 on v5

--- a/solution.py
+++ b/solution.py
@@ -504,24 +504,34 @@
     )
     mask_rows = sector_mask(row_sectors, column_sectors)
     site_local = site_y * jnp.transpose(mask_rows, (1, 2, 0))
-    site_all = lax.all_gather(site_local.astype(bf16), BOND, axis=0)
+    part = physical // 2
+    site_part = lax.dynamic_slice_in_dim(site_local, core * part, part, 0).astype(bf16)
+    site_half = lax.all_gather(site_part, BOND, axis=0)
     applied = jnp.einsum(
         "vwst,ktwa->vska", mpo_tensor, sketched, preferred_element_type=f32
     ).astype(bf16)
     contracted = lax.all_to_all(applied, MPO, split_axis=0, concat_axis=2, tiled=True)
+    contracted, _ = lax.optimization_barrier((contracted, site_part))
     contracted = contracted.reshape(width, physical * columns, depth)
 
     send = expand_half(other_core, env, contracted)
     got = lax.ppermute(send, CORE, SWAP)
     keep = expand_half(own_core, env, contracted)
     half = (keep.astype(f32) + got.astype(f32)).astype(bf16)
-    x_site, g_site = site_terms(env, site_all)
     arrived = lax.all_to_all(half.reshape(-1, share, columns), CHIPS, 0, 0, tiled=True)
     piece = arrived.astype(f32).sum(axis=0)
     mask_piece = lax.dynamic_slice(
         mask_rows, (core * share, lax.axis_index("mpo_0"), 0), (share, 1, columns)
     )[:, 0]
     piece = (piece * mask_piece).T.astype(bf16)
+    site_half, _ = lax.optimization_barrier((site_half, piece))
+    site_rest = lax.ppermute(site_half, CORE, SWAP)
+    site_all = jnp.where(
+        core == 0,
+        jnp.concatenate([site_half, site_rest], axis=1),
+        jnp.concatenate([site_rest, site_half], axis=1),
+    )
+    x_site, g_site = site_terms(env, site_all)
     own = lax.all_to_all(
         jnp.broadcast_to(piece[None], (blocks * physical, columns, share)), CHIPS, 0, 0, tiled=True
     )

time: 198 us -> 216 us (1.091)
  waiting for transfers between devices: 83.1 us -> 92.6 us
  other arithmetic: 5.22 us -> 11.9 us
    all_gather x1, waiting for transfers between devices: 0.02 us -> 16.2 us  [body(): site_half = lax.all_gather(site_part, BOND, axis=0)]
    select_n x0 -> x1, other arithmetic: none -> 5.82 us  [body(): jnp.where(core == 0, jnp.concatenate([site_half, site_rest], axis=1), jnp...]
    all_to_all x1, waiting for transfers between devices: 16.9 us -> 11.7 us  [body(): lax.all_to_all(jnp.broadcast_to(piece[None], (blocks * physical, columns,...]
  transfers between devices with their start and end apart: 8 -> 9, of which waited for: 5 -> 6; matrix products, arithmetic and copies ran while one was open for 4% -> 7% of each run, Pallas kernels for 14% -> 11%
where the time goes in v6:
time: 216 us; the launch traced here: 215 us
  waiting for transfers between devices  92.6 us (43%)
  Pallas kernels  59.4 us (28%)
  starting transfers between devices  28.5 us (13%)
  between operations  14.3 us (7%)
  other arithmetic  11.9 us (6%)
  local copies, waits for them, and re-layouts  7.93 us (4%)
    all_to_all x1, waiting for transfers between devices, body(): lax.all_to_all(half.reshape(-1, share, columns), CHIPS, 0, 0, tiled=True)  30.6 us
    all_to_all x1, waiting for transfers between devices, body(): lax.all_to_all(applied, MPO, split_axis=0, concat_axis=2, tiled=True)  17.9 us
    pallas_call x1, Pallas kernels, finish(): pl.pallas_call(kernel, in_specs=[pl.BlockSpec(memory_space=pltpu.SMEM)] +...  16.3 us
    all_gather x1, waiting for transfers between devices, body(): site_half = lax.all_gather(site_part, BOND, axis=0)  16.2 us
    all_to_all x1, waiting for transfers between devices, summed_over_chips(): return lax.all_to_all(half, CHIPS, 0, 0, tiled=True).astype(f32).sum(axis=0)  14.5 us
    pallas_call x1, Pallas kernels, sketch(): pl.pallas_call(kernel, grid=(last + 1,), in_specs=[pl.BlockSpec((rows, s,...  13.5 us
    pallas_call x1, Pallas kernels, site_terms(): pl.pallas_call(kernel, grid=(blocks // step,), in_specs=[pl.BlockSpec((wi...  11.7 us
    all_to_all x1, waiting for transfers between devices, body(): lax.all_to_all(jnp.broadcast_to(piece[None], (blocks * physical, columns,...  11.7 us
  transfers between devices with their start and end apart: 9, of which 6 were waited for; matrix products, arithmetic and copies ran while one was open for 7% of the time, Pallas kernels for 11%

profile of v6, /device:TPU:0, one launch (start us, length us, event | category | flops | bytes accessed | tf_op | source)
XLA Modules:
  0.0 215.3 jit_solution(2939897852525811857)
XLA Ops:
  7.2 13.5 %sketch.1 = (bf16[16,4,40,256]{3,2,1,0:T(8,128)(2,1)S(1)}, f32[4,128,256]{2,1,0:T(8,128)S(1)}) custom-call(bf16[256,4,4096]{2,1,0:T(4,128)(2,1)} %s_ref.1, bf16[16,40,4096]{2,1,0:T(8,128)(2,1)} %o_ref.1, bf16[4096,128]{1,0:T(8,128)(2,1)} %w_ref.1), custom_call_target="tpu_custom_call" | custom-call | flops 7000000000 | bytes 15000000 | tf_op jit(solution)/shard_map/sketch/pallas_call | solution.py:84
  20.7 0.6 fusion
  21.3 1.8 copy.21
  23.1 4.4 %all-to-all-start = ((bf16[40,4,16,256]{3,1,2,0:T(4,128)(2,1)}), bf16[40,4,16,256]{3,1,2,0:T(4,128)(2,1)S(1)}, u32[]{:S(2)}, u32[]{:S(2)}) async-start(bf16[40,4,16,256]{3,1,2,0:T(4,128)(2,1)} %copy.21), calls=%async_computation | async-start | bytes 2621440 | tf_op jit(solution)/shard_map/all_to_all | solution.py:513
  27.6 0.1 and_select_fusion.sl_ref
  27.7 0.7 dynamic-slice_convert_fusion
  28.4 17.9 %all-to-all-done = bf16[40,4,16,256]{3,1,2,0:T(4,128)(2,1)S(1)} async-done(((bf16[40,4,16,256]{3,1,2,0:T(4,128)(2,1)}), bf16[40,4,16,256]{3,1,2,0:T(4,128)(2,1)S(1)}, u32[]{:S(2)}, u32[]{:S(2)}) %all-to-all-start) | async-done | bytes 1310752 | tf_op jit(solution)/shard_map/all_to_all | solution.py:513
  46.3 0.3 copy.22
  46.7 6.2 %expand_half.3 = bf16[16,4,128,128]{3,2,1,0:T(8,128)(2,1)} custom-call(s32[1]{0:T(128)S(6)} %sub.3.core_ref, bf16[5,16,2,128,256]{4,3,2,1,0:T(8,128)(2,1)} %bitcast.64, bf16[5,512,256]{2,1,0:T(8,128)(2,1)S(1)} %bitcast.62), custom_call_target="tpu_custom_call" | custom-call | flops 2684354560 | bytes 9000000 | tf_op jit(solution)/shard_map/expand_half/pallas_call | solution.py:141
  53.0 4.9 %expand_half.2 = bf16[16,4,128,128]{3,2,1,0:T(8,128)(2,1)S(1)} custom-call(s32[1]{0:T(128)} %bitcast.core_ref, bf16[5,16,2,128,256]{4,3,2,1,0:T(8,128)(2,1)} %bitcast.65, bf16[5,512,256]{2,1,0:T(8,128)(2,1)S(1)} %bitcast.63), custom_call_target="tpu_custom_call" | custom-call | flops 2684354560 | bytes 9000000 | tf_op jit(solution)/shard_map/expand_half/pallas_call | solution.py:141
  57.9 3.7 %add_convert_fusion = bf16[16,4,128,128]{3,2,1,0:T(8,128)(2,1)} fusion(bf16[16,4,128,128]{3,2,1,0:T(8,128)(2,1)} %collective-permute-done, bf16[16,4,128,128]{3,2,1,0:T(8,128)(2,1)S(1)} %expand_half.2), kind=kLoop, calls=%fused_computation.2 | loop fusion | flops 4194304 | bytes 6291456 | tf_op jit(solution)/shard_map/convert_element_type | solution.py:520
  61.6 9.6 %all-to-all-start.1 = ((bf16[64,128,128]{2,1,0:T(8,128)(2,1)}), bf16[64,128,128]{2,1,0:T(8,128)(2,1)S(1)}, u32[]{:S(2)}, u32[]{:S(2)}) async-start(bf16[64,128,128]{2,1,0:T(8,128)(2,1)} %bitcast.22), calls=%async_computation.1 | async-start | bytes 4194304 | tf_op jit(solution)/shard_map/all_to_all | solution.py:521
  71.3 30.6 %all-to-all-done.1 = bf16[64,128,128]{2,1,0:T(8,128)(2,1)S(1)} async-done(((bf16[64,128,128]{2,1,0:T(8,128)(2,1)}), bf16[64,128,128]{2,1,0:T(8,128)(2,1)S(1)}, u32[]{:S(2)}, u32[]{:S(2)}) %all-to-all-start.1) | async-done | bytes 2097184 | tf_op jit(solution)/shard_map/all_to_all | solution.py:521
  101.9 0.3 convert_reduce_fusion
  102.3 16.2 %all-gather.3.cloned.1.call-done = bf16[32,128,256]{2,1,0:T(8,128)(2,1)} async-done(((bf16[2,128,256]{2,1,0:T(8,128)(2,1)}), bf16[32,128,256]{2,1,0:T(8,128)(2,1)}) %all-gather.3.cloned.1.call-update) | async-done | bytes 2097168 | tf_op jit(solution)/shard_map/all_gather | solution.py:509
  118.7 1.9 broadcast_in_dim.2
  120.6 8.3 %all-to-all-start.2 = ((bf16[64,128,128]{2,1,0:T(8,128)(2,1)}), bf16[64,128,128]{2,1,0:T(8,128)(2,1)S(1)}, u32[]{:S(2)}, u32[]{:S(2)}) async-start(bf16[64,128,128]{2,1,0:T(8,128)(2,1)} %broadcast_in_dim.2), calls=%async_computation.2 | async-start | bytes 4194304 | tf_op jit(solution)/shard_map/all_to_all | solution.py:535
  128.9 5.8 %maximum_select_fusion.s_ref = bf16[16,4,128,256]{3,2,1,0:T(8,128)(2,1)} fusion(bf16[16,2,128,256]{3,2,1,0:T(8,128)(2,1)} %collective-permute-done.1, bf16[16,2,128,256]{3,2,1,0:T(8,128)(2,1)} %bitcast.71, pred[]{:T(512)S(6)} %eq.56), kind=kLoop, calls=%fused_computation | loop fusion | flops 6291456 | bytes 8388609 | tf_op jit(solution)/shard_map/jit(_where)/select_n | solution.py:529
  134.7 11.7 %site_terms.1 = (f32[5,512,256]{2,1,0:T(8,128)S(1)}, f32[128,128]{1,0:T(8,128)S(1)}) custom-call(bf16[5,16,2,128,256]{4,3,2,1,0:T(8,128)(2,1)} %bitcast.66, bf16[16,4,128,256]{3,2,1,0:T(8,128)(2,1)} %maximum_select_fusion.s_ref), custom_call_target="tpu_custom_call" | custom-call | flops 6000000000 | bytes 17000000 | tf_op jit(solution)/shard_map/site_terms/pallas_call | solution.py:188
  146.5 1.5 copy-done
  148.0 11.7 %all-to-all-done.2 = bf16[64,128,128]{2,1,0:T(8,128)(2,1)S(1)} async-done(((bf16[64,128,128]{2,1,0:T(8,128)(2,1)}), bf16[64,128,128]{2,1,0:T(8,128)(2,1)S(1)}, u32[]{:S(2)}, u32[]{:S(2)}) %all-to-all-start.2) | async-done | bytes 2097184 | tf_op jit(solution)/shard_map/all_to_all | solution.py:535
  159.7 0.1 reshape.51
  159.9 0.1 reshape.52
  160.4 6.8 %expand_terms.1 = (f32[5,512,256]{2,1,0:T(8,128)S(1)}, f32[128,256]{1,0:T(8,128)S(1)}) custom-call(s32[1]{0:T(128)} %bitcast.core_ref, bf16[5,16,2,128,256]{4,3,2,1,0:T(8,128)(2,1)} %bitcast.67, bf16[16,4,128,256]{3,2,1,0:T(8,128)(2,1)} %maximum_select_fusion.s_ref, bf16[16,4,128,128]{3,2,1,0:T(8,128)(2,1)S(1)} %bitcast.60), custom_call_target="tpu_custom_call" | custom-call | flops 3300000000 | bytes 12000000 | tf_op jit(solution)/shard_map/expand_terms/pallas_call | solution.py:267
  167.2 16.3 %finish.1 = (bf16[256,512]{1,0:T(8,128)(2,1)S(1)}, bf16[16,160,128]{2,1,0:T(8,128)(2,1)S(1)}, f32[16,160,128]{2,1,0:T(8,128)S(1)}) custom-call(s32[2]{0:T(128)S(1)} %pad_add_fusion.sc_ref, bf16[5,16,2,128,256]{4,3,2,1,0:T(8,128)(2,1)} %bitcast.68, bf16[16,4,128,256]{3,2,1,0:T(8,128)(2,1)} %maximum_select_fusion.s_ref, ...), custom_call_target="tpu_custom_call" | custom-call | flops 4000000000 | bytes 20000000 | tf_op jit(solution)/shard_map/finish/pallas_call | solution.py:448
  183.6 0.6 collective-permute-start.3
  184.2 1.7 collective-permute-done.3
  185.9 1.0 add_convert_fusion.1
  186.9 5.5 %all-to-all-start.3 = ((bf16[64,40,128]{2,1,0:T(8,128)(2,1)}), bf16[64,40,128]{2,1,0:T(8,128)(2,1)S(1)}, u32[]{:S(2)}, u32[]{:S(2)}) async-start(bf16[64,40,128]{2,1,0:T(8,128)(2,1)} %bitcast.27), calls=%async_computation.3 | async-start | bytes 1310720 | tf_op jit(solution)/shard_map/all_to_all | solution.py:478
  192.4 0.8 reshape.54
  193.2 14.5 %all-to-all-done.3 = bf16[64,40,128]{2,1,0:T(8,128)(2,1)S(1)} async-done(((bf16[64,40,128]{2,1,0:T(8,128)(2,1)}), bf16[64,40,128]{2,1,0:T(8,128)(2,1)S(1)}, u32[]{:S(2)}, u32[]{:S(2)}) %all-to-all-start.3) | async-done | bytes 655392 | tf_op jit(solution)/shard_map/all_to_all | solution.py:478
  207.7 0.7 convert_reduce_fusion.1
  (31 shorter events, 1.1 us)
Async XLA Ops:
  7.2 13.6 %copy-start.3 = (bf16[40,40,4,4]{1,3,2,0:T(4,128)(2,1)S(1)}, bf16[40,40,4,4]{1,3,2,0:T(4,128)(2,1)}, u32[]{:S(2)}) copy-start(bf16[40,40,4,4]{1,3,2,0:T(4,128)(2,1)} %param.9) | copy-start | bytes 153604
  21.3 6.2 %copy-start.4 = (s32[2,128]{1,0:T(2,128)S(1)}, s32[2,128]{1,0:T(2,128)}, u32[]{:S(2)}) copy-start(s32[2,128]{1,0:T(2,128)} %param.13) | copy-start | bytes 3076
  21.3 6.3 %copy-start.2 = (s32[2,256,4]{1,2,0:T(4,128)S(1)}, s32[2,256,4]{1,2,0:T(4,128)}, u32[]{:S(2)}) copy-start(s32[2,256,4]{1,2,0:T(4,128)} %param.12) | copy-start | bytes 24580
  23.1 23.1 %all-to-all-start = ((bf16[40,4,16,256]{3,1,2,0:T(4,128)(2,1)}), bf16[40,4,16,256]{3,1,2,0:T(4,128)(2,1)S(1)}, u32[]{:S(2)}, u32[]{:S(2)}) async-start(bf16[40,4,16,256]{3,1,2,0:T(4,128)(2,1)} %copy.21), calls=%async_computation | async-start | bytes 2621440 | tf_op jit(solution)/shard_map/all_to_all | solution.py:513
  27.5 91.1 %all-gather.3.cloned.1.call-start = ((), (), s32[]{:S(2)}) async-start(), calls=%async_computation.4 | async-start | bytes 2228224 | tf_op jit(solution)/shard_map/all_gather | solution.py:509
  52.9 5.0 %collective-permute-start = (bf16[16,4,128,128]{3,2,1,0:T(8,128)(2,1)}, bf16[16,4,128,128]{3,2,1,0:T(8,128)(2,1)}, u32[]{:S(2)}, u32[]{:S(2)}) collective-permute-start(bf16[16,4,128,128]{3,2,1,0:T(8,128)(2,1)} %expand_half.3), channel_id=1, source_target_pairs={{0,16},{16,0},{1,17},{17,1},{2,18},{18,2},{3,19},{19,3},{4,20},{20... | collective-permute-start | bytes 6291464 | tf_op jit(solution)/shard_map/ppermute | solution.py:518
  61.6 40.3 %all-to-all-start.1 = ((bf16[64,128,128]{2,1,0:T(8,128)(2,1)}), bf16[64,128,128]{2,1,0:T(8,128)(2,1)S(1)}, u32[]{:S(2)}, u32[]{:S(2)}) async-start(bf16[64,128,128]{2,1,0:T(8,128)(2,1)} %bitcast.22), calls=%async_computation.1 | async-start | bytes 4194304 | tf_op jit(solution)/shard_map/all_to_all | solution.py:521
  118.6 10.3 %collective-permute-start.1 = (bf16[16,2,128,256]{3,2,1,0:T(8,128)(2,1)}, bf16[16,2,128,256]{3,2,1,0:T(8,128)(2,1)}, u32[]{:S(2)}, u32[]{:S(2)}) collective-permute-start(bf16[16,2,128,256]{3,2,1,0:T(8,128)(2,1)} %bitcast.70), channel_id=1, source_target_pairs={{0,16},{16,0},{1,17},{17,1},{2,18},{18,2},{3,19},{19,3},{4,20},{20... | collective-permute-start | bytes 6291464 | tf_op jit(solution)/shard_map/ppermute | solution.py:528
  120.6 39.1 %all-to-all-start.2 = ((bf16[64,128,128]{2,1,0:T(8,128)(2,1)}), bf16[64,128,128]{2,1,0:T(8,128)(2,1)S(1)}, u32[]{:S(2)}, u32[]{:S(2)}) async-start(bf16[64,128,128]{2,1,0:T(8,128)(2,1)} %broadcast_in_dim.2), calls=%async_computation.2 | async-start | bytes 4194304 | tf_op jit(solution)/shard_map/all_to_all | solution.py:535
  146.5 1.5 copy-start
  159.7 7.5 %collective-permute-start.2 = (bf16[16,4,128,128]{3,2,1,0:T(8,128)(2,1)S(1)}, bf16[16,4,128,128]{3,2,1,0:T(8,128)(2,1)}, u32[]{:S(2)}, u32[]{:S(2)}) collective-permute-start(bf16[16,4,128,128]{3,2,1,0:T(8,128)(2,1)S(1)} %bitcast.59), channel_id=1, source_target_pairs={{0,16},{16,0},{1,17},{17,1},{2,18},{18,2},{3,19},{19,3},{4,20},{20... | collective-permute-start | bytes 6291464 | tf_op jit(solution)/shard_map/ppermute | solution.py:540
  160.4 6.8 %copy-start.1 = (f32[5,512,256]{2,1,0:T(8,128)S(1)}, f32[5,512,256]{2,1,0:T(8,128)}, u32[]{:S(2)}) copy-start(f32[5,512,256]{2,1,0:T(8,128)} %copy-done) | copy-start | bytes 7864324
  183.6 2.3 %collective-permute-start.3 = (bf16[16,160,128]{2,1,0:T(8,128)(2,1)S(1)}, bf16[16,160,128]{2,1,0:T(8,128)(2,1)S(1)}, u32[]{:S(2)}, u32[]{:S(2)}) collective-permute-start(bf16[16,160,128]{2,1,0:T(8,128)(2,1)S(1)} %get-tuple-element.35), channel_id=1, source_target_pairs={{0,16},{16,0},{1,17},{17,1},{2,18},{18,2},{3,19},{19,3},{4,20},{20... | collective-permute-start | bytes 1966088 | tf_op jit(solution)/shard_map/ppermute | solution.py:549
  186.9 20.8 %all-to-all-start.3 = ((bf16[64,40,128]{2,1,0:T(8,128)(2,1)}), bf16[64,40,128]{2,1,0:T(8,128)(2,1)S(1)}, u32[]{:S(2)}, u32[]{:S(2)}) async-start(bf16[64,40,128]{2,1,0:T(8,128)(2,1)} %bitcast.27), calls=%async_computation.3 | async-start | bytes 1310720 | tf_op jit(solution)/shard_map/all_to_all | solution.py:478
Sparse Core Ops, SparseCore 0:
  53.1 65.4 all-gather.2

commit v7 on v5

--- a/solution.py
+++ b/solution.py
@@ -439,11 +439,11 @@
             give_ref[g] = stage[...].astype(bf16)
 
         def groups(i, carry):
-            for j in range(4):
-                group(i * 4 + j, stage_ref.at[j])
+            for j in range(8):
+                group(i * 8 + j, stage_ref.at[j])
             return carry
 
-        lax.fori_loop(0, k // 32, groups, 0)
+        lax.fori_loop(0, k // 64, groups, 0)
 
     return pl.pallas_call(
         kernel,
@@ -460,7 +460,7 @@
             pltpu.VMEM((width, s * k, depth), f32),
             pltpu.VMEM((k, 2 * k), f32),
             pltpu.VMEM((depth // k, k * pad, k), f32),
-            pltpu.VMEM((4, 8 * out_rows, k), f32),
+            pltpu.VMEM((8, 8 * out_rows, k), f32),
             pltpu.VMEM((s, k, share), bf16),
             pltpu.SemaphoreType.DMA,
         ]

time: 198 us -> 198 us (level)
  no operation moved by 1% of the time
where the time goes in v7:
time: 198 us
  waiting for transfers between devices  83.1 us (42%)
  Pallas kernels  57.9 us (29%)
  starting transfers between devices  29.1 us (15%)
  between operations  14.3 us (7%)
  local copies, waits for them, and re-layouts  7.3 us (4%)
  other arithmetic  5.22 us (3%)
    all_to_all x1, waiting for transfers between devices, body(): lax.all_to_all(half.reshape(-1, share, columns), CHIPS, 0, 0, tiled=True)  32.1 us
    all_to_all x1, waiting for transfers between devices, body(): lax.all_to_all(applied, MPO, split_axis=0, concat_axis=2, tiled=True)  17.8 us
    all_to_all x1, waiting for transfers between devices, body(): lax.all_to_all(jnp.broadcast_to(piece[None], (blocks * physical, columns,...  16.9 us
    pallas_call x1, Pallas kernels, finish(): pl.pallas_call(kernel, in_specs=[pl.BlockSpec(memory_space=pltpu.SMEM)] +...  16 us
    all_to_all x1, waiting for transfers between devices, summed_over_chips(): return lax.all_to_all(half, CHIPS, 0, 0, tiled=True).astype(f32).sum(axis=0)  14.5 us
    pallas_call x1, Pallas kernels, sketch(): pl.pallas_call(kernel, grid=(last + 1,), in_specs=[pl.BlockSpec((rows, s,...  13.5 us
    pallas_call x1, Pallas kernels, site_terms(): pl.pallas_call(kernel, grid=(blocks // step,), in_specs=[pl.BlockSpec((wi...  11.7 us
    pallas_call x2, Pallas kernels, expand_half(): pl.pallas_call(kernel, in_specs=[pl.BlockSpec(memory_space=pltpu.SMEM), p...  9.75 us
  transfers between devices with their start and end apart: 8, of which 5 were waited for; matrix products, arithmetic and copies ran while one was open for 4% of the time, Pallas kernels for 14%

profile of v7, /device:TPU:0, one launch (start us, length us, event | category | flops | bytes accessed | tf_op | source)
XLA Modules:
  0.0 197.5 jit_solution(7499746334527200563)
XLA Ops:
  7.2 13.5 %sketch.1 = (bf16[16,4,40,256]{3,2,1,0:T(8,128)(2,1)S(1)}, f32[4,128,256]{2,1,0:T(8,128)S(1)}) custom-call(bf16[256,4,4096]{2,1,0:T(4,128)(2,1)} %s_ref.1, bf16[16,40,4096]{2,1,0:T(8,128)(2,1)} %o_ref.1, bf16[4096,128]{1,0:T(8,128)(2,1)} %w_ref.1), custom_call_target="tpu_custom_call" | custom-call | flops 7000000000 | bytes 15000000 | tf_op jit(solution)/shard_map/sketch/pallas_call | solution.py:84
  20.7 0.6 fusion
  21.3 1.8 copy.17
  23.1 4.4 %all-to-all-start = ((bf16[40,4,16,256]{3,1,2,0:T(4,128)(2,1)}), bf16[40,4,16,256]{3,1,2,0:T(4,128)(2,1)S(1)}, u32[]{:S(2)}, u32[]{:S(2)}) async-start(bf16[40,4,16,256]{3,1,2,0:T(4,128)(2,1)} %copy.17), calls=%async_computation | async-start | bytes 2621440 | tf_op jit(solution)/shard_map/all_to_all | solution.py:511
  27.6 0.9 fusion.6
  28.5 17.8 %all-to-all-done = bf16[40,4,16,256]{3,1,2,0:T(4,128)(2,1)S(1)} async-done(((bf16[40,4,16,256]{3,1,2,0:T(4,128)(2,1)}), bf16[40,4,16,256]{3,1,2,0:T(4,128)(2,1)S(1)}, u32[]{:S(2)}, u32[]{:S(2)}) %all-to-all-start) | async-done | bytes 1310752 | tf_op jit(solution)/shard_map/all_to_all | solution.py:511
  46.3 0.3 copy.18
  46.6 0.2 copy.19
  46.7 4.9 %expand_half.3 = bf16[16,4,128,128]{3,2,1,0:T(8,128)(2,1)S(1)} custom-call(s32[1]{0:T(128)S(6)} %sub.3.core_ref, bf16[5,16,2,128,256]{4,3,2,1,0:T(8,128)(2,1)} %bitcast.63, bf16[5,512,256]{2,1,0:T(8,128)(2,1)S(1)} %bitcast.61), custom_call_target="tpu_custom_call" | custom-call | flops 2684354560 | bytes 9000000 | tf_op jit(solution)/shard_map/expand_half/pallas_call | solution.py:141
  51.7 4.9 %expand_half.2 = bf16[16,4,128,128]{3,2,1,0:T(8,128)(2,1)S(1)} custom-call(s32[1]{0:T(128)} %bitcast.core_ref, bf16[5,16,2,128,256]{4,3,2,1,0:T(8,128)(2,1)} %bitcast.64, bf16[5,512,256]{2,1,0:T(8,128)(2,1)S(1)} %bitcast.62), custom_call_target="tpu_custom_call" | custom-call | flops 2684354560 | bytes 9000000 | tf_op jit(solution)/shard_map/expand_half/pallas_call | solution.py:141
  56.6 2.1 %add_convert_fusion = bf16[16,4,128,128]{3,2,1,0:T(8,128)(2,1)} fusion(bf16[16,4,128,128]{3,2,1,0:T(8,128)(2,1)S(1)} %collective-permute-done, bf16[16,4,128,128]{3,2,1,0:T(8,128)(2,1)S(1)} %expand_half.2), kind=kLoop, calls=%fused_computation.1 | loop fusion | flops 4194304 | bytes 6291456 | tf_op jit(solution)/shard_map/convert_element_type | solution.py:517
  58.7 9.6 %all-to-all-start.1 = ((bf16[64,128,128]{2,1,0:T(8,128)(2,1)}), bf16[64,128,128]{2,1,0:T(8,128)(2,1)S(1)}, u32[]{:S(2)}, u32[]{:S(2)}) async-start(bf16[64,128,128]{2,1,0:T(8,128)(2,1)} %bitcast.21), calls=%async_computation.1 | async-start | bytes 4194304 | tf_op jit(solution)/shard_map/all_to_all | solution.py:519
  68.4 32.1 %all-to-all-done.1 = bf16[64,128,128]{2,1,0:T(8,128)(2,1)S(1)} async-done(((bf16[64,128,128]{2,1,0:T(8,128)(2,1)}), bf16[64,128,128]{2,1,0:T(8,128)(2,1)S(1)}, u32[]{:S(2)}, u32[]{:S(2)}) %all-to-all-start.1) | async-done | bytes 2097184 | tf_op jit(solution)/shard_map/all_to_all | solution.py:519
  100.5 0.3 convert_reduce_fusion
  100.9 0.1 copy.20
  101.1 1.9 broadcast_in_dim.2
  103.0 8.7 %all-to-all-start.2 = ((bf16[64,128,128]{2,1,0:T(8,128)(2,1)}), bf16[64,128,128]{2,1,0:T(8,128)(2,1)S(1)}, u32[]{:S(2)}, u32[]{:S(2)}) async-start(bf16[64,128,128]{2,1,0:T(8,128)(2,1)} %broadcast_in_dim.2), calls=%async_computation.2 | async-start | bytes 4194304 | tf_op jit(solution)/shard_map/all_to_all | solution.py:525
  111.7 11.7 %site_terms.1 = (f32[5,512,256]{2,1,0:T(8,128)S(1)}, f32[128,128]{1,0:T(8,128)S(1)}) custom-call(bf16[5,16,2,128,256]{4,3,2,1,0:T(8,128)(2,1)} %bitcast.65, bf16[16,4,128,256]{3,2,1,0:T(8,128)(2,1)} %bitcast.68), custom_call_target="tpu_custom_call" | custom-call | flops 6000000000 | bytes 17000000 | tf_op jit(solution)/shard_map/site_terms/pallas_call | solution.py:188
  123.5 1.5 copy-done
  125.0 16.9 %all-to-all-done.2 = bf16[64,128,128]{2,1,0:T(8,128)(2,1)S(1)} async-done(((bf16[64,128,128]{2,1,0:T(8,128)(2,1)}), bf16[64,128,128]{2,1,0:T(8,128)(2,1)S(1)}, u32[]{:S(2)}, u32[]{:S(2)}) %all-to-all-start.2) | async-done | bytes 2097184 | tf_op jit(solution)/shard_map/all_to_all | solution.py:525
  141.9 0.1 reshape.52
  142.2 0.1 reshape.53
  142.4 0.1 copy.22
  142.7 6.8 %expand_terms.1 = (f32[5,512,256]{2,1,0:T(8,128)S(1)}, f32[128,256]{1,0:T(8,128)S(1)}) custom-call(s32[1]{0:T(128)} %bitcast.core_ref, bf16[5,16,2,128,256]{4,3,2,1,0:T(8,128)(2,1)} %bitcast.66, bf16[16,4,128,256]{3,2,1,0:T(8,128)(2,1)} %bitcast.69, bf16[16,4,128,128]{3,2,1,0:T(8,128)(2,1)S(1)} %bitcast.59), custom_call_target="tpu_custom_call" | custom-call | flops 3300000000 | bytes 12000000 | tf_op jit(solution)/shard_map/expand_terms/pallas_call | solution.py:267
  149.5 16.0 %finish.1 = (bf16[256,512]{1,0:T(8,128)(2,1)S(1)}, bf16[16,160,128]{2,1,0:T(8,128)(2,1)S(1)}, f32[16,160,128]{2,1,0:T(8,128)S(1)}) custom-call(s32[2]{0:T(128)S(1)} %pad_add_fusion.sc_ref, bf16[5,16,2,128,256]{4,3,2,1,0:T(8,128)(2,1)} %bitcast.67, bf16[16,4,128,256]{3,2,1,0:T(8,128)(2,1)} %bitcast.70, ...), custom_call_target="tpu_custom_call" | custom-call | flops 4000000000 | bytes 20000000 | tf_op jit(solution)/shard_map/finish/pallas_call | solution.py:448
  165.5 0.6 collective-permute-start.2
  166.1 1.7 collective-permute-done.2
  167.9 1.0 add_convert_fusion.1
  168.9 5.8 %all-to-all-start.3 = ((bf16[64,40,128]{2,1,0:T(8,128)(2,1)}), bf16[64,40,128]{2,1,0:T(8,128)(2,1)S(1)}, u32[]{:S(2)}, u32[]{:S(2)}) async-start(bf16[64,40,128]{2,1,0:T(8,128)(2,1)} %bitcast.26), calls=%async_computation.3 | async-start | bytes 1310720 | tf_op jit(solution)/shard_map/all_to_all | solution.py:478
  174.7 0.8 reshape.55
  175.4 14.5 %all-to-all-done.3 = bf16[64,40,128]{2,1,0:T(8,128)(2,1)S(1)} async-done(((bf16[64,40,128]{2,1,0:T(8,128)(2,1)}), bf16[64,40,128]{2,1,0:T(8,128)(2,1)S(1)}, u32[]{:S(2)}, u32[]{:S(2)}) %all-to-all-start.3) | async-done | bytes 655392 | tf_op jit(solution)/shard_map/all_to_all | solution.py:478
  189.9 0.7 convert_reduce_fusion.1
  (27 shorter events, 0.7 us)
Async XLA Ops:
  7.2 13.6 %copy-start.3 = (bf16[40,40,4,4]{1,3,2,0:T(4,128)(2,1)S(1)}, bf16[40,40,4,4]{1,3,2,0:T(4,128)(2,1)}, u32[]{:S(2)}) copy-start(bf16[40,40,4,4]{1,3,2,0:T(4,128)(2,1)} %param.9) | copy-start | bytes 153604
  21.3 6.3 %copy-start.4 = (s32[2,128]{1,0:T(2,128)S(1)}, s32[2,128]{1,0:T(2,128)}, u32[]{:S(2)}) copy-start(s32[2,128]{1,0:T(2,128)} %param.13) | copy-start | bytes 3076
  21.3 6.3 %copy-start.2 = (s32[2,256,4]{1,2,0:T(4,128)S(1)}, s32[2,256,4]{1,2,0:T(4,128)}, u32[]{:S(2)}) copy-start(s32[2,256,4]{1,2,0:T(4,128)} %param.12) | copy-start | bytes 24580
  23.1 23.1 %all-to-all-start = ((bf16[40,4,16,256]{3,1,2,0:T(4,128)(2,1)}), bf16[40,4,16,256]{3,1,2,0:T(4,128)(2,1)S(1)}, u32[]{:S(2)}, u32[]{:S(2)}) async-start(bf16[40,4,16,256]{3,1,2,0:T(4,128)(2,1)} %copy.17), calls=%async_computation | async-start | bytes 2621440 | tf_op jit(solution)/shard_map/all_to_all | solution.py:511
  27.5 84.2 %all-gather.3.cloned.1.call-start = ((), (), s32[]{:S(2)}) async-start(), calls=%async_computation.4 | async-start | bytes 4456448 | tf_op jit(solution)/shard_map/all_gather | solution.py:507
  51.6 5.0 %collective-permute-start = (bf16[16,4,128,128]{3,2,1,0:T(8,128)(2,1)S(1)}, bf16[16,4,128,128]{3,2,1,0:T(8,128)(2,1)S(1)}, u32[]{:S(2)}, u32[]{:S(2)}) collective-permute-start(bf16[16,4,128,128]{3,2,1,0:T(8,128)(2,1)S(1)} %expand_half.3), channel_id=1, source_target_pairs={{0,16},{16,0},{1,17},{17,1},{2,18},{18,2},{3,19},{19,3},{4,20},{20... | collective-permute-start | bytes 6291464 | tf_op jit(solution)/shard_map/ppermute | solution.py:515
  58.7 41.8 %all-to-all-start.1 = ((bf16[64,128,128]{2,1,0:T(8,128)(2,1)}), bf16[64,128,128]{2,1,0:T(8,128)(2,1)S(1)}, u32[]{:S(2)}, u32[]{:S(2)}) async-start(bf16[64,128,128]{2,1,0:T(8,128)(2,1)} %bitcast.21), calls=%async_computation.1 | async-start | bytes 4194304 | tf_op jit(solution)/shard_map/all_to_all | solution.py:519
  103.0 39.0 %all-to-all-start.2 = ((bf16[64,128,128]{2,1,0:T(8,128)(2,1)}), bf16[64,128,128]{2,1,0:T(8,128)(2,1)S(1)}, u32[]{:S(2)}, u32[]{:S(2)}) async-start(bf16[64,128,128]{2,1,0:T(8,128)(2,1)} %broadcast_in_dim.2), calls=%async_computation.2 | async-start | bytes 4194304 | tf_op jit(solution)/shard_map/all_to_all | solution.py:525
  123.5 1.5 copy-start
  141.9 7.5 %collective-permute-start.1 = (bf16[16,4,128,128]{3,2,1,0:T(8,128)(2,1)S(1)}, bf16[16,4,128,128]{3,2,1,0:T(8,128)(2,1)}, u32[]{:S(2)}, u32[]{:S(2)}) collective-permute-start(bf16[16,4,128,128]{3,2,1,0:T(8,128)(2,1)S(1)} %bitcast.58), channel_id=1, source_target_pairs={{0,16},{16,0},{1,17},{17,1},{2,18},{18,2},{3,19},{19,3},{4,20},{20... | collective-permute-start | bytes 6291464 | tf_op jit(solution)/shard_map/ppermute | solution.py:530
  142.7 6.8 %copy-start.1 = (f32[5,512,256]{2,1,0:T(8,128)S(1)}, f32[5,512,256]{2,1,0:T(8,128)}, u32[]{:S(2)}) copy-start(f32[5,512,256]{2,1,0:T(8,128)} %copy-done) | copy-start | bytes 7864324
  165.5 2.3 %collective-permute-start.2 = (bf16[16,160,128]{2,1,0:T(8,128)(2,1)S(1)}, bf16[16,160,128]{2,1,0:T(8,128)(2,1)S(1)}, u32[]{:S(2)}, u32[]{:S(2)}) collective-permute-start(bf16[16,160,128]{2,1,0:T(8,128)(2,1)S(1)} %get-tuple-element.31), channel_id=1, source_target_pairs={{0,16},{16,0},{1,17},{17,1},{2,18},{18,2},{3,19},{19,3},{4,20},{20... | collective-permute-start | bytes 1966088 | tf_op jit(solution)/shard_map/ppermute | solution.py:539
  168.9 21.1 %all-to-all-start.3 = ((bf16[64,40,128]{2,1,0:T(8,128)(2,1)}), bf16[64,40,128]{2,1,0:T(8,128)(2,1)S(1)}, u32[]{:S(2)}, u32[]{:S(2)}) async-start(bf16[64,40,128]{2,1,0:T(8,128)(2,1)} %bitcast.26), calls=%async_computation.3 | async-start | bytes 1310720 | tf_op jit(solution)/shard_map/all_to_all | solution.py:478
Sparse Core Ops, SparseCore 0:
  31.1 77.0 all-gather.2
